TPU v7x, 32 devices: a whole 2x2x4 slice. The times are simulated.
32 devices in a mesh: img: 8 (over y, x, core), seq: 4 (over z).
Axes of the slice: x: 2, y: 2, z: 4, core: 2. Of those that a mesh axis runs over, the one named last changes fastest.
Arguments:
- tokens: bfloat16 [8192, 1152], P(('img', 'seq')), may hold values from -6 to 6
- cotangent: bfloat16 [8192, 1152], P(('img', 'seq')), may hold values from -6 to 6
- image_lengths: int32 [8, 2], P('img'), may hold values from 1 to 729, 1024 in all within a row
- qkv_weight: bfloat16 [2, 1152, 3456], P(None, ('img', 'seq')), may hold values from -0.1875 to 0.1875
- out_weight: bfloat16 [2, 1152, 1152], P(None, ('img', 'seq')), may hold values from -3 to 3
- up_weight: bfloat16 [2, 1152, 4304], P(None, ('img', 'seq')), may hold values from -0.1875 to 0.1875
- down_weight: bfloat16 [2, 1152, 4304], P(None, ('img', 'seq')), may hold values from -0.09375 to 0.09375
- up_bias: bfloat16 [2, 4304], replicated, may hold values from -3 to 3
- norm_scale: bfloat16 [2, 1152, 2], P(None, ('img', 'seq')), may hold values from 0.5 to 1.5
- shifts: bfloat16 [2, 1152, 6], P(None, ('img', 'seq')), may hold values from -3 to 3
Outputs:
- output: float32 [8192, 1152], P(('img', 'seq'))
- tokens_grad: float32 [8192, 1152], P(('img', 'seq'))
- qkv_grad: float32 [2, 1152, 3456], P(None, ('img', 'seq'))
- out_grad: float32 [2, 1152, 1152], P(None, ('img', 'seq'))
- up_grad: float32 [2, 1152, 4304], P(None, ('img', 'seq'))
- down_grad: float32 [2, 1152, 4304], P(None, ('img', 'seq'))
- up_bias_grad: float32 [2, 4304], replicated
- norm_scale_grad: float32 [2, 1152, 2], P(None, ('img', 'seq'))
- shifts_grad: float32 [2, 1152, 6], P(None, ('img', 'seq'))
Inputs may be any that keep to these rules, and one draw needn't show every extreme that they name: `image_lengths`: row g lists the lengths of the 2 images packed in order into the 1024 rows of group g; each row sums to 1024, and no image has more than 729 tokens.
All inputs are finite; a program needn't handle non-finite values.
Results may differ from a plain program's by a relative error of at most 0.012.
Values may be sent and summed in bfloat16 or wider, within the bound.
No kernel may reach another device: no remote copies, remote signals or barrier semaphores. Data moves between devices by JAX's collectives and lax.ppermute only.
A program may use at most 448 MiB of HBM per device.

v0:
```python
import jax
import jax.numpy as jnp
from jax import lax
from jax.sharding import PartitionSpec as P

HEADS = 16


EPSILON = 1e-06
NEGATIVE = -1e30


def normalize(inputs, gain, offset):
    centred = inputs - jnp.mean(inputs, axis=-1, keepdims=True)
    variance = jnp.mean(centred * centred, axis=-1, keepdims=True)
    return centred * lax.rsqrt(variance + EPSILON) * gain + offset


def gelu_tanh(inputs):
    return jax.nn.gelu(inputs, approximate=True)


def image_ids(finish, first_row, row_count):
    positions = first_row + jnp.arange(row_count, dtype=jnp.int32)
    return jnp.sum((positions[:, None] >= finish[None, :]).astype(jnp.int32), axis=1)


def split_heads(matrix):
    return matrix.reshape(matrix.shape[0], HEADS, matrix.shape[1] // HEADS)


def unchanged(state):
    return state


def contract_rows(left, right):
    return lax.dot_general(
        left, right, (((0,), (0,)), ((), ())), preferred_element_type=jnp.float32
    )


def contract_last(left, right):
    return lax.dot_general(
        left, right, (((1,), (1,)), ((), ())), preferred_element_type=jnp.float32
    )


def load_block(gathered, key_ids, turn, step_rows, width):
    first_row = turn * step_rows
    key_block = lax.dynamic_slice_in_dim(gathered, first_row, step_rows, 0)
    block_ids = lax.dynamic_slice_in_dim(key_ids, first_row, step_rows, 0)
    return (
        first_row,
        split_heads(key_block[:, :width]),
        split_heads(key_block[:, width:]),
        block_ids,
    )


def masked_scores(query_heads, key_heads, query_ids, block_ids, factor):
    scores = (
        jnp.einsum("qhd,khd->hqk", query_heads, key_heads, preferred_element_type=jnp.float32)
        * factor
    )
    same = (query_ids[:, None] == block_ids[None, :])[None]
    return (jnp.where(same, scores, NEGATIVE), same)


def touches(query_ids, block_ids):
    return jnp.logical_and(block_ids[0] <= query_ids[-1], block_ids[-1] >= query_ids[0])


def softmax_totals(query_heads, gathered, query_ids, key_ids, width, factor, step_rows):
    row_count = query_heads.shape[0]

    def softmax_turn_body(turn, running):
        first_row, key_heads, value_heads, block_ids = load_block(
            gathered, key_ids, turn, step_rows, width
        )

        def softmax_work(state):
            top, total = state
            scores, same = masked_scores(query_heads, key_heads, query_ids, block_ids, factor)
            new_top = jnp.maximum(top, jnp.max(scores, axis=2))
            weights = jnp.where(same, jnp.exp(scores - new_top[:, :, None]), 0.0)
            return (new_top, total * jnp.exp(top - new_top) + jnp.sum(weights, axis=2))

        return lax.cond(touches(query_ids, block_ids), softmax_work, unchanged, running)

    start_state = (
        jnp.full((HEADS, row_count), NEGATIVE, jnp.float32),
        jnp.zeros((HEADS, row_count), jnp.float32),
    )
    top, total = lax.fori_loop(0, gathered.shape[0] // step_rows, softmax_turn_body, start_state)
    return top + jnp.log(total)


def attention_values(
    query_heads, gathered, query_ids, key_ids, log_total, width, factor, step_rows
):
    row_count = query_heads.shape[0]

    def attention_turn_body(turn, output_sum):
        first_row, key_heads, value_heads, block_ids = load_block(
            gathered, key_ids, turn, step_rows, width
        )

        def attention_work(accum):
            scores, same = masked_scores(query_heads, key_heads, query_ids, block_ids, factor)
            probs = jnp.exp(scores - log_total[:, :, None]).astype(jnp.bfloat16)
            return accum + jnp.einsum(
                "hqk,khd->qhd", probs, value_heads, preferred_element_type=jnp.float32
            )

        return lax.cond(touches(query_ids, block_ids), attention_work, unchanged, output_sum)

    start_state = jnp.zeros((row_count, HEADS, width // HEADS), jnp.float32)
    result = lax.fori_loop(0, gathered.shape[0] // step_rows, attention_turn_body, start_state)
    return result.reshape(row_count, width)


def attention_backward(
    query_heads, gathered, query_ids, key_ids, log_total, grad_heads, width, factor, step_rows
):
    row_count = query_heads.shape[0]
    total_rows = gathered.shape[0]
    turns = total_rows // step_rows

    def delta_body(turn, running):
        first_row, key_heads, value_heads, block_ids = load_block(
            gathered, key_ids, turn, step_rows, width
        )

        def delta_work(accum):
            scores, same = masked_scores(query_heads, key_heads, query_ids, block_ids, factor)
            probs = jnp.exp(scores - log_total[:, :, None])
            grad_probs = jnp.einsum(
                "qhd,khd->hqk", grad_heads, value_heads, preferred_element_type=jnp.float32
            )
            return accum + jnp.sum(probs * grad_probs, axis=2)

        return lax.cond(touches(query_ids, block_ids), delta_work, unchanged, running)

    delta = lax.fori_loop(0, turns, delta_body, jnp.zeros((HEADS, row_count), jnp.float32))

    def grad_body(turn, running):
        first_row, key_heads, value_heads, block_ids = load_block(
            gathered, key_ids, turn, step_rows, width
        )

        def grad_work(state):
            query_grad, key_terms = state
            scores, same = masked_scores(query_heads, key_heads, query_ids, block_ids, factor)
            probs = jnp.exp(scores - log_total[:, :, None])
            grad_probs = jnp.einsum(
                "qhd,khd->hqk", grad_heads, value_heads, preferred_element_type=jnp.float32
            )
            score_grad = (probs * (grad_probs - delta[:, :, None])).astype(jnp.bfloat16)
            query_grad = query_grad + jnp.einsum(
                "hqk,khd->qhd", score_grad, key_heads, preferred_element_type=jnp.float32
            )
            key_grad = (
                jnp.einsum(
                    "hqk,qhd->khd", score_grad, query_heads, preferred_element_type=jnp.float32
                )
                * factor
            )
            value_grad = jnp.einsum(
                "hqk,qhd->khd",
                probs.astype(jnp.bfloat16),
                grad_heads,
                preferred_element_type=jnp.float32,
            )
            block_terms = jnp.concatenate(
                [key_grad.reshape(step_rows, width), value_grad.reshape(step_rows, width)], axis=1
            )
            return (
                query_grad,
                lax.dynamic_update_slice_in_dim(key_terms, block_terms, first_row, 0),
            )

        return lax.cond(touches(query_ids, block_ids), grad_work, unchanged, running)

    start_state = (
        jnp.zeros((row_count, HEADS, width // HEADS), jnp.float32),
        jnp.zeros((total_rows, 2 * width), jnp.float32),
    )
    query_grad, key_terms = lax.fori_loop(0, turns, grad_body, start_state)
    return (query_grad.reshape(row_count, width) * factor, key_terms)


def fetch_layer(qkv_piece, out_piece, up_piece, down_piece, gain_piece, offset_piece):
    return (
        lax.all_gather(qkv_piece, ("img", "seq"), axis=0, tiled=True),
        lax.all_gather(out_piece, ("img", "seq"), axis=0, tiled=True),
        lax.all_gather(up_piece, ("img", "seq"), axis=0, tiled=True),
        lax.all_gather(down_piece, ("img", "seq"), axis=0, tiled=True),
        lax.all_gather(gain_piece, ("img", "seq"), axis=0, tiled=True),
        lax.all_gather(offset_piece, ("img", "seq"), axis=0, tiled=True),
    )


def fetch_again(qkv_piece, out_piece, up_piece, down_piece, gain_piece, offset_piece):
    return (
        lax.all_gather(qkv_piece, ("img", "seq"), axis=0, tiled=True),
        lax.all_gather(out_piece, ("img", "seq"), axis=0, tiled=True),
        lax.all_gather(up_piece, ("img", "seq"), axis=0, tiled=True),
        lax.all_gather(down_piece, ("img", "seq"), axis=0, tiled=True),
        lax.all_gather(gain_piece, ("img", "seq"), axis=0, tiled=True),
        lax.all_gather(offset_piece, ("img", "seq"), axis=0, tiled=True),
    )


def sum_to_owners(
    attn_in,
    mixed_grad,
    attended,
    out_in,
    mlp_in,
    hidden_grad,
    down_in,
    activated,
    gain_grad,
    offset_grad,
):
    width = attn_in.shape[1]
    ff_width = activated.shape[1]
    owned = lax.psum_scatter(
        jnp.concatenate(
            [
                contract_rows(attn_in, mixed_grad),
                contract_rows(attended, out_in),
                contract_rows(mlp_in, hidden_grad),
                contract_rows(down_in, activated),
                gain_grad,
                offset_grad,
            ],
            axis=1,
        ),
        ("img", "seq"),
        scatter_dimension=0,
        tiled=True,
    )
    edges = [
        0,
        3 * width,
        4 * width,
        4 * width + ff_width,
        4 * width + 2 * ff_width,
        4 * width + 2 * ff_width + 2,
        4 * width + 2 * ff_width + 8,
    ]
    return tuple((owned[:, edges[index] : edges[index + 1]] for index in range(6)))


def body(
    tokens,
    cotangent,
    image_lengths,
    qkv_weight,
    out_weight,
    up_weight,
    down_weight,
    up_bias,
    norm_scale,
    shifts,
):
    row_count = tokens.shape[0]
    width = tokens.shape[1]
    group_rows = row_count * lax.axis_size("seq")
    finish = jnp.cumsum(image_lengths[0])
    query_ids = image_ids(finish, lax.axis_index("seq") * row_count, row_count)
    key_ids = image_ids(finish, 0, group_rows)
    factor = (width // HEADS) ** (-0.5)
    step_rows = 512
    layer_count = qkv_weight.shape[0]
    current = tokens.astype(jnp.float32)
    saved = []
    for layer_index in range(layer_count):
        params = fetch_layer(
            qkv_weight[layer_index],
            out_weight[layer_index],
            up_weight[layer_index],
            down_weight[layer_index],
            norm_scale[layer_index],
            shifts[layer_index],
        )
        qkv_full, out_full, up_full, down_full, gain_full, offset_full = params
        gains = gain_full.astype(jnp.float32)
        offsets = offset_full.astype(jnp.float32)
        attn_in = normalize(current, gains[:, 0], offsets[:, 0]).astype(jnp.bfloat16)
        qkv_bias = jnp.concatenate([offsets[:, 1], jnp.zeros((width,), jnp.float32), offsets[:, 2]])
        mixed = (jnp.dot(attn_in, qkv_full, preferred_element_type=jnp.float32) + qkv_bias).astype(
            jnp.bfloat16
        )
        queries = mixed[:, :width]
        local_kv = mixed[:, width:]
        gathered = lax.all_gather(local_kv, "seq", axis=0, tiled=True)
        query_heads = split_heads(queries)
        log_total = softmax_totals(
            query_heads, gathered, query_ids, key_ids, width, factor, step_rows
        )
        attended = attention_values(
            query_heads, gathered, query_ids, key_ids, log_total, width, factor, step_rows
        ).astype(jnp.bfloat16)
        after_attn = current + (
            jnp.dot(attended, out_full, preferred_element_type=jnp.float32) + offsets[:, 3]
        )
        mlp_in = normalize(after_attn, gains[:, 1], offsets[:, 4]).astype(jnp.bfloat16)
        hidden = jnp.dot(mlp_in, up_full, preferred_element_type=jnp.float32) + up_bias[
            layer_index
        ].astype(jnp.float32)
        activated = gelu_tanh(hidden).astype(jnp.bfloat16)
        saved.append(
            (
                current,
                attn_in,
                queries,
                local_kv,
                gathered,
                log_total,
                attended,
                after_attn,
                mlp_in,
                hidden,
                activated,
                params,
            )
        )
        current = after_attn + (contract_last(activated, down_full) + offsets[:, 5])
    grad_current = cotangent.astype(jnp.float32)
    qkv_parts, out_parts, up_parts, down_parts, gain_parts, offset_parts, bias_parts = (
        [],
        [],
        [],
        [],
        [],
        [],
        [],
    )
    for layer_index in reversed(range(layer_count)):
        (
            layer_input,
            attn_in,
            queries,
            local_kv,
            gathered,
            log_total,
            attended,
            after_attn,
            mlp_in,
            hidden,
            activated,
            params,
        ) = saved[layer_index]
        qkv_full, out_full, up_full, down_full, gain_full, offset_full = fetch_again(
            qkv_weight[layer_index],
            out_weight[layer_index],
            up_weight[layer_index],
            down_weight[layer_index],
            norm_scale[layer_index],
            shifts[layer_index],
        )
        gains = gain_full.astype(jnp.float32)
        offsets = offset_full.astype(jnp.float32)
        down_in = grad_current.astype(jnp.bfloat16)
        down_bias_grad = jnp.sum(down_in.astype(jnp.float32), axis=0)
        grad_act = jnp.dot(down_in, down_full, preferred_element_type=jnp.float32)
        gelu_value, gelu_pull = jax.vjp(gelu_tanh, hidden)
        hidden_grad = gelu_pull(grad_act)[0].astype(jnp.bfloat16)
        bias_parts.append(jnp.sum(hidden_grad.astype(jnp.float32), axis=0))
        grad_mlp_in = contract_last(hidden_grad, up_full)
        norm_value, norm_pull = jax.vjp(normalize, after_attn, gains[:, 1], offsets[:, 4])
        resid_grad, gain_grad_two, offset_grad_two = norm_pull(grad_mlp_in)
        grad_current = grad_current + resid_grad
        out_in = grad_current.astype(jnp.bfloat16)
        out_bias_grad = jnp.sum(out_in.astype(jnp.float32), axis=0)
        attended_grad = contract_last(out_in, out_full).astype(jnp.bfloat16)
        query_grad, key_terms = attention_backward(
            split_heads(queries),
            gathered,
            query_ids,
            key_ids,
            log_total,
            split_heads(attended_grad),
            width,
            factor,
            step_rows,
        )
        key_value_grad = lax.psum_scatter(
            key_terms.astype(jnp.bfloat16), "seq", scatter_dimension=0, tiled=True
        ).astype(jnp.float32)
        mixed_grad = jnp.concatenate([query_grad, key_value_grad], axis=1).astype(jnp.bfloat16)
        column_sums = jnp.sum(mixed_grad.astype(jnp.float32), axis=0)
        grad_attn_in = contract_last(mixed_grad, qkv_full)
        norm_value, norm_pull = jax.vjp(normalize, layer_input, gains[:, 0], offsets[:, 0])
        resid_grad, gain_grad_one, offset_grad_one = norm_pull(grad_attn_in)
        grad_current = grad_current + resid_grad
        gain_grad = jnp.stack([gain_grad_one, gain_grad_two], axis=1)
        offset_grad = jnp.stack(
            [
                offset_grad_one,
                column_sums[:width],
                column_sums[2 * width :],
                out_bias_grad,
                offset_grad_two,
                down_bias_grad,
            ],
            axis=1,
        )
        owned = sum_to_owners(
            attn_in,
            mixed_grad,
            attended,
            out_in,
            mlp_in,
            hidden_grad,
            down_in,
            activated,
            gain_grad,
            offset_grad,
        )
        qkv_parts.append(owned[0])
        out_parts.append(owned[1])
        up_parts.append(owned[2])
        down_parts.append(owned[3])
        gain_parts.append(owned[4])
        offset_parts.append(owned[5])
    bias_terms = jnp.stack(bias_parts[::-1], axis=0)
    up_bias_grad = lax.psum(bias_terms, ("img", "seq"))
    return (
        current,
        grad_current,
        jnp.stack(qkv_parts[::-1], axis=0),
        jnp.stack(out_parts[::-1], axis=0),
        jnp.stack(up_parts[::-1], axis=0),
        jnp.stack(down_parts[::-1], axis=0),
        up_bias_grad,
        jnp.stack(gain_parts[::-1], axis=0),
        jnp.stack(offset_parts[::-1], axis=0),
    )


def solution(mesh):
    in_specs = (
        P(("img", "seq"), None),
        P(("img", "seq"), None),
        P("img", None),
        P(None, ("img", "seq"), None),
        P(None, ("img", "seq"), None),
        P(None, ("img", "seq"), None),
        P(None, ("img", "seq"), None),
        P(),
        P(None, ("img", "seq"), None),
        P(None, ("img", "seq"), None),
    )
    out_specs = (
        P(("img", "seq"), None),
        P(("img", "seq"), None),
        P(None, ("img", "seq"), None),
        P(None, ("img", "seq"), None),
        P(None, ("img", "seq"), None),
        P(None, ("img", "seq"), None),
        P(),
        P(None, ("img", "seq"), None),
        P(None, ("img", "seq"), None),
    )
    return jax.shard_map(body, mesh=mesh, in_specs=in_specs, out_specs=out_specs, check_vma=False)
```

profile of v0, /device:TPU:1, one launch (start us, length us, event | category | flops | bytes accessed | tf_op | source)
XLA Modules:
  0.0 3477.5 jit_solution(2548936910184736666)
XLA Ops:
  14.8 75.6 %all-gather = bf16[1,1152,2]{2,0,1:T(2,128)(2,1)S(1)} all-gather(bf16[1,36,2]{2,0,1:T(2,128)(2,1)S(1)} %copy.228), channel_id=2, replica_groups=mesh['img'=8,'seq'=4] {'img','seq'}, dimensions={1}, use_global_device_ids=true | all-gather | bytes 4752 | tf_op jit(solution)/shard_map/all_gather | solution.py:198
  91.0 75.8 %all-gather.1 = bf16[1,1152,6]{2,0,1:T(2,128)(2,1)S(1)} all-gather(bf16[1,36,6]{2,0,1:T(2,128)(2,1)S(1)} %copy.229), channel_id=3, replica_groups=mesh['img'=8,'seq'=4] {'img','seq'}, dimensions={1}, use_global_device_ids=true | all-gather | bytes 14256 | tf_op jit(solution)/shard_map/all_gather | solution.py:199
  167.3 76.6 %all-gather.7 = bf16[1,1152,6]{2,0,1:T(2,128)(2,1)S(1)} all-gather(bf16[1,36,6]{2,0,1:T(2,128)(2,1)S(1)} %copy.231), channel_id=9, replica_groups=mesh['img'=8,'seq'=4] {'img','seq'}, dimensions={1}, use_global_device_ids=true | all-gather | bytes 14256 | tf_op jit(solution)/shard_map/all_gather | solution.py:199
  261.3 76.9 %all-gather.6 = bf16[1,1152,2]{2,0,1:T(2,128)(2,1)S(1)} all-gather(bf16[1,36,2]{2,0,1:T(2,128)(2,1)S(1)} %copy.230), channel_id=8, replica_groups=mesh['img'=8,'seq'=4] {'img','seq'}, dimensions={1}, use_global_device_ids=true | all-gather | bytes 4752 | tf_op jit(solution)/shard_map/all_gather | solution.py:198
  342.0 40.5 %copy.183 = bf16[1,1152,4304]{1,2,0:T(8,128)(2,1)} copy(bf16[1,1152,4304]{2,0,1:T(2,128)(2,1)} %all-gather.31.cloned.1.call-done) | data formatting | bytes 19832832 | tf_op jit(solution)/shard_map/all_gather | solution.py:196
  382.5 31.0 all-gather.33.cloned.1.call-done
  413.5 40.2 %copy.184 = bf16[1,1152,4304]{1,2,0:T(8,128)(2,1)} copy(bf16[1,1152,4304]{2,0,1:T(2,128)(2,1)} %all-gather.33.cloned.1.call-done) | data formatting | bytes 19832832 | tf_op jit(solution)/shard_map/all_gather | solution.py:197
  453.8 49.0 %all-gather.23.cloned.1.call-done = bf16[1024,2304]{1,0:T(8,128)(2,1)} async-done(((bf16[256,2304]{1,0:T(8,128)(2,1)}), bf16[1024,2304]{1,0:T(8,128)(2,1)}) %all-gather.23.cloned.1.call-update) | async-done | bytes 4718608 | tf_op jit(solution)/shard_map/all_gather | solution.py:298
  528.0 22.3 while.125
  597.1 85.6 %all-gather.35.cloned.1.call-done = bf16[1,1152,3456]{2,0,1:T(2,128)(2,1)} async-done(((bf16[1,36,3456]{2,0,1:T(2,128)(2,1)}), bf16[1,1152,3456]{2,0,1:T(2,128)(2,1)}) %all-gather.35.cloned.1.call-update) | async-done | bytes 7962640 | tf_op jit(solution)/shard_map/all_gather | solution.py:194
  692.8 121.7 %all-gather.39.cloned.1.call-done = bf16[1,1152,4304]{2,0,1:T(2,128)(2,1)} async-done(((bf16[1,36,4304]{2,0,1:T(2,128)(2,1)}), bf16[1,1152,4304]{2,0,1:T(2,128)(2,1)}) %all-gather.39.cloned.1.call-update) | async-done | bytes 9916432 | tf_op jit(solution)/shard_map/all_gather | solution.py:196
  814.5 40.4 %copy.191 = bf16[1,1152,4304]{1,2,0:T(8,128)(2,1)} copy(bf16[1,1152,4304]{2,0,1:T(2,128)(2,1)} %all-gather.39.cloned.1.call-done) | data formatting | bytes 19832832 | tf_op jit(solution)/shard_map/all_gather | solution.py:196
  854.8 91.3 %all-gather.41.cloned.1.call-done = bf16[1,1152,4304]{2,0,1:T(2,128)(2,1)} async-done(((bf16[1,36,4304]{2,0,1:T(2,128)(2,1)}), bf16[1,1152,4304]{2,0,1:T(2,128)(2,1)}) %all-gather.41.cloned.1.call-update) | async-done | bytes 9916432 | tf_op jit(solution)/shard_map/all_gather | solution.py:197
  946.1 40.3 %copy.192 = bf16[1,1152,4304]{1,2,0:T(8,128)(2,1)} copy(bf16[1,1152,4304]{2,0,1:T(2,128)(2,1)} %all-gather.41.cloned.1.call-done) | data formatting | bytes 19832832 | tf_op jit(solution)/shard_map/all_gather | solution.py:197
  986.7 48.8 %all-gather.25.cloned.1.call-done = bf16[1024,2304]{1,0:T(8,128)(2,1)} async-done(((bf16[256,2304]{1,0:T(8,128)(2,1)}), bf16[1024,2304]{1,0:T(8,128)(2,1)}) %all-gather.25.cloned.1.call-update) | async-done | bytes 4718608 | tf_op jit(solution)/shard_map/all_gather | solution.py:298
  1060.1 20.8 while.127
  1082.2 21.3 all-gather.37.cloned.1.call-done
  1157.8 32.8 while.129
  1191.6 82.9 %reduce-scatter.5.cloned.1.call-done = bf16[256,2304]{0,1:T(8,128)(2,1)} async-done(((bf16[1024,2304]{0,1:T(8,128)(2,1)}), bf16[256,2304]{0,1:T(8,128)(2,1)}) %reduce-scatter.5.cloned.1.call-update) | async-done | bytes 1179664 | tf_op jit(solution)/shard_map/reduce_scatter | solution.py:390
  1327.4 33.1 while.131
  1394.4 139.5 %concatenate.33 = f32[1152,13224]{0,1:T(8,128)} concatenate(f32[1152,3456]{0,1:T(8,128)} %fusion.173, f32[1152,1152]{0,1:T(8,128)} %fusion.237, f32[1152,4304]{0,1:T(8,128)} %fusion.194, f32[1152,4304]{0,1:T(8,128)} %convolution_bitcast_fusion.2, f32[1152,1]{0,1:T(1,128)S(1)} %stack.120, f32[1152,1]{0,1:T(1,128)S(1)} %stack.121, f32[1152,1]{0,1:T(1,128)S(1)} %stack.122, ...), dimensions={1} | concatenate | bytes 121872384 | tf_op jit(solution)/shard_map/concatenate | solution.py:229
  1577.7 140.3 %concatenate.32 = f32[1152,13224]{0,1:T(8,128)} concatenate(f32[1152,3456]{0,1:T(8,128)} %fusion.172, f32[1152,1152]{0,1:T(8,128)} %fusion.236, f32[1152,4304]{0,1:T(8,128)} %fusion.193, f32[1152,4304]{0,1:T(8,128)} %fusion.187, f32[1152,1]{0,1:T(1,128)} %stack.111, f32[1152,1]{0,1:T(1,128)} %stack.112, f32[1152,1]{0,1:T(1,128)} %stack.113, f32[1152,1]{0,1:T(1,128)} %stack.114, ...), dimensions={1} | concatenate | bytes 121872384 | tf_op jit(solution)/shard_map/concatenate | solution.py:229
  1728.2 43.7 %psum.7 = f32[2,4304]{1,0:T(2,128)} all-reduce(f32[2,4304]{1,0:T(2,128)S(1)} %pad_maximum_fusion.10), channel_id=1, replica_groups=mesh['img'=8,'seq'=4] {'img','seq'}, use_global_device_ids=true, to_apply=%region_77.78 | all-reduce | flops 8608 | bytes 68864 | tf_op jit(solution)/shard_map/psum | solution.py:430
  1775.1 1645.9 %all-reduce.5.cloned.1.call-done = (f32[1152,13224]{0,1:T(8,128)}, f32[1152,13224]{0,1:T(8,128)}) async-done(((f32[1152,13224]{0,1:T(8,128)}, f32[1152,13224]{0,1:T(8,128)}), (f32[1152,13224]{0,1:T(8,128)}, f32[1152,13224]{0,1:T(8,128)})) %all-reduce.5.cloned.1.call-update) | async-done | bytes 121872400
  (634 shorter events, 649.9 us)
Async XLA Ops:
  7.2 240.7 %all-gather.27.cloned.1.call-start = ((), (), s32[]{:S(2)}) async-start(), calls=%async_computation.6 | async-start | bytes 16422912 | tf_op jit(solution)/shard_map/all_gather | solution.py:194
  10.3 331.7 %all-gather.31.cloned.1.call-start = ((), (), s32[]{:S(2)}) async-start(), calls=%async_computation.8 | async-start | bytes 20680704 | tf_op jit(solution)/shard_map/all_gather | solution.py:196
  12.3 401.2 %all-gather.33.cloned.1.call-start = ((), (), s32[]{:S(2)}) async-start(), calls=%async_computation.9 | async-start | bytes 20680704 | tf_op jit(solution)/shard_map/all_gather | solution.py:197
  14.3 488.4 %all-gather.23.cloned.1.call-start = ((), (), s32[]{:S(2)}) async-start(), calls=%async_computation.2 | async-start | bytes 5898240 | tf_op jit(solution)/shard_map/all_gather | solution.py:298
  14.8 231.6 %copy-start.5 = (bf16[256,1152]{1,0:T(8,128)(2,1)S(1)}, bf16[256,1152]{1,0:T(8,128)(2,1)}, u32[]{:S(2)}) copy-start(bf16[256,1152]{1,0:T(8,128)(2,1)} %param.42) | copy-start | bytes 1769476
  257.9 312.3 %all-gather.29.cloned.1.call-start = ((), (), s32[]{:S(2)}) async-start(), calls=%async_computation.7 | async-start | bytes 5474304 | tf_op jit(solution)/shard_map/all_gather | solution.py:195
  258.9 423.8 %all-gather.35.cloned.1.call-start = ((), (), s32[]{:S(2)}) async-start(), calls=%async_computation.10 | async-start | bytes 16422912 | tf_op jit(solution)/shard_map/all_gather | solution.py:194
  259.5 555.0 %all-gather.39.cloned.1.call-start = ((), (), s32[]{:S(2)}) async-start(), calls=%async_computation.12 | async-start | bytes 20680704 | tf_op jit(solution)/shard_map/all_gather | solution.py:196
  260.2 685.9 %all-gather.41.cloned.1.call-start = ((), (), s32[]{:S(2)}) async-start(), calls=%async_computation.13 | async-start | bytes 20680704 | tf_op jit(solution)/shard_map/all_gather | solution.py:197
  261.0 774.5 %all-gather.25.cloned.1.call-start = ((), (), s32[]{:S(2)}) async-start(), calls=%async_computation.3 | async-start | bytes 5898240 | tf_op jit(solution)/shard_map/all_gather | solution.py:298
  593.4 89.3 %copy-start.50 = (f32[1152]{0:T(1024)S(1)}, f32[1152]{0:T(1024)}, u32[]{:S(2)}) copy-start(f32[1152]{0:T(1024)} %get-tuple-element.1968) | copy-start | bytes 13828
  593.4 89.3 %copy-start.57 = (f32[1152]{0:T(1024)S(1)}, f32[1152]{0:T(1024)}, u32[]{:S(2)}) copy-start(f32[1152]{0:T(1024)} %get-tuple-element.1976) | copy-start | bytes 13828
  593.5 89.3 %copy-start.86 = (f32[3456]{0:T(1024)S(1)}, f32[3456]{0:T(1024)}, u32[]{:S(2)}) copy-start(f32[3456]{0:T(1024)} %get-tuple-element.2208) | copy-start | bytes 41476
  596.8 94.2 %copy-start.17 = (f32[256,1152]{1,0:T(8,128)}, f32[256,1152]{1,0:T(8,128)S(1)}, u32[]{:S(2)}) copy-start(f32[256,1152]{1,0:T(8,128)S(1)} %get-tuple-element.2217) | copy-start | bytes 3538948
  596.8 94.2 %copy-start.87 = (f32[256]{0:T(256)}, f32[256]{0:T(256)S(1)}, u32[]{:S(2)}) copy-start(f32[256]{0:T(256)S(1)} %broadcast_multiply_fusion.1) | copy-start | bytes 3076
  597.1 93.9 %copy-start.107 = (f32[256]{0:T(256)}, f32[256]{0:T(256)S(1)}, u32[]{:S(2)}) copy-start(f32[256]{0:T(256)S(1)} %multiply_reduce_fusion.7) | copy-start | bytes 3076
  597.1 93.9 %copy-start.109 = (f32[256]{0:T(256)}, f32[256]{0:T(256)S(1)}, u32[]{:S(2)}) copy-start(f32[256]{0:T(256)S(1)} %fusion.181) | copy-start | bytes 3076
  692.1 411.3 %all-gather.37.cloned.1.call-start = ((), (), s32[]{:S(2)}) async-start(), calls=%async_computation.11 | async-start | bytes 5474304 | tf_op jit(solution)/shard_map/all_gather | solution.py:195
  692.7 581.8 %reduce-scatter.5.cloned.1.call-start = ((), (), s32[]{:S(2)}) async-start(), calls=%async_computation.4 | async-start | bytes 5898240 | tf_op jit(solution)/shard_map/reduce_scatter | solution.py:390
  1190.5 84.0 %copy-start.110 = (f32[256]{0:T(256)S(1)}, f32[256]{0:T(256)}, u32[]{:S(2)}) copy-start(f32[256]{0:T(256)} %copy-done.109) | copy-start | bytes 3076
  1190.6 95.8 %slice-start.16 = ((s8[4407296]{0:T(1024)(128)(4,1)}), s8[212992]{0:T(1024)(128)(4,1)S(1)}, s32[]{:S(2)}) async-start(s8[4407296]{0:T(1024)(128)(4,1)} %bitcast.378), calls=%async_computation.31 | async-start | bytes 425984
  1190.6 365.7 %reduce-scatter.7.cloned.1.call-start = ((), (), s32[]{:S(2)}) async-start(), calls=%async_computation.5 | async-start | bytes 5898240 | tf_op jit(solution)/shard_map/reduce_scatter | solution.py:390
  1360.5 2060.4 %all-reduce.5.cloned.1.call-start = ((), (), s32[]{:S(2)}) async-start(), calls=%async_computation.14 | async-start | bytes 243744768
  1394.4 139.7 %copy-start.41 = (bf16[256,1152]{1,0:T(8,128)(2,1)S(1)}, bf16[256,1152]{1,0:T(8,128)(2,1)}, u32[]{:S(2)}) copy-start(bf16[256,1152]{1,0:T(8,128)(2,1)} %copy-done.40) | copy-start | bytes 1769476
  (138 other events, 1504.2 us)
Sparse Core Ops, SparseCore 0:
  11.4 122.7 all-gather.26
  137.7 138.5 all-gather.30
  279.6 133.8 all-gather.32
  415.5 87.1 all-gather.22
  505.4 64.6 all-gather.28
  572.8 109.8 all-gather.34
  686.1 128.3 all-gather.38
  817.8 128.2 all-gather.40
  948.2 87.1 all-gather.24
  1038.7 64.7 all-gather.36
  1190.7 83.7 reduce-scatter.4
  1360.7 85.7 reduce-scatter.6
  1718.1 1702.8 all-reduce.4
where the time goes:
time: 3500 us; the launch traced here: 3480 us
  waiting for transfers between devices  2200 us (63%)
  local copies, waits for them, and re-layouts  575 us (16%)
  blocking collectives  349 us (10%)
  matrix products  254 us (7%)
  loops' own time  42.8 us (1%)
  other arithmetic  42.4 us (1%)
    unnamed x14, waiting for transfers between devices  1650 us
    concatenate x2, local copies, waits for them, and re-layouts, sum_to_owners(): jnp.concatenate([contract_rows(attn_in, mixed_grad), contract_rows(attend...  280 us
    all_gather x2, blocking collectives, fetch_layer(): lax.all_gather(gain_piece, ('img', 'seq'), axis=0, tiled=True)  153 us
    all_gather x2, blocking collectives, fetch_layer(): lax.all_gather(offset_piece, ('img', 'seq'), axis=0, tiled=True)  152 us
    all_gather x2, waiting for transfers between devices, fetch_layer(): lax.all_gather(down_piece, ('img', 'seq'), axis=0, tiled=True)  122 us
    all_gather x2, waiting for transfers between devices, fetch_layer(): lax.all_gather(up_piece, ('img', 'seq'), axis=0, tiled=True)  122 us
    all_gather x2, waiting for transfers between devices, body(): gathered = lax.all_gather(local_kv, 'seq', axis=0, tiled=True)  97.7 us
    all_gather x2, waiting for transfers between devices, fetch_layer(): lax.all_gather(qkv_piece, ('img', 'seq'), axis=0, tiled=True)  85.6 us
  transfers between devices with their start and end apart: 13, of which 10 were waited for; matrix products, arithmetic and copies ran while one was open for 14% of the time, Pallas kernels for 0%

commit v1 on v0

v1 whole, which is shorter than its diff:
```python
import functools
import math

import jax
import jax.numpy as jnp
from jax import lax
from jax.experimental import pallas as pl
from jax.experimental.pallas import tpu as pltpu
from jax.sharding import Mesh
from jax.sharding import PartitionSpec as P

HEADS = 16
RANKS = 4
EPSILON = 1e-06
NEGATIVE = -1e30
AXES = ("hi", "x", "c", "seq")
SWAP = ((0, 1), (1, 0))
bf16, f32 = jnp.bfloat16, jnp.float32


def attend_kernel(heads, dim, offset, qid_ref, kid_ref, q_ref, kv_ref, o_ref):
    factor = dim**-0.5 * math.log2(math.e)
    same = qid_ref[...] == kid_ref[...]
    width = heads * dim
    outs = []
    for h in range(heads):
        lo, hi = h * dim, (h + 1) * dim
        q = q_ref[:, lo:hi]
        k = kv_ref[:, offset + lo : offset + hi]
        v = kv_ref[:, offset + width + lo : offset + width + hi]
        s = lax.dot_general(q, k, (((1,), (1,)), ((), ())), preferred_element_type=f32)
        s = jnp.where(same, s, NEGATIVE)
        top = jnp.max(s, axis=1, keepdims=True)
        p = jnp.exp2((s - top) * factor)
        total = jnp.sum(p, axis=1, keepdims=True)
        o = jnp.dot(p.astype(bf16), v, preferred_element_type=f32)
        outs.append(o / total)
    o_ref[...] = jnp.concatenate(outs, axis=1).astype(o_ref.dtype)


def attend(qkv, kv, offset, query_ids, key_ids, heads, dim):
    rows, keys, width = qkv.shape[0], kv.shape[0], heads * dim
    block = min(rows, 512 * 1024 // keys)
    return pl.pallas_call(
        functools.partial(attend_kernel, heads, dim, offset),
        grid=(rows // block,),
        in_specs=[
            pl.BlockSpec((block, 1), lambda i: (i, 0)),
            pl.BlockSpec((1, keys), lambda i: (0, 0)),
            pl.BlockSpec((block, qkv.shape[1]), lambda i: (i, 0)),
            pl.BlockSpec(kv.shape, lambda i: (0, 0)),
        ],
        out_specs=pl.BlockSpec((block, width), lambda i: (i, 0)),
        out_shape=jax.ShapeDtypeStruct((rows, width), bf16),
        compiler_params=pltpu.CompilerParams(vmem_limit_bytes=48 * 2**20),
        cost_estimate=pl.CostEstimate(
            flops=4 * rows * keys * width,
            bytes_accessed=8 * rows * width,
            transcendentals=heads * rows * keys,
        ),
    )(query_ids[:, None], key_ids[None, :], qkv, kv)


def attend_back_kernel(
    heads, dim, offset, qid_ref, kid_ref, q_ref, kv_ref, do_ref, dq_ref, dkv_ref, dk_sum, dv_sum
):
    scale = dim**-0.5
    factor = scale * math.log2(math.e)
    step = pl.program_id(0)

    @pl.when(step == 0)
    def _():
        dk_sum[...] = jnp.zeros_like(dk_sum)
        dv_sum[...] = jnp.zeros_like(dv_sum)

    same = kid_ref[...] == qid_ref[...]
    width = heads * dim
    dqs = []
    for h in range(heads):
        lo, hi = h * dim, (h + 1) * dim
        q = q_ref[:, lo:hi]
        do = do_ref[:, lo:hi]
        k = kv_ref[:, offset + lo : offset + hi]
        v = kv_ref[:, offset + width + lo : offset + width + hi]
        s = lax.dot_general(k, q, (((1,), (1,)), ((), ())), preferred_element_type=f32)
        s = jnp.where(same, s, NEGATIVE)
        top = jnp.max(s, axis=0, keepdims=True)
        p = jnp.exp2((s - top) * factor)
        p = p * (1.0 / jnp.sum(p, axis=0, keepdims=True))
        dp = lax.dot_general(v, do, (((1,), (1,)), ((), ())), preferred_element_type=f32)
        delta = jnp.sum(p * dp, axis=0, keepdims=True)
        ds = (p * (dp - delta)).astype(bf16)
        dv_sum[h] += jnp.dot(p.astype(bf16), do, preferred_element_type=f32)
        dk_sum[h] += jnp.dot(ds, q, preferred_element_type=f32)
        dq = lax.dot_general(ds, k, (((0,), (0,)), ((), ())), preferred_element_type=f32)
        dqs.append(dq * scale)
    dq_ref[...] = jnp.concatenate(dqs, axis=1).astype(dq_ref.dtype)

    @pl.when(step == pl.num_programs(0) - 1)
    def _():
        parts = [dk_sum[h] * scale for h in range(heads)] + [dv_sum[h] for h in range(heads)]
        dkv_ref[...] = jnp.concatenate(parts, axis=1).astype(dkv_ref.dtype)


def attend_back(qkv, kv, offset, query_ids, key_ids, grad, heads, dim):
    rows, keys, width = qkv.shape[0], kv.shape[0], heads * dim
    block = min(rows, 512 * 1024 // keys)
    return pl.pallas_call(
        functools.partial(attend_back_kernel, heads, dim, offset),
        grid=(rows // block,),
        in_specs=[
            pl.BlockSpec((1, block), lambda i: (0, i)),
            pl.BlockSpec((keys, 1), lambda i: (0, 0)),
            pl.BlockSpec((block, qkv.shape[1]), lambda i: (i, 0)),
            pl.BlockSpec(kv.shape, lambda i: (0, 0)),
            pl.BlockSpec((block, width), lambda i: (i, 0)),
        ],
        out_specs=[
            pl.BlockSpec((block, width), lambda i: (i, 0)),
            pl.BlockSpec((keys, 2 * width), lambda i: (0, 0)),
        ],
        out_shape=[
            jax.ShapeDtypeStruct((rows, width), bf16),
            jax.ShapeDtypeStruct((keys, 2 * width), bf16),
        ],
        scratch_shapes=[pltpu.VMEM((heads, keys, dim), f32)] * 2,
        compiler_params=pltpu.CompilerParams(vmem_limit_bytes=56 * 2**20),
        cost_estimate=pl.CostEstimate(
            flops=10 * rows * keys * width,
            bytes_accessed=20 * rows * width,
            transcendentals=heads * rows * keys,
        ),
    )(query_ids[None, :], key_ids[:, None], qkv, kv, grad)


def dot(left, right, kind=f32):
    return jnp.dot(left, right, preferred_element_type=f32).astype(kind)


def dot_last(left, right, kind=f32):
    dims = (((1,), (1,)), ((), ()))
    return lax.dot_general(left, right, dims, preferred_element_type=f32).astype(kind)


def dot_rows(left, right, kind=f32):
    dims = (((0,), (0,)), ((), ()))
    return lax.dot_general(left, right, dims, preferred_element_type=f32).astype(kind)


def pick(array, index, axis=0):
    return lax.dynamic_index_in_dim(array, index, axis, keepdims=False)


def standardize(v):
    centred = v - jnp.mean(v, axis=-1, keepdims=True)
    scale = lax.rsqrt(jnp.mean(centred * centred, axis=-1, keepdims=True) + EPSILON)
    return centred * scale, scale


def norm(v, gain, offset):
    return standardize(v)[0] * gain + offset


def norm_back(v, gain, t):
    n, scale = standardize(v)
    w = t * gain
    mean_w = jnp.mean(w, axis=-1, keepdims=True)
    mean_wn = jnp.mean(w * n, axis=-1, keepdims=True)
    grad = scale * (w - mean_w - n * mean_wn)
    return grad, jnp.sum(t * n, axis=0), jnp.sum(t, axis=0)


def gelu_tanh(v):
    return jax.nn.gelu(v, approximate=True)


def swap_x(v):
    return lax.ppermute(v, "x", SWAP)


def swap_c(v):
    return lax.ppermute(v, "c", SWAP)


def x_order(own, other):
    first = lax.axis_index("x") == 0
    return jnp.where(first, own, other), jnp.where(first, other, own)


def exchange(blocks):
    xi, ci = lax.axis_index("x"), lax.axis_index("c")
    blocks = blocks.reshape((2, 2) + blocks.shape[1:])
    mine = pick(blocks, xi)
    theirs = swap_x(pick(blocks, 1 - xi))
    ahead, behind = x_order(mine, theirs)
    both = jnp.stack([ahead, behind])
    kept = pick(both, ci, 1)
    come = swap_c(pick(both, 1 - ci, 1))
    first = ci == 0
    out = jnp.stack([jnp.where(first, kept, come), jnp.where(first, come, kept)], axis=1)
    return out.reshape((RANKS,) + blocks.shape[2:])


def gather_rows(payload):
    size = lax.axis_size("hi")
    place = lax.axis_index("hi")
    full = lax.all_gather(payload, "seq", axis=0, tiled=True)[None]
    step = 1
    while step < size:
        come = lax.ppermute(full, "hi", [(i, i ^ step) for i in range(size)])
        low = (place & step) == 0
        full = jnp.concatenate([jnp.where(low, full, come), jnp.where(low, come, full)])
        step *= 2
    return full.reshape((-1,) + payload.shape[1:])


def scatter_rows(terms):
    size = lax.axis_size("hi")
    place = lax.axis_index("hi")
    step = size // 2
    while step:
        halves = terms.reshape((2, -1) + terms.shape[1:])
        bit = (place // step) % 2
        come = lax.ppermute(pick(halves, 1 - bit), "hi", [(i, i ^ step) for i in range(size)])
        terms = (pick(halves, bit).astype(f32) + come.astype(f32)).astype(terms.dtype)
        step //= 2
    return lax.psum_scatter(terms, "seq", scatter_dimension=0, tiled=True)


def sum_everywhere(v):
    for axis in AXES[::-1]:
        size = lax.axis_size(axis)
        step = 1
        while step < size:
            v = v + lax.ppermute(v, axis, [(i, i ^ step) for i in range(size)])
            step *= 2
    return v


def body(
    tokens,
    cotangent,
    image_lengths,
    qkv_weight,
    out_weight,
    up_weight,
    down_weight,
    up_bias,
    norm_scale,
    shifts,
):
    rows, width = tokens.shape
    layers, held = qkv_weight.shape[0], qkv_weight.shape[1]
    blocks, seqs = lax.axis_size("hi"), lax.axis_size("seq")
    ways = seqs // RANKS
    shards = blocks * seqs
    chunk = seqs * held
    heads = HEADS // RANKS
    dim = width // HEADS
    part = width // RANKS
    ff = up_weight.shape[2]
    ff_part = ff // RANKS
    ff_pad = -(-ff_part // 128) * 128
    assert ff_pad % shards == 0
    xi, ci = lax.axis_index("x"), lax.axis_index("c")
    rank = 2 * xi + ci

    def mixed_order(v):
        lead = v.shape[:-1]
        v = v.reshape(lead + (blocks, RANKS, seqs, held))
        return jnp.swapaxes(v, -3, -2).reshape(lead + (width,))

    def plain_order(v):
        lead = v.shape[:-1]
        v = v.reshape(lead + (blocks, seqs, RANKS, held))
        return jnp.swapaxes(v, -3, -2).reshape(lead + (width,))

    def mine(v):
        return pick(v.reshape(blocks, seqs, RANKS, held), rank, 2).reshape(part)

    there = []
    for b in range(blocks):
        for r in range(RANKS):
            for s in range(seqs):
                target = (b * RANKS + s % RANKS) * seqs + r * ways + s // RANKS
                there.append(((b * RANKS + r) * seqs + s, target))
    back = [(target, source) for source, target in there]

    def rank_columns(piece):
        piece = piece.reshape(held, 3, blocks, RANKS, chunk)
        return piece.transpose(3, 0, 1, 2, 4).reshape(RANKS, held, 3 * part)

    def ff_columns(piece):
        piece = piece.reshape(held, RANKS, ff_part).transpose(1, 0, 2)
        return jnp.pad(piece, ((0, 0), (0, 0), (0, ff_pad - ff_part)))

    smalls = jnp.concatenate([norm_scale, shifts], axis=2)
    kinds = smalls.shape[2]
    small_size = layers * kinds * held
    small_row = smalls.transpose(0, 2, 1).reshape(1, 1, small_size)
    small_row = jnp.pad(small_row, ((0, 0), (0, 0), (0, 3 * part - small_size)))
    small_row = jnp.broadcast_to(small_row, (RANKS, 1, 3 * part))
    extra = 8
    assert RANKS * small_size <= extra * width

    gathered_attn, gathered_ff = [], []
    small_full = None
    for l in range(layers):
        sent = rank_columns(qkv_weight[l])
        if l == 0:
            sent = jnp.concatenate([sent, small_row], axis=1)
        came = exchange(sent)
        out_piece = mixed_order(out_weight[l]).reshape(held, RANKS, part).transpose(1, 0, 2)
        payload = jnp.concatenate([came[:, :held], out_piece], axis=2)
        payload = payload.reshape(RANKS * held, width)
        if l == 0:
            small_block = came[:, held, :small_size].reshape(RANKS * small_size)
            small_block = jnp.pad(small_block, (0, extra * width - RANKS * small_size))
            payload = jnp.concatenate([payload, small_block.reshape(extra, width)], axis=0)
        full = gather_rows(payload)
        if l == 0:
            full = full.reshape(shards, RANKS * held + extra, width)
            small_full = full[:, RANKS * held :].reshape(shards, extra * width)
            small_full = small_full[:, : RANKS * small_size]
            small_full = small_full.reshape(shards, RANKS, layers, kinds, held)
            small_full = small_full.transpose(2, 3, 0, 1, 4).reshape(layers, kinds, width)
            small_full = small_full.astype(f32)
            full = full[:, : RANKS * held].reshape(width, width)
        qkv_full = full[:, : 3 * part]
        out_full = full[:, 3 * part :].reshape(shards, RANKS, held, part)
        out_full = out_full.transpose(0, 2, 1, 3).reshape(part, width)
        gathered_attn.append((qkv_full, out_full))
        sent = jnp.concatenate([ff_columns(up_weight[l]), ff_columns(down_weight[l])], axis=2)
        payload = exchange(sent).reshape(RANKS * held, 2 * ff_pad)
        full = gather_rows(payload)
        gathered_ff.append((full[:, :ff_pad], full[:, ff_pad:]))
    up_shift = pick(up_bias.reshape(layers, RANKS, ff_part), rank, 1).astype(f32)
    up_shift = jnp.pad(up_shift, ((0, 0), (0, ff_pad - ff_part)))

    held_rows = 2 * rows
    lengths = lax.ppermute(image_lengths, AXES, there)
    finish = jnp.cumsum(lengths[0])
    base = jnp.arange(rows, dtype=jnp.int32)
    local = jnp.concatenate(
        [base + (2 * x + c) * rows for c in (ci, 1 - ci) for x in (0, 1)]
    )
    group = RANKS * rows
    query_pos = local + (lax.axis_index("seq") % ways) * group
    key_pos = jnp.concatenate([local + w * group for w in range(ways)])

    def ids_of(pos):
        return jnp.sum((pos[:, None] >= finish[None, :]).astype(jnp.int32), axis=1)

    query_ids, key_ids = ids_of(query_pos), ids_of(key_pos)
    seq_groups = [[j * ways + w for w in range(ways)] for j in range(seqs // ways)]

    def keys_of(qkv):
        if ways == 1:
            return qkv, part
        kv = lax.all_gather(
            qkv[:, part:], "seq", axis=0, tiled=True, axis_index_groups=seq_groups
        )
        return kv, 0

    def to_group(v):
        own = lax.ppermute(mixed_order(v), AXES, there)
        return jnp.concatenate(x_order(own, swap_x(own)), axis=0)

    def share(own):
        return jnp.concatenate([own, swap_c(own)], axis=0)

    def reduce_core(own, other):
        return (own + swap_c(other).astype(f32)).astype(bf16)

    def reduce_all(own, other):
        q = reduce_core(own, other)
        return q.astype(f32) + swap_x(q).astype(f32)

    def reduce_mine(own, other):
        q = reduce_core(own, other).reshape(2, rows, width)
        come = swap_x(pick(q, 1 - xi))
        return pick(q, xi).astype(f32) + come.astype(f32)

    def my_rows(v):
        return pick(v.reshape(2, rows, width), xi)

    current = to_group(tokens).astype(f32)
    saved = []
    output = None
    for l in range(layers):
        qkv_full, out_full = gathered_attn[l]
        up_full, down_full = gathered_ff[l]
        gain_one, gain_two, off_one, q_shift, v_shift, o_shift, off_two, d_shift = small_full[l]
        attn_in = share(norm(current, gain_one, off_one).astype(bf16))
        qkv_shift = jnp.concatenate([mine(q_shift), jnp.zeros((part,), f32), mine(v_shift)])
        qkv = (dot(attn_in, qkv_full) + qkv_shift).astype(bf16)
        kv, kv_offset = keys_of(qkv)
        attended = attend(qkv, kv, kv_offset, query_ids, key_ids, heads, dim)
        other = dot(attended[held_rows:], out_full, bf16)
        own = dot(attended[:held_rows], out_full)
        after_attn = current + (reduce_all(own, other) + o_shift)
        mlp_in = share(norm(after_attn, gain_two, off_two).astype(bf16))
        hidden = dot(mlp_in, up_full) + up_shift[l]
        activated = gelu_tanh(hidden).astype(bf16)
        other = dot_last(activated[held_rows:], down_full, bf16)
        own = dot_last(activated[:held_rows], down_full)
        saved.append((current, attn_in, qkv, kv, kv_offset, attended, after_attn, mlp_in, hidden, activated))
        if l < layers - 1:
            current = after_attn + (reduce_all(own, other) + d_shift)
        else:
            final = my_rows(after_attn) + (reduce_mine(own, other) + d_shift)
            output = lax.ppermute(final.astype(bf16), AXES, back)
            output = plain_order(output).astype(f32)

    grads = [None] * layers
    bias_rows = [None] * layers
    down_in = to_group(cotangent)
    grad_current = down_in.astype(f32)
    tokens_grad = None
    for l in reversed(range(layers)):
        (current, attn_in, qkv, kv, kv_offset, attended, after_attn, mlp_in, hidden, activated) = saved[l]
        qkv_full, out_full = gathered_attn[l]
        up_full, down_full = gathered_ff[l]
        gain_one, gain_two = small_full[l, 0], small_full[l, 1]
        down_in = share(down_in)
        grad_act = dot(down_in, down_full)
        hidden_grad = jax.vjp(gelu_tanh, hidden)[1](grad_act)[0].astype(bf16)
        other = dot_last(hidden_grad[held_rows:], up_full, bf16)
        own = dot_last(hidden_grad[:held_rows], up_full)
        d_sum = 0.5 * jnp.sum(down_in[:held_rows].astype(f32), axis=0)
        bias_sum = jnp.sum(hidden_grad.astype(f32), axis=0)
        resid, gain_two_sum, off_two_sum = norm_back(after_attn, gain_two, reduce_all(own, other))
        grad_current = grad_current + resid
        ff_terms = jnp.concatenate(
            [dot_rows(mlp_in, hidden_grad, bf16), dot_rows(down_in, activated, bf16)], axis=1
        ).reshape(shards, RANKS * held, 2 * ff_pad)
        piece = ff_pad // shards
        bias_row = jnp.pad(
            bias_sum.astype(bf16).reshape(shards, 1, piece),
            ((0, 0), (0, extra - 1), (0, 2 * ff_pad - piece)),
        )
        ff_terms = jnp.concatenate([ff_terms, bias_row], axis=1)
        ff_owned = scatter_rows(
            ff_terms.reshape(shards * (RANKS * held + extra), 2 * ff_pad)
        )
        bias_rows[l] = ff_owned[RANKS * held, :piece]
        ff_owned = exchange(ff_owned[: RANKS * held].reshape(RANKS, held, 2 * ff_pad))
        up_grad = ff_owned[:, :, :ff_part].transpose(1, 0, 2).reshape(held, ff)
        down_grad = ff_owned[:, :, ff_pad : ff_pad + ff_part].transpose(1, 0, 2).reshape(held, ff)

        out_own = grad_current.astype(bf16)
        o_sum = 0.5 * jnp.sum(out_own.astype(f32), axis=0)
        out_in = share(out_own)
        attended_grad = dot_last(out_in, out_full, bf16)
        q_grad, kv_grad = attend_back(
            qkv, kv, kv_offset, query_ids, key_ids, attended_grad, heads, dim
        )
        if ways > 1:
            kv_grad = lax.psum_scatter(
                kv_grad, "seq", scatter_dimension=0, tiled=True, axis_index_groups=seq_groups
            )
        qkv_grad = jnp.concatenate([q_grad, kv_grad], axis=1)
        other = dot_last(qkv_grad[held_rows:], qkv_full, bf16)
        own = dot_last(qkv_grad[:held_rows], qkv_full)
        column_sums = jnp.sum(qkv_grad.astype(f32), axis=0)

        def placed(v):
            spots = (jnp.arange(RANKS) == rank)[None, None, :, None]
            return jnp.where(spots, v.reshape(blocks, seqs, 1, held), 0.0).reshape(width)

        if l > 0:
            resid, gain_one_sum, off_one_sum = norm_back(current, gain_one, reduce_all(own, other))
            grad_current = grad_current + resid
            gain_one_sum, off_one_sum = 0.5 * gain_one_sum, 0.5 * off_one_sum
            down_in = grad_current.astype(bf16)
        else:
            resid, gain_one_sum, off_one_sum = norm_back(
                my_rows(current), gain_one, reduce_mine(own, other)
            )
            final = my_rows(grad_current) + resid
            tokens_grad = lax.ppermute(final.astype(bf16), AXES, back)
            tokens_grad = plain_order(tokens_grad).astype(f32)
        vectors = jnp.stack(
            [
                gain_one_sum,
                0.5 * gain_two_sum,
                off_one_sum,
                placed(column_sums[:part]),
                placed(column_sums[2 * part :]),
                o_sum,
                0.5 * off_two_sum,
                d_sum,
            ]
        )
        vectors = vectors.astype(bf16).reshape(kinds, shards, RANKS, held)
        vectors = vectors.transpose(1, 2, 0, 3).reshape(shards, 1, RANKS * kinds * held)
        vectors = jnp.pad(
            vectors, ((0, 0), (0, 0), (0, extra * width - RANKS * kinds * held))
        ).reshape(shards, extra, width)
        out_terms = dot_rows(attended, out_in, bf16).reshape(shards, held, RANKS, part)
        out_terms = out_terms.transpose(0, 2, 1, 3).reshape(shards, RANKS * held, part)
        qkv_terms = dot_rows(attn_in, qkv_grad, bf16).reshape(shards, RANKS * held, 3 * part)
        attn_terms = jnp.concatenate(
            [jnp.concatenate([qkv_terms, out_terms], axis=2), vectors], axis=1
        )
        owned = scatter_rows(attn_terms.reshape(shards * (RANKS * held + extra), width))
        out_grad = owned[: RANKS * held, 3 * part :].reshape(RANKS, held, part)
        out_grad = plain_order(out_grad.transpose(1, 0, 2).reshape(held, width))
        vector_row = owned[RANKS * held :].reshape(extra * width)[: RANKS * kinds * held]
        vector_row = vector_row.reshape(RANKS, 1, kinds * held)
        vector_row = jnp.pad(vector_row, ((0, 0), (0, 0), (0, 3 * part - kinds * held)))
        came = exchange(
            jnp.concatenate(
                [owned[: RANKS * held, : 3 * part].reshape(RANKS, held, 3 * part), vector_row],
                axis=1,
            )
        )
        qkv_out = came[:, :held].reshape(RANKS, held, 3, blocks, chunk)
        qkv_out = qkv_out.transpose(1, 2, 3, 0, 4).reshape(held, 3 * width)
        sums = jnp.sum(came[:, held, : kinds * held].astype(f32), axis=0).reshape(kinds, held)
        grads[l] = (
            qkv_out.astype(f32),
            out_grad.astype(f32),
            up_grad.astype(f32),
            down_grad.astype(f32),
            sums[:2].T,
            sums[2:].T,
        )

    bias = jnp.stack(bias_rows)
    place = jnp.arange(shards * RANKS) == lax.axis_index(AXES)
    bias = jnp.where(place[:, None, None], bias[None], jnp.zeros((), bf16))
    bias = sum_everywhere(bias.reshape(shards * RANKS, -1))
    bias = bias.reshape(blocks, RANKS, seqs, layers, -1).transpose(3, 1, 0, 2, 4)
    bias = bias.reshape(layers, RANKS, ff_pad)[:, :, :ff_part].reshape(layers, ff)
    stacked = [jnp.stack([grads[l][i] for l in range(layers)]) for i in range(6)]
    return (
        output,
        tokens_grad,
        stacked[0],
        stacked[1],
        stacked[2],
        stacked[3],
        bias.astype(f32),
        stacked[4],
        stacked[5],
    )


def solution(mesh):
    sizes = mesh.shape
    devices = mesh.devices.reshape(sizes["img"] // RANKS, 2, 2, sizes["seq"])
    fine = Mesh(devices, AXES)
    row = P(AXES, None)
    param = P(None, AXES, None)
    in_specs = (row, row, P(AXES[:3], None), param, param, param, param, P(), param, param)
    out_specs = (row, row, param, param, param, param, P(), param, param)
    return jax.shard_map(
        body, mesh=fine, in_specs=in_specs, out_specs=out_specs, check_vma=False
    )
```

time: 3500 us -> 1000 us (0.29)
  waiting for transfers between devices: 2200 us -> 316 us
  local copies, waits for them, and re-layouts: 575 us -> 197 us
  blocking collectives: 349 us -> 0 us
  starting transfers between devices: 0.52 us -> 135 us
  matrix products: 254 us -> 138 us
  other arithmetic: 42.4 us -> 124 us
  Pallas kernels: 0 us -> 64.3 us
  loops' own time: 42.8 us -> 0 us
    unnamed x14 -> x8, waiting for transfers between devices: 1650 us -> 96.8 us
    all_gather x10 -> x4, waiting for transfers between devices: 467 us -> 31.3 us  [gather_rows(): full = lax.all_gather(payload, 'seq', axis=0, tiled=True)[None]]
    all_gather x4 -> x0, blocking collectives: 305 us -> none  [the longest x2 153 us: fetch_layer(): lax.all_gather(gain_piece, ('img', 'seq'), axis=0, tiled=True)]
    concatenate x2 -> x9, local copies, waits for them, and re-layouts: 280 us -> 18.6 us  [the longest x2 17.7 us: body(): jnp.concatenate([dot_rows(mlp_in, hidden_grad, bf16), dot_rows(down_in, a...]
    ppermute x0 -> x60, waiting for transfers between devices: none -> 169 us  [the longest x4 76 us: gather_rows(): come = lax.ppermute(full, 'hi', [(i, i ^ step) for i in range(size)])]
    all_gather x6 -> x0, local copies, waits for them, and re-layouts: 162 us -> none  [the longest x2 80.9 us: fetch_layer(): lax.all_gather(up_piece, ('img', 'seq'), axis=0, tiled=True)]
    ppermute x0 -> x60, starting transfers between devices: none -> 135 us  [the longest x24 59.3 us: swap_c(): return lax.ppermute(v, 'c', SWAP)]
    dot_general x60 -> x32, matrix products: 254 us -> 138 us  [the longest x14 53.7 us: dot_last(): lax.dot_general(left, right, dims, preferred_element_type=f32).astype(kind)]
  transfers between devices with their start and end apart: 13 -> 67, of which waited for: 10 -> 27; matrix products, arithmetic and copies ran while one was open for 14% -> 43% of each run, Pallas kernels for 0% -> 6%
where the time goes in v1:
time: 1000 us; the launch traced here: 992 us
  waiting for transfers between devices  316 us (32%)
  local copies, waits for them, and re-layouts  197 us (20%)
  matrix products  138 us (14%)
  starting transfers between devices  135 us (14%)
  other arithmetic  124 us (12%)
  Pallas kernels  64.3 us (6%)
  between operations  17.8 us (2%)
    unnamed x8, waiting for transfers between devices  96.8 us
    ppermute x4, waiting for transfers between devices, gather_rows(): come = lax.ppermute(full, 'hi', [(i, i ^ step) for i in range(size)])  76 us
    ppermute x18, waiting for transfers between devices, swap_x(): return lax.ppermute(v, 'x', SWAP)  72.9 us
    ppermute x24, starting transfers between devices, swap_c(): return lax.ppermute(v, 'c', SWAP)  59.3 us
    dot_general x14, matrix products, dot_last(): lax.dot_general(left, right, dims, preferred_element_type=f32).astype(kind)  53.7 us
    dot_general x10, matrix products, dot(): return jnp.dot(left, right, preferred_element_type=f32).astype(kind)  47.3 us
    pallas_call x2, Pallas kernels, attend_back(): pl.pallas_call(functools.partial(attend_back_kernel, heads, dim, offset),...  43.7 us
    dot_general x8, matrix products, dot_rows(): lax.dot_general(left, right, dims, preferred_element_type=f32).astype(kind)  36.8 us
  transfers between devices with their start and end apart: 67, of which 27 were waited for; matrix products, arithmetic and copies ran while one was open for 43% of the time, Pallas kernels for 6%

profile of v1, /device:TPU:1, one launch (start us, length us, event | category | flops | bytes accessed | tf_op | source)
XLA Modules:
  0.0 992.5 jit_solution(18355885611187286301)
XLA Ops:
  66.4 9.4 all-gather.5.cloned.1.call-done
  81.5 25.5 %collective-permute-done.5 = bf16[1,608,1152]{2,1,0:T(8,128)(2,1)} collective-permute-done((bf16[1,608,1152]{2,1,0:T(8,128)(2,1)}, bf16[1,608,1152]{2,1,0:T(8,128)(2,1)}, u32[]{:S(2)}, u32[]{:S(2)}) %collective-permute-start.5) | collective-permute-done | bytes 1400864 | tf_op jit(solution)/shard_map/ppermute | solution.py:210
  137.0 10.4 %shard_map.169 = bf16[1024,288]{1,0:T(8,128)(2,1)S(1)} custom-call(s32[1024,1]{1,0:T(8,128)S(1)} %copy.538.qid_ref, s32[1,1024]{1,0:T(1,128)S(1)} %bitcast.384, bf16[1024,864]{1,0:T(8,128)(2,1)S(1)} %add_convert_fusion.1.q_ref.kv_ref, bf16[1024,864]{1,0:T(8,128)(2,1)S(1)} %add_convert_fusion.1.q_ref.kv_ref), custom_call_target="tpu_custom_call" | custom-call | flops 1207959552 | bytes 2359296 | tf_op jit(solution)/shard_map/pallas_call | solution.py:44
  160.3 22.7 %collective-permute-done.8 = bf16[512,1152]{1,0:T(8,128)(2,1)} collective-permute-done((bf16[512,1152]{1,0:T(8,128)(2,1)}, bf16[512,1152]{1,0:T(8,128)(2,1)}, u32[]{:S(2)}, u32[]{:S(2)}) %collective-permute-start.8) | collective-permute-done | bytes 1179680 | tf_op jit(solution)/shard_map/ppermute | solution.py:178
  187.7 27.8 %collective-permute-done.12 = bf16[1,576,2304]{2,1,0:T(8,128)(2,1)} collective-permute-done((bf16[1,576,2304]{2,1,0:T(8,128)(2,1)}, bf16[1,576,2304]{2,1,0:T(8,128)(2,1)}, u32[]{:S(2)}, u32[]{:S(2)}) %collective-permute-start.12) | collective-permute-done | bytes 2654240 | tf_op jit(solution)/shard_map/ppermute | solution.py:210
  243.0 21.8 %all-gather.9.cloned.1.call-done = bf16[576,1152]{1,0:T(8,128)(2,1)} async-done(((bf16[144,1152]{1,0:T(8,128)(2,1)}), bf16[576,1152]{1,0:T(8,128)(2,1)}) %all-gather.9.cloned.1.call-update) | async-done | bytes 1327120 | tf_op jit(solution)/shard_map/all_gather | solution.py:207
  273.7 20.7 %collective-permute-done.18 = bf16[1,576,1152]{2,1,0:T(8,128)(2,1)S(1)} collective-permute-done((bf16[1,576,1152]{2,1,0:T(8,128)(2,1)}, bf16[1,576,1152]{2,1,0:T(8,128)(2,1)S(1)}, u32[]{:S(2)}, u32[]{:S(2)}) %collective-permute-start.18) | collective-permute-done | bytes 1327136 | tf_op jit(solution)/shard_map/ppermute | solution.py:210
  308.2 10.2 %shard_map.170 = bf16[1024,288]{1,0:T(8,128)(2,1)S(1)} custom-call(s32[1024,1]{1,0:T(8,128)S(1)} %copy.538.qid_ref, s32[1,1024]{1,0:T(1,128)S(1)} %bitcast.385, bf16[1024,864]{1,0:T(8,128)(2,1)S(1)} %add_convert_fusion.q_ref.kv_ref, bf16[1024,864]{1,0:T(8,128)(2,1)S(1)} %add_convert_fusion.q_ref.kv_ref), custom_call_target="tpu_custom_call" | custom-call | flops 1207959552 | bytes 2359296 | tf_op jit(solution)/shard_map/pallas_call | solution.py:44
  335.4 12.5 %collective-permute-done.28 = bf16[256,1152]{1,0:T(8,128)(2,1)} collective-permute-done((bf16[256,1152]{1,0:T(8,128)(2,1)}, bf16[256,1152]{1,0:T(8,128)(2,1)}, u32[]{:S(2)}, u32[]{:S(2)}) %collective-permute-start.28) | collective-permute-done | bytes 589856 | tf_op jit(solution)/shard_map/ppermute | solution.py:366
  368.2 15.2 %collective-permute-start.30 = (bf16[512,1152]{1,0:T(8,128)(2,1)}, bf16[512,1152]{1,0:T(8,128)(2,1)}, u32[]{:S(2)}, u32[]{:S(2)}) collective-permute-start(bf16[512,1152]{1,0:T(8,128)(2,1)} %pad_maximum_fusion.37), channel_id=1, source_target_pairs={{0,4},{4,0},{1,5},{5,1},{2,6},{6,2},{3,7},{7,3},{8,12},{12,8},{9,1... | collective-permute-start | bytes 3538952 | tf_op jit(solution)/shard_map/ppermute | solution.py:182
  393.2 8.4 collective-permute-start.21
  424.1 13.5 %collective-permute-start.25 = (bf16[512,1152]{1,0:T(8,128)(2,1)}, bf16[512,1152]{1,0:T(8,128)(2,1)}, u32[]{:S(2)}, u32[]{:S(2)}) collective-permute-start(bf16[512,1152]{1,0:T(8,128)(2,1)} %convolution_convert_fusion.10), channel_id=1, source_target_pairs={{0,4},{4,0},{1,5},{5,1},{2,6},{6,2},{3,7},{7,3},{8,12},{12,8},{9,1... | collective-permute-start | bytes 3538952 | tf_op jit(solution)/shard_map/ppermute | solution.py:182
  437.6 8.2 fusion.197
  463.1 9.0 copy.611
  507.7 12.2 %collective-permute-start.27 = (bf16[256,1152]{0,1:T(8,128)(2,1)}, bf16[256,1152]{0,1:T(8,128)(2,1)}, u32[]{:S(2)}, u32[]{:S(2)}) collective-permute-start(bf16[256,1152]{0,1:T(8,128)(2,1)} %fusion.93), channel_id=1, source_target_pairs={{0,0},{4,1},{8,2},{12,3},{1,4},{5,5},{9,6},{13,7},{2,8},{6,9},{10,... | collective-permute-start | bytes 1769480 | tf_op jit(solution)/shard_map/ppermute | solution.py:412
  525.6 21.6 %shard_map.171 = (bf16[1024,288]{1,0:T(8,128)(2,1)}, bf16[1024,576]{1,0:T(8,128)(2,1)}) custom-call(s32[1,1024]{1,0:T(1,128)} %bitcast.487, s32[1024,1]{1,0:T(8,128)} %copy.567.kid_ref, bf16[1024,864]{1,0:T(8,128)(2,1)} %copy-done.3, bf16[1024,864]{1,0:T(8,128)(2,1)} %copy-done.3, bf16[1024,288]{1,0:T(8,128)(2,1)} %copy.568.do_ref), custom_call_target="tpu_custom_call" | custom-call | flops 3019898880 | bytes 5898240 | tf_op jit(solution)/shard_map/pallas_call | solution.py:108
  607.8 9.0 fusion.198
  634.1 8.7 copy.604
  665.8 19.5 %collective-permute-done.38 = bf16[512,1152]{1,0:T(8,128)(2,1)S(1)} collective-permute-done((bf16[512,1152]{1,0:T(8,128)(2,1)S(1)}, bf16[512,1152]{1,0:T(8,128)(2,1)S(1)}, u32[]{:S(2)}, u32[]{:S(2)}) %collective-permute-start.38) | collective-permute-done | bytes 1179680 | tf_op jit(solution)/shard_map/ppermute | solution.py:178
  700.8 22.1 %shard_map.172 = (bf16[1024,288]{1,0:T(8,128)(2,1)}, bf16[1024,576]{1,0:T(8,128)(2,1)}) custom-call(s32[1,1024]{1,0:T(1,128)} %bitcast.488, s32[1024,1]{1,0:T(8,128)} %copy.567.kid_ref, bf16[1024,864]{1,0:T(8,128)(2,1)} %copy-done.2, bf16[1024,864]{1,0:T(8,128)(2,1)} %copy-done.2, bf16[1024,288]{1,0:T(8,128)(2,1)} %copy.572.do_ref), custom_call_target="tpu_custom_call" | custom-call | flops 3019898880 | bytes 5898240 | tf_op jit(solution)/shard_map/pallas_call | solution.py:108
  767.1 6.8 collective-permute-start.42
  785.8 19.4 %reduce-scatter.3.cloned.1.call-done = bf16[152,2304]{1,0:T(8,128)(2,1)} async-done(((bf16[608,2304]{1,0:T(8,128)(2,1)}), bf16[152,2304]{1,0:T(8,128)(2,1)}) %reduce-scatter.3.cloned.1.call-update) | async-done | bytes 700432 | tf_op jit(solution)/shard_map/reduce_scatter | solution.py:227
  806.1 8.6 collective-permute-start.55
  864.9 96.7 %all-reduce.18.cloned.1.call-done = (bf16[608,1152]{1,0:T(8,128)(2,1)}, bf16[608,1152]{1,0:T(8,128)(2,1)}) async-done(((bf16[608,1152]{1,0:T(8,128)(2,1)}, bf16[608,1152]{1,0:T(8,128)(2,1)}), (bf16[608,1152]{1,0:T(8,128)(2,1)}, bf16[608,1152]{1,0:T(8,128)(2,1)})) %all-reduce.18.cloned.1.call-update) | async-done | bytes 2801680
  (758 shorter events, 534.7 us)
Async XLA Ops:
  7.2 68.7 %all-gather.5.cloned.1.call-start = ((), (), s32[]{:S(2)}) async-start(), calls=%async_computation.2 | async-start | bytes 1751040 | tf_op jit(solution)/shard_map/all_gather | solution.py:207
  18.6 45.0 %collective-permute-start = (bf16[256,1152]{1,0:T(8,128)(2,1)}, bf16[256,1152]{1,0:T(8,128)(2,1)}, u32[]{:S(2)}, u32[]{:S(2)}) collective-permute-start(bf16[256,1152]{1,0:T(8,128)(2,1)} %copy.527), channel_id=1, source_target_pairs={{0,0},{1,4},{2,8},{3,12},{4,1},{5,5},{6,9},{7,13},{8,2},{9,6},{10,... | collective-permute-start | bytes 1769480 | tf_op jit(solution)/shard_map/ppermute | solution.py:366
  43.4 113.1 %all-gather.7.cloned.1.call-start = ((), (), s32[]{:S(2)}) async-start(), calls=%async_computation.3 | async-start | bytes 3317760 | tf_op jit(solution)/shard_map/all_gather | solution.py:207
  75.8 31.1 %collective-permute-start.5 = (bf16[1,608,1152]{2,1,0:T(8,128)(2,1)}, bf16[1,608,1152]{2,1,0:T(8,128)(2,1)}, u32[]{:S(2)}, u32[]{:S(2)}) collective-permute-start(bf16[1,608,1152]{2,1,0:T(8,128)(2,1)} %bitcast.442), channel_id=1, source_target_pairs={{0,16},{16,0},{1,17},{17,1},{2,18},{18,2},{3,19},{19,3},{4,20},{20... | collective-permute-start | bytes 4202504 | tf_op jit(solution)/shard_map/ppermute | solution.py:210
  79.1 185.8 %all-gather.9.cloned.1.call-start = ((), (), s32[]{:S(2)}) async-start(), calls=%async_computation.4 | async-start | bytes 1658880 | tf_op jit(solution)/shard_map/all_gather | solution.py:207
  156.5 59.0 %collective-permute-start.12 = (bf16[1,576,2304]{2,1,0:T(8,128)(2,1)}, bf16[1,576,2304]{2,1,0:T(8,128)(2,1)}, u32[]{:S(2)}, u32[]{:S(2)}) collective-permute-start(bf16[1,576,2304]{2,1,0:T(8,128)(2,1)} %bitcast.434), channel_id=1, source_target_pairs={{0,16},{16,0},{1,17},{17,1},{2,18},{18,2},{3,19},{19,3},{4,20},{20... | collective-permute-start | bytes 7962632 | tf_op jit(solution)/shard_map/ppermute | solution.py:210
  159.4 68.9 %collective-permute-start.16 = (bf16[2,36,864]{2,0,1:T(2,128)(2,1)S(1)}, bf16[2,36,864]{2,0,1:T(2,128)(2,1)S(1)}, u32[]{:S(2)}, u32[]{:S(2)}) collective-permute-start(bf16[2,36,864]{2,0,1:T(2,128)(2,1)S(1)} %dynamic-slice_bitcast_fusion.6), channel_id=1, source_target_pairs={{0,8},{8,0},{1,9},{9,1},{2,10},{10,2},{3,11},{11,3},{4,12},{12,4},... | collective-permute-start | bytes 373256 | tf_op jit(solution)/shard_map/ppermute | solution.py:178
  186.7 31.4 %collective-permute-start.9 = (bf16[512,1152]{1,0:T(8,128)(2,1)S(1)}, bf16[512,1152]{1,0:T(8,128)(2,1)S(1)}, u32[]{:S(2)}, u32[]{:S(2)}) collective-permute-start(bf16[512,1152]{1,0:T(8,128)(2,1)S(1)} %add_convert_fusion.11), channel_id=1, source_target_pairs={{0,4},{4,0},{1,5},{5,1},{2,6},{6,2},{3,7},{7,3},{8,12},{12,8},{9,1... | collective-permute-start | bytes 3538952 | tf_op jit(solution)/shard_map/ppermute | solution.py:182
  234.2 122.7 %all-gather.11.cloned.1.call-start = ((), (), s32[]{:S(2)}) async-start(), calls=%async_computation.5 | async-start | bytes 3317760 | tf_op jit(solution)/shard_map/all_gather | solution.py:207
  242.9 406.8 %reduce-scatter.5.cloned.1.call-start = ((), (), s32[]{:S(2)}) async-start(), calls=%async_computation.7 | async-start | bytes 3502080 | tf_op jit(solution)/shard_map/reduce_scatter | solution.py:227
  272.6 30.2 %collective-permute-start.15 = (bf16[512,1152]{1,0:T(8,128)(2,1)}, bf16[512,1152]{1,0:T(8,128)(2,1)}, u32[]{:S(2)}, u32[]{:S(2)}) collective-permute-start(bf16[512,1152]{1,0:T(8,128)(2,1)} %add_convert_fusion.9), channel_id=1, source_target_pairs={{0,4},{4,0},{1,5},{5,1},{2,6},{6,2},{3,7},{7,3},{8,12},{12,8},{9,1... | collective-permute-start | bytes 3538952 | tf_op jit(solution)/shard_map/ppermute | solution.py:182
  320.2 37.9 %collective-permute-start.19 = (bf16[512,1152]{1,0:T(8,128)(2,1)}, bf16[512,1152]{1,0:T(8,128)(2,1)}, u32[]{:S(2)}, u32[]{:S(2)}) collective-permute-start(bf16[512,1152]{1,0:T(8,128)(2,1)} %convolution_convert_fusion.11), channel_id=1, source_target_pairs={{0,4},{4,0},{1,5},{5,1},{2,6},{6,2},{3,7},{7,3},{8,12},{12,8},{9,1... | collective-permute-start | bytes 3538952 | tf_op jit(solution)/shard_map/ppermute | solution.py:182
  356.9 46.8 %collective-permute-start.24 = (bf16[1,576,2304]{2,1,0:T(8,128)(2,1)}, bf16[1,576,2304]{2,1,0:T(8,128)(2,1)}, u32[]{:S(2)}, u32[]{:S(2)}) collective-permute-start(bf16[1,576,2304]{2,1,0:T(8,128)(2,1)} %bitcast.435), channel_id=1, source_target_pairs={{0,16},{16,0},{1,17},{17,1},{2,18},{18,2},{3,19},{19,3},{4,20},{20... | collective-permute-start | bytes 7962632 | tf_op jit(solution)/shard_map/ppermute | solution.py:210
  368.2 69.4 %collective-permute-start.30 = (bf16[512,1152]{1,0:T(8,128)(2,1)}, bf16[512,1152]{1,0:T(8,128)(2,1)}, u32[]{:S(2)}, u32[]{:S(2)}) collective-permute-start(bf16[512,1152]{1,0:T(8,128)(2,1)} %pad_maximum_fusion.37), channel_id=1, source_target_pairs={{0,4},{4,0},{1,5},{5,1},{2,6},{6,2},{3,7},{7,3},{8,12},{12,8},{9,1... | collective-permute-start | bytes 3538952 | tf_op jit(solution)/shard_map/ppermute | solution.py:182
  424.1 48.0 %collective-permute-start.25 = (bf16[512,1152]{1,0:T(8,128)(2,1)}, bf16[512,1152]{1,0:T(8,128)(2,1)}, u32[]{:S(2)}, u32[]{:S(2)}) collective-permute-start(bf16[512,1152]{1,0:T(8,128)(2,1)} %convolution_convert_fusion.10), channel_id=1, source_target_pairs={{0,4},{4,0},{1,5},{5,1},{2,6},{6,2},{3,7},{7,3},{8,12},{12,8},{9,1... | collective-permute-start | bytes 3538952 | tf_op jit(solution)/shard_map/ppermute | solution.py:182
  501.7 68.2 %collective-permute-start.52 = (bf16[608,2304]{1,0:T(8,128)(2,1)}, bf16[608,2304]{1,0:T(8,128)(2,1)}, u32[]{:S(2)}, u32[]{:S(2)}) collective-permute-start(bf16[608,2304]{1,0:T(8,128)(2,1)} %dynamic-slice_bitcast_fusion), channel_id=1, source_target_pairs={{0,16},{16,0},{1,17},{17,1},{2,18},{18,2},{3,19},{19,3},{4,20},{20... | collective-permute-start | bytes 8405000 | tf_op jit(solution)/shard_map/ppermute | solution.py:224
  507.7 44.2 %collective-permute-start.27 = (bf16[256,1152]{0,1:T(8,128)(2,1)}, bf16[256,1152]{0,1:T(8,128)(2,1)}, u32[]{:S(2)}, u32[]{:S(2)}) collective-permute-start(bf16[256,1152]{0,1:T(8,128)(2,1)} %fusion.93), channel_id=1, source_target_pairs={{0,0},{4,1},{8,2},{12,3},{1,4},{5,5},{9,6},{13,7},{2,8},{6,9},{10,... | collective-permute-start | bytes 1769480 | tf_op jit(solution)/shard_map/ppermute | solution.py:412
  574.7 230.5 %reduce-scatter.3.cloned.1.call-start = ((), (), s32[]{:S(2)}) async-start(), calls=%async_computation.6 | async-start | bytes 3502080 | tf_op jit(solution)/shard_map/reduce_scatter | solution.py:227
  622.3 30.5 %collective-permute-start.37 = (bf16[512,1152]{1,0:T(8,128)(2,1)}, bf16[512,1152]{1,0:T(8,128)(2,1)S(1)}, u32[]{:S(2)}, u32[]{:S(2)}) collective-permute-start(bf16[512,1152]{1,0:T(8,128)(2,1)} %convolution_convert_fusion.7), channel_id=1, source_target_pairs={{0,4},{4,0},{1,5},{5,1},{2,6},{6,2},{3,7},{7,3},{8,12},{12,8},{9,1... | collective-permute-start | bytes 3538952 | tf_op jit(solution)/shard_map/ppermute | solution.py:182
  649.1 81.2 %collective-permute-start.49 = (bf16[608,2304]{1,0:T(8,128)(2,1)}, bf16[608,2304]{1,0:T(8,128)(2,1)}, u32[]{:S(2)}, u32[]{:S(2)}) collective-permute-start(bf16[608,2304]{1,0:T(8,128)(2,1)} %dynamic-slice_bitcast_fusion.1), channel_id=1, source_target_pairs={{0,16},{16,0},{1,17},{17,1},{2,18},{18,2},{3,19},{19,3},{4,20},{20... | collective-permute-start | bytes 8405000 | tf_op jit(solution)/shard_map/ppermute | solution.py:224
  735.3 226.4 %all-reduce.18.cloned.1.call-start = ((), (), s32[]{:S(2)}) async-start(), calls=%async_computation.8 | async-start | bytes 5603328
  767.1 55.3 %collective-permute-start.42 = (bf16[256,1152]{0,1:T(8,128)(2,1)}, bf16[256,1152]{0,1:T(8,128)(2,1)}, u32[]{:S(2)}, u32[]{:S(2)}) collective-permute-start(bf16[256,1152]{0,1:T(8,128)(2,1)} %fusion.94), channel_id=1, source_target_pairs={{0,0},{4,1},{8,2},{12,3},{1,4},{5,5},{9,6},{13,7},{2,8},{6,9},{10,... | collective-permute-start | bytes 1769480 | tf_op jit(solution)/shard_map/ppermute | solution.py:481
  783.1 51.6 %collective-permute-start.46 = (bf16[608,1152]{1,0:T(8,128)(2,1)}, bf16[608,1152]{1,0:T(8,128)(2,1)}, u32[]{:S(2)}, u32[]{:S(2)}) collective-permute-start(bf16[608,1152]{1,0:T(8,128)(2,1)} %dynamic-slice_bitcast_fusion.2), channel_id=1, source_target_pairs={{0,16},{16,0},{1,17},{17,1},{2,18},{18,2},{3,19},{19,3},{4,20},{20... | collective-permute-start | bytes 4202504 | tf_op jit(solution)/shard_map/ppermute | solution.py:224
  816.0 31.2 %collective-permute-start.43 = (bf16[608,1152]{1,0:T(8,128)(2,1)}, bf16[608,1152]{1,0:T(8,128)(2,1)}, u32[]{:S(2)}, u32[]{:S(2)}) collective-permute-start(bf16[608,1152]{1,0:T(8,128)(2,1)} %dynamic-slice_bitcast_fusion.3), channel_id=1, source_target_pairs={{0,16},{16,0},{1,17},{17,1},{2,18},{18,2},{3,19},{19,3},{4,20},{20... | collective-permute-start | bytes 4202504 | tf_op jit(solution)/shard_map/ppermute | solution.py:224
  (149 other events, 1971.4 us)
Sparse Core Ops, SparseCore 0:
  43.5 32.2 all-gather.4
  79.2 54.3 all-gather.6
  234.3 30.4 all-gather.8
  266.8 54.9 all-gather.10
  574.8 57.9 reduce-scatter.4
  735.4 69.7 reduce-scatter.2
  850.1 111.5 all-reduce.17

commit v2 on v1

v2 whole, which is shorter than its diff:
```python
import functools
import math

import jax
import jax.numpy as jnp
from jax import lax
from jax.experimental import pallas as pl
from jax.experimental.pallas import tpu as pltpu
from jax.sharding import Mesh
from jax.sharding import PartitionSpec as P

HEADS = 16
RANKS = 4
CHUNKS = 1
EPSILON = 1e-06
NEGATIVE = -1e30
ROOT = math.sqrt(2.0 / math.pi)
AXES = ("hi", "x", "c", "seq")
SWAP = ((0, 1), (1, 0))
bf16, f32 = jnp.bfloat16, jnp.float32
VMEM = pl.BlockSpec(memory_space=pltpu.VMEM)


def mm(left, right):
    return jnp.dot(left, right, preferred_element_type=f32)


def mm_last(left, right):
    dims = (((1,), (1,)), ((), ()))
    return lax.dot_general(left, right, dims, preferred_element_type=f32)


def mm_first(left, right):
    dims = (((0,), (0,)), ((), ()))
    return lax.dot_general(left, right, dims, preferred_element_type=f32)


def shape(dims, kind):
    return jax.ShapeDtypeStruct(tuple(dims), kind)


def params(mib):
    return pltpu.CompilerParams(vmem_limit_bytes=mib * 2**20)


def cost(flops, moved, exps=0):
    share = 0.1
    return pl.CostEstimate(
        flops=int(share * flops), bytes_accessed=int(share * moved), transcendentals=int(share * exps)
    )


def const(dims):
    return pl.BlockSpec(tuple(dims), lambda i: (0,) * len(dims))


def split(half, block, width):
    n = half // block
    own = pl.BlockSpec((block, width), lambda i: (jnp.minimum(i, n - 1), 0))
    rec = pl.BlockSpec((block, width), lambda i: (jnp.maximum(i - n, 0), 0))
    strip = pl.BlockSpec((block, width), lambda i: (i, 0))
    return n, own, rec, strip


def either(own_work, rec_work):
    step, half = pl.program_id(0), pl.num_programs(0) // 2
    pl.when(step < half)(own_work)
    pl.when(step >= half)(rec_work)


def project_kernel(own_ref, rec_ref, w_ref, shift_ref, out_ref):
    width = out_ref.shape[1]

    def work(ref):
        out_ref[...] = (mm(ref[...], w_ref[:, :width]) + shift_ref[...]).astype(bf16)

    either(lambda: work(own_ref), lambda: work(rec_ref))


def project(own, rec, weight, shift):
    half, depth = own.shape
    width = shift.shape[0]
    n, own_spec, rec_spec, _ = split(half, min(half, 256), depth)
    return pl.pallas_call(
        project_kernel,
        grid=(2 * n,),
        in_specs=[own_spec, rec_spec, const(weight.shape), const((1, width))],
        out_specs=pl.BlockSpec((half // n, width), lambda i: (i, 0)),
        out_shape=shape((2 * half, width), bf16),
        compiler_params=params(24),
        cost_estimate=cost(4 * half * depth * width, 2 * depth * (2 * half + width)),
    )(own, rec, weight, shift[None])


def attend_kernel(heads, dim, offset, count, *refs):
    qid_ref, kid_ref, q_ref, wo_ref = refs[:4]
    kv_refs = refs[4 : 4 + count]
    o_ref, own_ref, rec_ref = refs[4 + count :]
    factor = dim**-0.5 * math.log2(math.e)
    width = heads * dim
    same = qid_ref[...] == kid_ref[...]
    outs = []
    for h in range(heads):
        lo = h * dim
        at = offset + width + lo
        q = q_ref[:, lo : lo + dim]
        k = jnp.concatenate([ref[:, offset + lo : offset + lo + dim] for ref in kv_refs])
        v = jnp.concatenate([ref[:, at : at + dim] for ref in kv_refs])
        s = jnp.where(same, mm_last(q, k), NEGATIVE)
        top = jnp.max(s, axis=1, keepdims=True)
        p = jnp.exp2((s - top) * factor)
        total = jnp.sum(p, axis=1, keepdims=True)
        outs.append(mm(p.astype(bf16), v) / total)
    o = jnp.concatenate(outs, axis=1).astype(bf16)
    o_ref[...] = o
    terms = mm(o, wo_ref[...])

    def own_work():
        own_ref[...] = terms

    def rec_work():
        rec_ref[...] = terms.astype(bf16)

    either(own_work, rec_work)


def attend(qkv, kvs, offset, query_ids, key_ids, out_full, heads, dim):
    rows, width, wide = qkv.shape[0], heads * dim, out_full.shape[1]
    keys = sum(kv.shape[0] for kv in kvs)
    n, own_spec, rec_spec, _ = split(rows // 2, min(rows // 2, 512 * 1024 // keys), wide)
    block = rows // (2 * n)
    return pl.pallas_call(
        functools.partial(attend_kernel, heads, dim, offset, len(kvs)),
        grid=(2 * n,),
        in_specs=[
            pl.BlockSpec((block, 1), lambda i: (i, 0)),
            const((1, keys)),
            pl.BlockSpec((block, qkv.shape[1]), lambda i: (i, 0)),
            const(out_full.shape),
        ]
        + [const(kv.shape) for kv in kvs],
        out_specs=[pl.BlockSpec((block, width), lambda i: (i, 0)), own_spec, rec_spec],
        out_shape=[
            shape((rows, width), bf16),
            shape((rows // 2, wide), f32),
            shape((rows // 2, wide), bf16),
        ],
        compiler_params=params(44),
        cost_estimate=cost(10 * rows * keys * width, 16 * rows * width, heads * rows * keys),
    )(query_ids[:, None], key_ids[None, :], qkv, out_full, *kvs)


def attend_back_kernel(heads, dim, offset, count, first, last, *refs):
    qid_ref, kid_ref, q_ref, wo_ref, own_ref, rec_ref = refs[:6]
    kv_refs = refs[6 : 6 + count]
    rest = refs[6 + count :]
    if not first:
        before_ref, rest = rest[0], rest[1:]
    dq_ref, dkv_ref, do_ref, acc_ref = rest
    step = pl.program_id(0)
    scale = dim**-0.5
    factor = scale * math.log2(math.e)
    width = heads * dim

    @pl.when(step == 0)
    def _():
        acc_ref[...] = jnp.zeros_like(acc_ref) if first else before_ref[...]

    def own_work():
        do_ref[...] = mm_last(own_ref[...], wo_ref[...]).astype(bf16)

    def rec_work():
        do_ref[...] = mm_last(rec_ref[...], wo_ref[...]).astype(bf16)

    either(own_work, rec_work)
    same = kid_ref[...] == qid_ref[...]
    dqs = []
    for h in range(heads):
        lo = h * dim
        at = offset + width + lo
        q = q_ref[:, lo : lo + dim]
        do = do_ref[:, lo : lo + dim]
        k = jnp.concatenate([ref[:, offset + lo : offset + lo + dim] for ref in kv_refs])
        v = jnp.concatenate([ref[:, at : at + dim] for ref in kv_refs])
        s = jnp.where(same, mm_last(k, q), NEGATIVE)
        top = jnp.max(s, axis=0, keepdims=True)
        p = jnp.exp2((s - top) * factor)
        p = p * (1.0 / jnp.sum(p, axis=0, keepdims=True))
        dp = mm_last(v, do)
        delta = jnp.sum(p * dp, axis=0, keepdims=True)
        ds = (p * (dp - delta)).astype(bf16)
        acc_ref[heads + h] += mm(p.astype(bf16), do)
        acc_ref[h] += mm(ds, q)
        dqs.append(mm_first(ds, k) * scale)
    dq_ref[...] = jnp.concatenate(dqs, axis=1).astype(bf16)

    @pl.when(step == pl.num_programs(0) - 1)
    def _():
        if last:
            parts = [acc_ref[h] * scale for h in range(heads)]
            parts += [acc_ref[heads + h] for h in range(heads)]
            dkv_ref[...] = jnp.concatenate(parts, axis=1).astype(bf16)
        else:
            dkv_ref[...] = acc_ref[...]


def attend_back(qkv, kvs, offset, query_ids, key_ids, out_full, own, rec, before, last, heads, dim):
    rows, width, wide = qkv.shape[0], heads * dim, out_full.shape[1]
    keys = sum(kv.shape[0] for kv in kvs)
    sums = (2 * heads, keys, dim)
    extra = [] if before is None else [before]
    n, own_spec, rec_spec, _ = split(rows // 2, min(rows // 2, 512 * 1024 // keys), wide)
    block = rows // (2 * n)
    done = shape((keys, 2 * width), bf16) if last else shape(sums, f32)
    return pl.pallas_call(
        functools.partial(attend_back_kernel, heads, dim, offset, len(kvs), before is None, last),
        grid=(2 * n,),
        in_specs=[
            pl.BlockSpec((1, block), lambda i: (0, i)),
            const((keys, 1)),
            pl.BlockSpec((block, qkv.shape[1]), lambda i: (i, 0)),
            const(out_full.shape),
            own_spec,
            rec_spec,
        ]
        + [const(v.shape) for v in list(kvs) + extra],
        out_specs=[pl.BlockSpec((block, width), lambda i: (i, 0)), const(done.shape)],
        out_shape=[shape((rows, width), bf16), done],
        scratch_shapes=[pltpu.VMEM((block, width), bf16), pltpu.VMEM(sums, f32)],
        compiler_params=params(52),
        cost_estimate=cost(24 * rows * keys * width, 30 * rows * width, heads * rows * keys),
    )(query_ids[None, :], key_ids[:, None], qkv, out_full, own, rec, *kvs, *extra)


def join_kernel(dq_ref, dkv_ref, w_ref, dqkv_ref, own_ref, rec_ref, sum_ref):
    @pl.when(pl.program_id(0) == 0)
    def _():
        sum_ref[...] = jnp.zeros_like(sum_ref)

    dqkv = jnp.concatenate([dq_ref[...], dkv_ref[...]], axis=1)
    dqkv_ref[...] = dqkv
    sum_ref[...] += jnp.sum(dqkv.astype(f32), axis=0, keepdims=True)
    terms = mm_last(dqkv, w_ref[:, : dqkv.shape[1]])

    def own_work():
        own_ref[...] = terms

    def rec_work():
        rec_ref[...] = terms.astype(bf16)

    either(own_work, rec_work)


def join(dq, dkv, chunk, weight):
    rows, width, wide = dq.shape[0], dq.shape[1] + dkv.shape[1], weight.shape[0]
    n, own_spec, rec_spec, _ = split(rows // 2, min(rows // 2, 256), wide)
    block, at = rows // (2 * n), 2 * n * chunk
    return pl.pallas_call(
        join_kernel,
        grid=(2 * n,),
        in_specs=[
            pl.BlockSpec((block, dq.shape[1]), lambda i: (i, 0)),
            pl.BlockSpec((block, dkv.shape[1]), lambda i: (at + i, 0)),
            const(weight.shape),
        ],
        out_specs=[pl.BlockSpec((block, width), lambda i: (i, 0)), own_spec, rec_spec, const((1, width))],
        out_shape=[
            shape((rows, width), bf16),
            shape((rows // 2, wide), f32),
            shape((rows // 2, wide), bf16),
            shape((1, width), f32),
        ],
        compiler_params=params(24),
        cost_estimate=cost(2 * rows * width * wide, 4 * wide * (rows + width)),
    )(dq, dkv, weight)


def hidden_kernel(own_ref, rec_ref, up_ref, down_ref, shift_ref, slope_ref, act_ref, po_ref, pr_ref):
    def work(ref, out_ref):
        e = mm(ref[...], up_ref[...]) + shift_ref[...]
        square = e * e
        h = 0.5 * jnp.tanh(e * (square * (ROOT * 0.044715) + ROOT)) + 0.5
        g = e * h
        slope = h + g * (1.0 - h) * (square * (6 * ROOT * 0.044715) + 2 * ROOT)
        g = g.astype(bf16)
        act_ref[...] = g
        slope_ref[...] = slope.astype(bf16)
        out_ref[...] = mm_last(g, down_ref[...]).astype(out_ref.dtype)

    either(lambda: work(own_ref, po_ref), lambda: work(rec_ref, pr_ref))


def tile_of(size):
    return 384 if size % 384 == 0 else 128


def hidden(own, rec, up, down, shift):
    half, wide = own.shape
    ff = up.shape[1]
    n, own_spec, rec_spec, _ = split(half, min(half, 256), wide)
    strip = pl.BlockSpec((half // n, ff), lambda i: (i, 0))
    return pl.pallas_call(
        hidden_kernel,
        grid=(2 * n,),
        in_specs=[own_spec, rec_spec, const(up.shape), const(down.shape), const((1, ff))],
        out_specs=[strip, strip, own_spec, rec_spec],
        out_shape=[
            shape((2 * half, ff), bf16),
            shape((2 * half, ff), bf16),
            shape((half, wide), f32),
            shape((half, wide), bf16),
        ],
        compiler_params=params(30),
        cost_estimate=cost(8 * half * wide * ff, 4 * wide * ff + 20 * half * wide, 2 * half * ff),
    )(own, rec, up, down, shift[None])


def hidden_back_kernel(own_ref, rec_ref, slope_ref, up_ref, down_ref, de_ref, sum_ref, po_ref, pr_ref):
    @pl.when(pl.program_id(0) == 0)
    def _():
        sum_ref[...] = jnp.zeros_like(sum_ref)

    def work(ref, out_ref):
        de = (mm(ref[...], down_ref[...]) * slope_ref[...].astype(f32)).astype(bf16)
        de_ref[...] = de
        sum_ref[...] += jnp.sum(de.astype(f32), axis=0, keepdims=True)
        out_ref[...] = mm_last(de, up_ref[...]).astype(out_ref.dtype)

    either(lambda: work(own_ref, po_ref), lambda: work(rec_ref, pr_ref))


def hidden_back(own, rec, slope, up, down):
    half, wide = own.shape
    ff = up.shape[1]
    n, own_spec, rec_spec, _ = split(half, min(half, 256), wide)
    strip = pl.BlockSpec((half // n, ff), lambda i: (i, 0))
    return pl.pallas_call(
        hidden_back_kernel,
        grid=(2 * n,),
        in_specs=[own_spec, rec_spec, strip, const(up.shape), const(down.shape)],
        out_specs=[strip, const((1, ff)), own_spec, rec_spec],
        out_shape=[
            shape((2 * half, ff), bf16),
            shape((1, ff), f32),
            shape((half, wide), f32),
            shape((half, wide), bf16),
        ],
        compiler_params=params(30),
        cost_estimate=cost(8 * half * wide * ff, 4 * wide * ff + 16 * half * wide),
    )(own, rec, slope, up, down)


def outer_kernel(lefts, rights, beside, bit_ref, *refs):
    left_refs, right_refs = refs[:lefts], refs[lefts : lefts + rights]
    rest = refs[lefts + rights :]
    if beside:
        beside_ref, rest = rest[0], rest[1:]
    mine_ref, theirs_ref = rest
    turned = right_refs[0].shape[0]
    cuts = [ref.shape[0] for ref in left_refs]
    total, at = None, 0
    for ref, size in zip(left_refs, cuts):
        low = at % turned
        right = right_refs[at // turned]
        part = mm_first(ref[...], right[low : low + size, :])
        total = part if total is None else total + part
        at += size
    out = total.astype(bf16)
    if beside:
        out = jnp.concatenate([out, beside_ref[...]], axis=1)
    half = out.shape[0] // 2

    @pl.when(bit_ref[0] == 0)
    def _():
        mine_ref[...], theirs_ref[...] = out[:half], out[half:]

    @pl.when(bit_ref[0] == 1)
    def _():
        mine_ref[...], theirs_ref[...] = out[half:], out[:half]


def outer(lefts, rights, bit, beside=None):
    depth, width = lefts[0].shape[1], rights[0].shape[1]
    rows = sum(v.shape[0] for v in lefts)
    extra = [] if beside is None else [beside]
    out = shape((depth // 2, width + sum(v.shape[1] for v in extra)), bf16)
    return pl.pallas_call(
        functools.partial(outer_kernel, len(lefts), len(rights), len(extra)),
        in_specs=[pl.BlockSpec(memory_space=pltpu.SMEM)]
        + [VMEM] * (len(lefts) + len(rights) + len(extra)),
        out_specs=[VMEM] * 2,
        out_shape=[out] * 2,
        compiler_params=params(30),
        cost_estimate=cost(2 * rows * depth * width, 2 * rows * (depth + width) + 2 * depth * width),
    )(bit, *lefts, *rights, *extra)


def outer_out_kernel(count, o_ref, *refs):
    out_ref = refs[count]
    total, at = None, 0
    for ref in refs[:count]:
        part = mm_first(o_ref[at : at + ref.shape[0], :], ref[...])
        total = part if total is None else total + part
        at += ref.shape[0]
    out_ref[...] = total.astype(bf16)


def outer_out(attended, rights):
    depth, width, rows = attended.shape[1], rights[0].shape[1], attended.shape[0]
    return pl.pallas_call(
        functools.partial(outer_out_kernel, len(rights)),
        in_specs=[VMEM] * (1 + len(rights)),
        out_specs=VMEM,
        out_shape=shape((depth, width), bf16),
        compiler_params=params(24),
        cost_estimate=cost(2 * rows * depth * width, 2 * rows * (depth + width) + 2 * depth * width),
    )(attended, *rights)


def spread(v):
    centred = v - jnp.mean(v, axis=-1, keepdims=True)
    scale = lax.rsqrt(jnp.mean(centred * centred, axis=-1, keepdims=True) + EPSILON)
    return centred * scale, scale


def norm_kernel(rows_of, v_ref, q_ref, come_ref, small_ref, next_ref, u_ref, m_ref):
    shift, gain, offset = rows_of
    u = v_ref[...] + (q_ref[...].astype(f32) + come_ref[...].astype(f32) + small_ref[shift : shift + 1, :])
    u_ref[...] = u
    n = spread(u)[0] * next_ref[gain : gain + 1, :] + next_ref[offset : offset + 1, :]
    m_ref[...] = n.astype(bf16)


def add_norm(v, q, come, small, following, rows_of):
    rows, width = v.shape
    block = pl.BlockSpec((min(rows, 256), width), lambda i: (i, 0))
    return pl.pallas_call(
        functools.partial(norm_kernel, rows_of),
        grid=(rows // min(rows, 256),),
        in_specs=[block] * 3 + [const(small.shape)] * 2,
        out_specs=[block] * 2,
        out_shape=[shape(v.shape, f32), shape(v.shape, bf16)],
        compiler_params=params(16),
        cost_estimate=cost(12 * v.size, 14 * v.size),
    )(v, q, come, small, following)


def norm_back_kernel(gain, v_ref, q_ref, come_ref, grad_ref, small_ref, out_ref, round_ref, sum_ref):
    @pl.when(pl.program_id(0) == 0)
    def _():
        sum_ref[...] = jnp.zeros_like(sum_ref)

    t = q_ref[...].astype(f32) + come_ref[...].astype(f32)
    n, scale = spread(v_ref[...])
    w = t * small_ref[gain : gain + 1, :]
    mean_w = jnp.mean(w, axis=-1, keepdims=True)
    mean_wn = jnp.mean(w * n, axis=-1, keepdims=True)
    out = grad_ref[...] + scale * (w - mean_w - n * mean_wn)
    out_ref[...] = out
    rounded = out.astype(bf16)
    round_ref[...] = rounded
    sum_ref[0:1, :] += jnp.sum(t * n, axis=0, keepdims=True)
    sum_ref[1:2, :] += jnp.sum(t, axis=0, keepdims=True)
    sum_ref[2:3, :] += jnp.sum(rounded.astype(f32), axis=0, keepdims=True)


def norm_back(v, q, come, grad, small, gain):
    rows, width = v.shape
    block = pl.BlockSpec((min(rows, 256), width), lambda i: (i, 0))
    return pl.pallas_call(
        functools.partial(norm_back_kernel, gain),
        grid=(rows // min(rows, 256),),
        in_specs=[block] * 4 + [const(small.shape)],
        out_specs=[block] * 2 + [const((8, width))],
        out_shape=[shape(v.shape, f32), shape(v.shape, bf16), shape((8, width), f32)],
        compiler_params=params(20),
        cost_estimate=cost(24 * v.size, 18 * v.size),
    )(v, q, come, grad, small)


def tie(values):
    return lax.optimization_barrier(values)


def pick(array, index, axis=0):
    return lax.dynamic_index_in_dim(array, index, axis, keepdims=False)


def swap_x(v):
    return lax.ppermute(v, "x", SWAP)


def swap_c(v):
    return lax.ppermute(v, "c", SWAP)


def in_order(axis, own, other):
    first = lax.axis_index(axis) == 0
    return jnp.where(first, own, other), jnp.where(first, other, own)


def exchange(blocks):
    xi, ci = lax.axis_index("x"), lax.axis_index("c")
    blocks = blocks.reshape((2, 2) + blocks.shape[1:])
    both = jnp.stack(in_order("x", pick(blocks, xi), swap_x(pick(blocks, 1 - xi))))
    out = in_order("c", pick(both, ci, 1), swap_c(pick(both, 1 - ci, 1)))
    return jnp.stack(out, axis=1).reshape((RANKS,) + blocks.shape[2:])


def flip(v, axis, step):
    size = lax.axis_size(axis)
    return lax.ppermute(v, axis, [(i, i ^ step) for i in range(size)])


def gather_rows(payload):
    return lax.all_gather(payload, ("hi", "seq"), axis=0, tiled=True)


def halve_rows(mine, theirs):
    step = lax.axis_size("hi") // 2
    place = lax.axis_index("hi")
    terms = (mine.astype(f32) + flip(theirs, "hi", step).astype(f32)).astype(bf16)
    step //= 2
    while step:
        halves = terms.reshape((2, -1) + terms.shape[1:])
        bit = (place // step) % 2
        come = flip(pick(halves, 1 - bit), "hi", step)
        terms = (pick(halves, bit).astype(f32) + come.astype(f32)).astype(bf16)
        step //= 2
    return terms


def scatter_rows(terms):
    return lax.psum_scatter(terms, "seq", scatter_dimension=0, tiled=True)


def sum_everywhere(v):
    for axis in AXES[::-1]:
        step = 1
        while step < lax.axis_size(axis):
            v = v + flip(v, axis, step)
            step *= 2
    return v


def body(
    tokens,
    cotangent,
    image_lengths,
    qkv_weight,
    out_weight,
    up_weight,
    down_weight,
    up_bias,
    norm_scale,
    shifts,
):
    rows, width = tokens.shape
    layers, held = qkv_weight.shape[0], qkv_weight.shape[1]
    blocks, seqs = lax.axis_size("hi"), lax.axis_size("seq")
    ways = seqs // RANKS
    shards = blocks * seqs
    chunk = seqs * held
    heads = HEADS // RANKS
    dim = width // HEADS
    part = width // RANKS
    ff = up_weight.shape[2]
    ff_part = ff // RANKS
    ff_pad = -(-ff_part // 128) * 128
    xi, ci = lax.axis_index("x"), lax.axis_index("c")
    rank = 2 * xi + ci

    spot = jnp.arange(width, dtype=jnp.int32)
    natural = ((spot // (RANKS * held * seqs) * RANKS + spot // held % RANKS) * seqs) * held
    natural = natural + spot // (RANKS * held) % seqs * held + spot % held
    turn_matrix = (spot[:, None] == natural[None, :]).astype(bf16)

    def mixed_order(v):
        return mm(v, turn_matrix).astype(bf16)

    def plain_order(v):
        return mm_last(v, turn_matrix)

    def mine(v):
        return pick(v.reshape(blocks, seqs, RANKS, held), rank, 2).reshape(part)

    def placed(v):
        v = v.reshape(blocks, seqs, 1, held)
        spots = (jnp.arange(RANKS) == rank)[None, None, :, None]
        return jnp.where(spots, v, 0.0).reshape(width)

    there = []
    for b in range(blocks):
        for r in range(RANKS):
            for s in range(seqs):
                target = (b * RANKS + s % RANKS) * seqs + r * ways + s // RANKS
                there.append(((b * RANKS + r) * seqs + s, target))
    back = [(target, source) for source, target in there]

    def rank_columns(piece):
        piece = piece.reshape(held, 3, blocks, RANKS, chunk)
        return piece.transpose(3, 0, 1, 2, 4).reshape(RANKS, held, 3 * part)

    def ff_columns(piece):
        piece = piece.reshape(held, RANKS, ff_part).transpose(1, 0, 2)
        return jnp.pad(piece, ((0, 0), (0, 0), (0, ff_pad - ff_part)))

    def out_rows(l):
        return mixed_order(out_weight[l]).reshape(held * RANKS, part)

    kinds = norm_scale.shape[2] + shifts.shape[2]
    smalls = jnp.concatenate([norm_scale, shifts], axis=2)
    smalls = smalls.transpose(1, 0, 2).reshape(1, held, layers * kinds)
    smalls = jnp.broadcast_to(smalls, (RANKS, held, layers * kinds))

    qkv_fulls, out_fulls, up_fulls, down_fulls = [], [], [], []
    came = exchange(jnp.concatenate([rank_columns(qkv_weight[0]), smalls], axis=2))
    came = came.reshape(RANKS * held, -1)
    payload = jnp.concatenate([came[:, : 3 * part], out_rows(0), came[:, 3 * part :]], axis=1)
    first = gather_rows(payload)
    small_full = first[:, width:].T.reshape(layers, kinds, width).astype(f32)
    qkv_fulls.append(first)
    out_fulls.append(first[:, 3 * part : width].reshape(part, width))
    later = [
        ff_columns(piece) for l in range(layers) for piece in (up_weight[l], down_weight[l])
    ] + [rank_columns(qkv_weight[l]) for l in range(1, layers)]
    arrived = lax.ppermute(tokens, AXES, there)
    later, arrived, _ = tie((jnp.concatenate(later, axis=2), arrived, payload))
    later = exchange(later).reshape(RANKS * held, -1)
    for l in range(layers):
        if l > 0:
            at = 2 * layers * ff_pad + (l - 1) * 3 * part
            payload = jnp.concatenate([later[:, at : at + 3 * part], out_rows(l)], axis=1)
            full = gather_rows(payload)
            qkv_fulls.append(full)
            out_fulls.append(full[:, 3 * part :].reshape(part, width))
        at = 2 * l * ff_pad
        full = gather_rows(later[:, at : at + 2 * ff_pad])
        up_fulls.append(full[:, :ff_pad])
        down_fulls.append(full[:, ff_pad:])
    up_shift = pick(up_bias.reshape(layers, RANKS, ff_part), rank, 1).astype(f32)
    up_shift = jnp.pad(up_shift, ((0, 0), (0, ff_pad - ff_part)))

    xs = [(0, 1)] if CHUNKS == 1 else [(0,), (1,)]
    span = 4 * rows // CHUNKS
    lengths = lax.ppermute(image_lengths, AXES, there)
    finish = jnp.cumsum(lengths[0])
    base = jnp.arange(rows, dtype=jnp.int32)
    local = [
        jnp.concatenate([base + (2 * x + c) * rows for c in (ci, 1 - ci) for x in chunk_xs])
        for chunk_xs in xs
    ]
    group = RANKS * rows
    turn = lax.axis_index("seq") % ways

    def ids_of(pos):
        return jnp.sum((pos[:, None] >= finish[None, :]).astype(jnp.int32), axis=1)

    query_ids = [ids_of(v + turn * group) for v in local]
    key_ids = ids_of(jnp.concatenate([v + w * group for v in local for w in range(ways)]))
    seq_groups = [[j * ways + w for w in range(ways)] for j in range(seqs // ways)]

    def keys_of(qkv):
        if ways == 1:
            return qkv, part
        kv = lax.all_gather(
            qkv[:, part:], "seq", axis=0, tiled=True, axis_index_groups=seq_groups
        )
        return kv, 0

    def chunks_of(v):
        own = mixed_order(v)
        pair = in_order("x", own, swap_x(own))
        return list(pair) if CHUNKS == 2 else [jnp.concatenate(pair)]

    def at_x(chunks, index):
        if CHUNKS == 2:
            return jnp.where(index == 0, chunks[0], chunks[1])
        return pick(chunks[0].reshape((2, rows) + chunks[0].shape[1:]), index)

    def core_sum(own, other):
        return (own + swap_c(other).astype(f32)).astype(bf16)

    def last_sum(qs):
        return at_x(qs, xi), swap_x(at_x(qs, 1 - xi))

    def to_rows(v):
        return plain_order(lax.ppermute(v.astype(bf16), AXES, back))

    GAIN1, GAIN2, OFF1, QB, VB, OB, OFF2, DB = range(8)
    starts = chunks_of(arrived)
    current = [v.astype(f32) for v in starts]
    normed = [
        (spread(v)[0] * small_full[0, GAIN1] + small_full[0, OFF1]).astype(bf16) for v in current
    ]
    saved = []
    output = None
    for l in range(layers):
        small = small_full[l]
        attn_in = [(v, swap_c(v)) for v in normed]
        shift = jnp.concatenate([mine(small[QB]), jnp.zeros((part,), f32), mine(small[VB])])
        qkv = [project(own, rec, qkv_fulls[l], shift) for own, rec in attn_in]
        kvs = [keys_of(v) for v in qkv]
        offset, kvs = kvs[0][1], [v[0] for v in kvs]
        attended, after, normed = [], [], []
        for j in range(CHUNKS):
            o, own, other = attend(
                qkv[j], kvs, offset, query_ids[j], key_ids, out_fulls[l], heads, dim
            )
            attended.append(o)
            q = core_sum(own, other)
            if l == layers - 1 and j == 0:
                q, cotangent = tie((q, cotangent))
                arrived = lax.ppermute(cotangent, AXES, there)
            come = swap_x(q)
            if l == layers - 1 and j == 0:
                come, arrived = tie((come, arrived))
            u, m = add_norm(current[j], q, come, small, small, (OB, GAIN2, OFF2))
            after.append(u)
            normed.append(m)
        mlp_in = [(v, swap_c(v)) for v in normed]
        if l == layers - 1:
            mlp_in, rounded = tie((mlp_in, chunks_of(arrived)))
        slopes, acts, qs, following, normed = [], [], [], [], []
        for j in range(CHUNKS):
            slope, act, own, other = hidden(*mlp_in[j], up_fulls[l], down_fulls[l], up_shift[l])
            slopes.append(slope)
            acts.append(act)
            q = core_sum(own, other)
            qs.append(q)
            if l < layers - 1:
                u, m = add_norm(
                    after[j], q, swap_x(q), small, small_full[l + 1], (DB, GAIN1, OFF1)
                )
                following.append(u)
                normed.append(m)
        saved.append((current, attn_in, qkv, kvs, attended, after, mlp_in, slopes, acts))
        current = following
        if l == layers - 1:
            q, come = last_sum(qs)
            final = at_x(after, xi) + (q.astype(f32) + come.astype(f32) + small[DB])
            output = to_rows(final)

    grads = [None] * layers
    vectors = [None] * layers
    biases = [None] * layers
    grad = [v.astype(f32) for v in rounded]
    d_sum = 0.5 * sum(jnp.sum(v, axis=0) for v in grad)
    tokens_grad = None
    top_bit = (lax.axis_index("hi") // (blocks // 2)).astype(jnp.int32)[None]

    waiting = None
    for l in reversed(range(layers)):
        (current, attn_in, qkv, kvs, attended, after, mlp_in, slopes, acts) = saved[l]
        small = small_full[l]
        down_in = [(v, swap_c(v)) for v in rounded]
        des, qs, bias = [], [], 0.0
        for j in range(CHUNKS):
            de, sums, own, other = hidden_back(*down_in[j], slopes[j], up_fulls[l], down_fulls[l])
            des.append(de)
            bias = bias + sums[0]
            qs.append(core_sum(own, other))
        biases[l] = bias
        qs, des, down_in = tie((qs, des, down_in))
        comes = [swap_x(q) for q in qs]
        down_terms = outer([v for pair in down_in for v in pair], acts, top_bit)
        up_terms = outer([v for pair in mlp_in for v in pair], des, top_bit)
        if waiting is None:
            comes, down_terms, up_terms = tie((comes, down_terms, up_terms))
        else:
            waiting = halve_rows(*waiting)
            comes, down_terms, up_terms, waiting = tie((comes, down_terms, up_terms, waiting))
            grads[l + 1][2] = scatter_rows(waiting)
        rounded, mid, sums = [], [], 0.0
        for j in range(CHUNKS):
            g, r, s = norm_back(after[j], qs[j], comes[j], grad[j], small, GAIN2)
            mid.append(g)
            rounded.append(r)
            sums = sums + 0.5 * s
        gain_two_sum, off_two_sum, o_sum = sums[0], sums[1], sums[2]
        out_in = [(v, swap_c(v)) for v in rounded]
        acc, dqs = None, []
        for j in range(CHUNKS):
            dq, acc = attend_back(
                qkv[j], kvs, 0 if ways > 1 else part, query_ids[j], key_ids, out_fulls[l],
                *out_in[j], acc, j == CHUNKS - 1, heads, dim,
            )
            dqs.append(dq)
        if ways > 1:
            acc = acc.reshape(CHUNKS, ways, span, 2 * part).swapaxes(0, 1)
            acc = lax.psum_scatter(
                acc.reshape(ways * CHUNKS * span, 2 * part),
                "seq",
                scatter_dimension=0,
                tiled=True,
                axis_index_groups=seq_groups,
            )
        dqkvs, qs, columns = [], [], 0.0
        for j in range(CHUNKS):
            dqkv, own, other, s = join(dqs[j], acc, j, qkv_fulls[l])
            dqkvs.append(dqkv)
            columns = columns + s[0]
            qs.append(core_sum(own, other))
        down_terms = halve_rows(*down_terms)
        qs, dqkvs, out_in, down_terms = tie((qs, dqkvs, out_in, down_terms))
        down_owned = scatter_rows(down_terms)
        if l > 0:
            comes = [swap_x(q) for q in qs]
        else:
            q, comes = last_sum(qs)
        out_terms = outer_out(
            jnp.concatenate(attended) if CHUNKS > 1 else attended[0],
            [v for pair in out_in for v in pair],
        ).reshape(width, part)
        waiting = outer([v for pair in attn_in for v in pair], dqkvs, top_bit, out_terms)
        up_terms = halve_rows(*up_terms)
        comes, waiting, up_terms = tie((comes, waiting, up_terms))
        up_owned = scatter_rows(up_terms)
        d_next = None
        if l > 0:
            grad, rounded, sums = [], [], 0.0
            for j in range(CHUNKS):
                g, r, s = norm_back(current[j], qs[j], comes[j], mid[j], small, GAIN1)
                grad.append(g)
                rounded.append(r)
                sums = sums + 0.5 * s
            d_next = sums[2]
        else:
            g, r, sums = norm_back(at_x(current, xi), q, comes, at_x(mid, xi), small, GAIN1)
            tokens_grad = to_rows(r)
        vectors[l] = jnp.stack(
            [
                sums[0],
                gain_two_sum,
                sums[1],
                placed(columns[:part]),
                placed(columns[2 * part :]),
                o_sum,
                off_two_sum,
                d_sum,
            ]
        )
        d_sum = d_next
        grads[l] = [up_owned, down_owned, None]

    waiting = halve_rows(*waiting)
    early = [v for l in range(layers) for v in grads[l][: 2 if l == 0 else 3]]
    early, waiting = tie((early, waiting))
    grads[0][2] = scatter_rows(waiting)
    for l in range(1, layers):
        grads[l][2] = early[3 * l + 1]
    early = [v[:, : 3 * part] if i > 2 and i % 3 == 1 else v for i, v in enumerate(early)]
    widths = [v.shape[1] for v in early]
    early = exchange(jnp.concatenate(early, axis=1).reshape(RANKS, held, -1))
    homes = iter(
        lax.slice_in_dim(early, sum(widths[:i]), sum(widths[: i + 1]), axis=2)
        for i in range(len(widths))
    )
    results = [[None] * layers for _ in range(4)]
    for l in range(layers):
        owned = grads[l][2]
        results[1][l] = plain_order(owned[:, 3 * part :].reshape(held, width))
        for i in (2, 3):
            results[i][l] = next(homes)[:, :, :ff_part].transpose(1, 0, 2).reshape(held, ff)
        owned = owned[:, : 3 * part].reshape(RANKS, held, 3 * part)
        qkv_grad = exchange(owned) if l == 0 else next(homes)
        qkv_grad = qkv_grad.reshape(RANKS, held, 3, blocks, chunk).transpose(1, 2, 3, 0, 4)
        results[0][l] = qkv_grad.reshape(held, 3 * width)
    results = [jnp.stack(v).astype(f32) for v in results]

    spots = (jnp.arange(RANKS) == rank)[None, :, None]
    bias = jnp.where(spots, jnp.stack(biases)[:, None, :], 0.0).reshape(layers * RANKS, ff_pad)
    wide = max(ff_pad, width)
    both = jnp.concatenate(
        [
            jnp.pad(jnp.concatenate(vectors), ((0, 0), (0, wide - width))),
            jnp.pad(bias, ((0, 0), (0, wide - ff_pad))),
        ]
    )
    both = sum_everywhere(both)
    vector = both[: layers * kinds, :width].reshape(layers, kinds, blocks, seqs, RANKS, held)
    for axis, index in ((2, "hi"), (2, "seq")):
        vector = pick(vector, lax.axis_index(index), axis)
    vector = pick(vector, rank, 2).swapaxes(1, 2)
    bias = both[layers * kinds :, :ff_part].reshape(layers, ff)
    return (
        output,
        tokens_grad,
        *results,
        bias,
        vector[:, :, :2],
        vector[:, :, 2:],
    )


def solution(mesh):
    sizes = mesh.shape
    devices = mesh.devices.reshape(sizes["img"] // RANKS, 2, 2, sizes["seq"])
    fine = Mesh(devices, AXES)
    row = P(AXES, None)
    param = P(None, AXES, None)
    in_specs = (row, row, P(AXES[:3], None), param, param, param, param, P(), param, param)
    out_specs = (row, row, param, param, param, param, P(), param, param)
    return jax.shard_map(
        body, mesh=fine, in_specs=in_specs, out_specs=out_specs, check_vma=False
    )
```

time: 1000 us -> 860 us (0.86)
  Pallas kernels: 64.3 us -> 193 us
  matrix products: 138 us -> 13 us
  other arithmetic: 124 us -> 68.7 us
  local copies, waits for them, and re-layouts: 197 us -> 145 us
  starting transfers between devices: 135 us -> 101 us
    pallas_call x4 -> x27, Pallas kernels: 64.3 us -> 193 us  [the longest x2 46.6 us: attend_back(): pl.pallas_call(functools.partial(attend_back_kernel, heads, dim, offset,...]
    dot_general x32 -> x8, matrix products: 138 us -> 13 us  [the longest x4 7.57 us: mm_last(): return lax.dot_general(left, right, dims, preferred_element_type=f32)]
    unnamed x8 -> x10, waiting for transfers between devices: 96.8 us -> 0.17 us
    convert_element_type x34 -> x0, local copies, waits for them, and re-layouts: 37.7 us -> none  [the longest x2 8.3 us: dot_rows(): lax.dot_general(left, right, dims, preferred_element_type=f32).astype(kind)]
    ppermute x17 -> x15, waiting for transfers between devices: 89.9 us -> 127 us  [the longest x11 101 us: flip(): return lax.ppermute(v, axis, [(i, i ^ step) for i in range(size)])]
    reduce_sum x21 -> x3, other arithmetic: 34.3 us -> 0.88 us  [the longest x1 0.45 us: spread(): jnp.mean(centred * centred, axis=-1, keepdims=True) + EPSILON]
    unnamed x236 -> x290, local copies, waits for them, and re-layouts: 32 us -> 65 us
    reduce_scatter x2 -> x6, waiting for transfers between devices: 19.4 us -> 47.8 us  [scatter_rows(): return lax.psum_scatter(terms, 'seq', scatter_dimension=0, tiled=True)]
  transfers between devices with their start and end apart: 67 -> 60, of which waited for: 27 -> 32; matrix products, arithmetic and copies ran while one was open for 43% -> 20% of each run, Pallas kernels for 6% -> 21%
where the time goes in v2:
time: 860 us; the launch traced here: 848 us
  waiting for transfers between devices  310 us (36%)
  Pallas kernels  193 us (22%)
  local copies, waits for them, and re-layouts  145 us (17%)
  starting transfers between devices  101 us (12%)
  other arithmetic  68.7 us (8%)
  between operations  16.5 us (2%)
  matrix products  13 us (2%)
    ppermute x11, waiting for transfers between devices, flip(): return lax.ppermute(v, axis, [(i, i ^ step) for i in range(size)])  101 us
    ppermute x14, waiting for transfers between devices, swap_x(): return lax.ppermute(v, 'x', SWAP)  99.6 us
    unnamed x290, local copies, waits for them, and re-layouts  65 us
    ppermute x20, starting transfers between devices, swap_c(): return lax.ppermute(v, 'c', SWAP)  53.2 us
    reduce_scatter x6, waiting for transfers between devices, scatter_rows(): return lax.psum_scatter(terms, 'seq', scatter_dimension=0, tiled=True)  47.8 us
    pallas_call x2, Pallas kernels, attend_back(): pl.pallas_call(functools.partial(attend_back_kernel, heads, dim, offset,...  46.6 us
    pallas_call x2, Pallas kernels, attend(): pl.pallas_call(functools.partial(attend_kernel, heads, dim, offset, len(k...  33.9 us
    pallas_call x6, Pallas kernels, outer(): pl.pallas_call(functools.partial(outer_kernel, len(lefts), len(rights), l...  30.5 us
  transfers between devices with their start and end apart: 60, of which 32 were waited for; matrix products, arithmetic and copies ran while one was open for 20% of the time, Pallas kernels for 21%

profile of v2, /device:TPU:1, one launch (start us, length us, event | category | flops | bytes accessed | tf_op | source)
XLA Modules:
  0.0 847.8 jit_solution(16183040257742263732)
XLA Ops:
  41.8 18.6 %collective-permute-done.9 = bf16[2,36,5472]{2,0,1:T(2,128)(2,1)S(1)} collective-permute-done((bf16[2,36,5472]{2,0,1:T(2,128)(2,1)S(1)}, bf16[2,36,5472]{2,0,1:T(2,128)(2,1)S(1)}, u32[]{:S(2)}, u32[]{:S(2)}) %collective-permute-start.9) | collective-permute-done | bytes 788000 | tf_op jit(solution)/shard_map/ppermute | solution.py:490
  80.3 13.4 %collective-permute-done.3 = bf16[256,1152]{1,0:T(8,128)(2,1)S(1)} collective-permute-done((bf16[256,1152]{1,0:T(8,128)(2,1)S(1)}, bf16[256,1152]{1,0:T(8,128)(2,1)S(1)}, u32[]{:S(2)}, u32[]{:S(2)}) %collective-permute-start.3) | collective-permute-done | bytes 589856 | tf_op jit(solution)/shard_map/ppermute | solution.py:490
  126.3 17.2 %shard_map.170 = (bf16[1024,288]{1,0:T(8,128)(2,1)S(1)}, f32[512,1152]{1,0:T(8,128)S(1)}, bf16[512,1152]{1,0:T(8,128)(2,1)}) custom-call(s32[1024,1]{1,0:T(8,128)S(1)} %copy.186.refs_0_, s32[1,1024]{1,0:T(1,128)S(1)} %bitcast.185, bf16[1024,864]{1,0:T(8,128)(2,1)S(1)} %shard_map.169.refs_2_.refs_4_.refs_6_, bf16[288,1152]{1,0:T(8,128)(2,1)S(1)} %copy-done.16, ...), custom_call_target="tpu_custom_call" | custom-call | flops 301989888 | bytes 471859 | tf_op jit(solution)/shard_map/pallas_call | solution.py:132
  156.5 23.9 %collective-permute-done.7.come_ref = bf16[512,1152]{1,0:T(8,128)(2,1)} collective-permute-done((bf16[512,1152]{1,0:T(8,128)(2,1)S(1)}, bf16[512,1152]{1,0:T(8,128)(2,1)}, u32[]{:S(2)}, u32[]{:S(2)}) %collective-permute-start.7) | collective-permute-done | bytes 1179680 | tf_op jit(solution)/shard_map/ppermute | solution.py:490
  192.7 10.0 %shard_map.172 = (bf16[1024,1152]{1,0:T(8,128)(2,1)S(1)}, bf16[1024,1152]{1,0:T(8,128)(2,1)S(1)}, f32[512,1152]{1,0:T(8,128)S(1)}, bf16[512,1152]{1,0:T(8,128)(2,1)S(1)}) custom-call(bf16[512,1152]{1,0:T(8,128)(2,1)S(1)} %get-tuple-element.128.own_ref.refs_0_, bf16[512,1152]{1,0:T(8,128)(2,1)} %collective-permute-done.8.rec_ref.refs_1_, ...), custom_call_target="tpu_custom_call" | custom-call | flops 543581824 | bytes 1710489 | tf_op jit(solution)/shard_map/pallas_call | solution.py:302
  208.3 26.1 %collective-permute-done.12.come_ref = bf16[512,1152]{1,0:T(8,128)(2,1)S(1)} collective-permute-done((bf16[512,1152]{1,0:T(8,128)(2,1)S(1)}, bf16[512,1152]{1,0:T(8,128)(2,1)S(1)}, u32[]{:S(2)}, u32[]{:S(2)}) %collective-permute-start.12) | collective-permute-done | bytes 1179680 | tf_op jit(solution)/shard_map/ppermute | solution.py:490
  238.8 6.3 all-gather.9.cloned.1.call-done.w_ref
  256.9 16.6 %shard_map.175 = (bf16[1024,288]{1,0:T(8,128)(2,1)S(1)}, f32[512,1152]{1,0:T(8,128)S(1)}, bf16[512,1152]{1,0:T(8,128)(2,1)S(1)}) custom-call(s32[1024,1]{1,0:T(8,128)S(1)} %copy-done.41, s32[1,1024]{1,0:T(1,128)S(1)} %bitcast.186, bf16[1024,864]{1,0:T(8,128)(2,1)S(1)} %shard_map.174.refs_2_.refs_4_.refs_6_, bf16[288,1152]{1,0:T(8,128)(2,1)S(1)} %reshape.393.refs_3_, ...), custom_call_target="tpu_custom_call" | custom-call | flops 301989888 | bytes 471859 | tf_op jit(solution)/shard_map/pallas_call | solution.py:132
  283.3 24.2 %collective-permute-done.16 = bf16[256,1152]{1,0:T(8,128)(2,1)S(1)} collective-permute-done((bf16[256,1152]{1,0:T(8,128)(2,1)S(1)}, bf16[256,1152]{1,0:T(8,128)(2,1)S(1)}, u32[]{:S(2)}, u32[]{:S(2)}) %collective-permute-start.16) | collective-permute-done | bytes 589856 | tf_op jit(solution)/shard_map/ppermute | solution.py:714
  317.8 31.6 %collective-permute-start.17 = (bf16[512,1152]{1,0:T(8,128)(2,1)S(1)}, bf16[512,1152]{1,0:T(8,128)(2,1)S(1)}, u32[]{:S(2)}, u32[]{:S(2)}) collective-permute-start(bf16[512,1152]{1,0:T(8,128)(2,1)S(1)} %get-tuple-element.142.own_ref.refs_0_), channel_id=1, source_target_pairs={{0,4},{4,0},{1,5},{5,1},{2,6},{6,2},{3,7},{7,3},{8,12},{12,8},{9,1... | collective-permute-start | bytes 3538952 | tf_op jit(solution)/shard_map/ppermute | solution.py:494
  360.4 9.3 %shard_map.177 = (bf16[1024,1152]{1,0:T(8,128)(2,1)S(1)}, bf16[1024,1152]{1,0:T(8,128)(2,1)S(1)}, f32[512,1152]{1,0:T(8,128)S(1)}, bf16[512,1152]{1,0:T(8,128)(2,1)}) custom-call(bf16[512,1152]{1,0:T(8,128)(2,1)S(1)} %copy-done.30, bf16[512,1152]{1,0:T(8,128)(2,1)S(1)} %copy-done.33, bf16[1152,1152]{1,0:T(8,128)(2,1)S(1)} %get-tuple-element.315.up_ref, ...), custom_call_target="tpu_custom_call" | custom-call | flops 543581824 | bytes 1710489 | tf_op jit(solution)/shard_map/pallas_call | solution.py:302
  372.5 8.8 %shard_map.178 = (bf16[1024,1152]{1,0:T(8,128)(2,1)S(1)}, f32[1,1152]{1,0:T(1,128)S(1)}, f32[512,1152]{1,0:T(8,128)S(1)}, bf16[512,1152]{1,0:T(8,128)(2,1)S(1)}) custom-call(bf16[512,1152]{1,0:T(8,128)(2,1)S(1)} %pad_maximum_fusion.3.own_ref.refs_0_, bf16[512,1152]{1,0:T(8,128)(2,1)} %collective-permute-done.22.rec_ref.refs_1_, ...), custom_call_target="tpu_custom_call" | custom-call | flops 543581824 | bytes 1474560 | tf_op jit(solution)/shard_map/pallas_call | solution.py:337
  396.2 6.0 shard_map.179
  402.3 11.5 %collective-permute-done.24.come_ref = bf16[512,1152]{1,0:T(8,128)(2,1)} collective-permute-done((bf16[512,1152]{1,0:T(8,128)(2,1)}, bf16[512,1152]{1,0:T(8,128)(2,1)}, u32[]{:S(2)}, u32[]{:S(2)}) %collective-permute-start.24) | collective-permute-done | bytes 1179680 | tf_op jit(solution)/shard_map/ppermute | solution.py:490
  426.1 23.3 %shard_map.182 = (bf16[1024,288]{1,0:T(8,128)(2,1)S(1)}, bf16[1024,576]{1,0:T(8,128)(2,1)}) custom-call(s32[1,1024]{1,0:T(1,128)S(1)} %bitcast.183, s32[1024,1]{1,0:T(8,128)S(1)} %copy-done.38, bf16[1024,864]{1,0:T(8,128)(2,1)} %copy-done.1, bf16[288,1152]{1,0:T(8,128)(2,1)S(1)} %copy-done.19, bf16[512,1152]{1,0:T(8,128)(2,1)} %get-tuple-element.172.refs_4_.refs_0_, ...), custom_call_target="tpu_custom_call" | custom-call | flops 724775744 | bytes 884736 | tf_op jit(solution)/shard_map/pallas_call | solution.py:215
  466.2 23.3 %collective-permute-done.29 = bf16[576,1152]{1,0:T(8,128)(2,1)} collective-permute-done((bf16[576,1152]{1,0:T(8,128)(2,1)}, bf16[576,1152]{1,0:T(8,128)(2,1)}, u32[]{:S(2)}, u32[]{:S(2)}) %collective-permute-start.29) | collective-permute-done | bytes 1327136 | tf_op jit(solution)/shard_map/ppermute | solution.py:512
  502.7 5.8 shard_map.185
  520.4 8.5 %shard_map.187 = (bf16[1024,1152]{1,0:T(8,128)(2,1)S(1)}, f32[1,1152]{1,0:T(1,128)S(1)}, f32[512,1152]{1,0:T(8,128)S(1)}, bf16[512,1152]{1,0:T(8,128)(2,1)}) custom-call(bf16[512,1152]{1,0:T(8,128)(2,1)S(1)} %get-tuple-element.186.own_ref.refs_0_, bf16[512,1152]{1,0:T(8,128)(2,1)S(1)} %collective-permute-done.30.rec_ref.refs_1_, ...), custom_call_target="tpu_custom_call" | custom-call | flops 543581824 | bytes 1474560 | tf_op jit(solution)/shard_map/pallas_call | solution.py:337
  540.2 23.3 %collective-permute-done.33 = bf16[576,1152]{1,0:T(8,128)(2,1)} collective-permute-done((bf16[576,1152]{1,0:T(8,128)(2,1)}, bf16[576,1152]{1,0:T(8,128)(2,1)}, u32[]{:S(2)}, u32[]{:S(2)}) %collective-permute-start.33) | collective-permute-done | bytes 1327136 | tf_op jit(solution)/shard_map/ppermute | solution.py:512
  594.5 23.4 %shard_map.191 = (bf16[1024,288]{1,0:T(8,128)(2,1)S(1)}, bf16[1024,576]{1,0:T(8,128)(2,1)}) custom-call(s32[1,1024]{1,0:T(1,128)S(1)} %bitcast.184, s32[1024,1]{1,0:T(8,128)S(1)} %copy-done.39, bf16[1024,864]{1,0:T(8,128)(2,1)} %copy-done, bf16[288,1152]{1,0:T(8,128)(2,1)S(1)} %copy-done.17, bf16[512,1152]{1,0:T(8,128)(2,1)} %get-tuple-element.209.refs_4_.refs_0_, ...), custom_call_target="tpu_custom_call" | custom-call | flops 724775744 | bytes 884736 | tf_op jit(solution)/shard_map/pallas_call | solution.py:215
  642.0 25.4 %collective-permute-done.38 = bf16[576,1152]{1,0:T(8,128)(2,1)} collective-permute-done((bf16[576,1152]{1,0:T(8,128)(2,1)}, bf16[576,1152]{1,0:T(8,128)(2,1)}, u32[]{:S(2)}, u32[]{:S(2)}) %collective-permute-start.38) | collective-permute-done | bytes 1327136 | tf_op jit(solution)/shard_map/ppermute | solution.py:512
  691.7 19.7 %collective-permute-done.40 = bf16[576,1152]{1,0:T(8,128)(2,1)} collective-permute-done((bf16[576,1152]{1,0:T(8,128)(2,1)}, bf16[576,1152]{1,0:T(8,128)(2,1)}, u32[]{:S(2)}, u32[]{:S(2)}) %collective-permute-start.40) | collective-permute-done | bytes 1327136 | tf_op jit(solution)/shard_map/ppermute | solution.py:512
  728.5 5.5 collective-permute-done.46
  784.9 43.4 %reduce-scatter.17.cloned.1.call-done = bf16[144,1152]{1,0:T(8,128)(2,1)} async-done(((bf16[576,1152]{1,0:T(8,128)(2,1)}), bf16[144,1152]{1,0:T(8,128)(2,1)}) %reduce-scatter.17.cloned.1.call-update) | async-done | bytes 331792 | tf_op jit(solution)/shard_map/reduce_scatter | solution.py:534
  (626 shorter events, 406.3 us)
Async XLA Ops:
  7.2 93.8 %all-gather.5.cloned.1.call-start = ((), (), s32[]{:S(2)}) async-start(), calls=%async_computation.6 | async-start | bytes 3317760 | tf_op jit(solution)/shard_map/all_gather | solution.py:516
  7.2 32.7 %collective-permute-start = (bf16[256,1152]{1,0:T(8,128)(2,1)}, bf16[256,1152]{1,0:T(8,128)(2,1)}, u32[]{:S(2)}, u32[]{:S(2)}) collective-permute-start(bf16[256,1152]{1,0:T(8,128)(2,1)} %param.10), channel_id=1, source_target_pairs={{0,0},{1,4},{2,8},{3,12},{4,1},{5,5},{6,9},{7,13},{8,2},{9,6},{10,... | collective-permute-start | bytes 1769480 | tf_op jit(solution)/shard_map/ppermute | solution.py:627
  41.8 147.9 %all-gather.7.cloned.1.call-start = ((), (), s32[]{:S(2)}) async-start(), calls=%async_computation.7 | async-start | bytes 5971968 | tf_op jit(solution)/shard_map/all_gather | solution.py:516
  76.7 168.4 %all-gather.9.cloned.1.call-start = ((), (), s32[]{:S(2)}) async-start(), calls=%async_computation.8 | async-start | bytes 2985984 | tf_op jit(solution)/shard_map/all_gather | solution.py:516
  95.9 261.3 %all-gather.11.cloned.1.call-start = ((), (), s32[]{:S(2)}) async-start(), calls=%async_computation.9 | async-start | bytes 5971968 | tf_op jit(solution)/shard_map/all_gather | solution.py:516
  154.9 559.7 %reduce-scatter.13.cloned.1.call-start = ((), (), s32[]{:S(2)}) async-start(), calls=%async_computation.13 | async-start | bytes 1658880 | tf_op jit(solution)/shard_map/reduce_scatter | solution.py:534
  278.3 34.4 %collective-permute-start.15 = (bf16[512,1152]{1,0:T(8,128)(2,1)S(1)}, bf16[512,1152]{1,0:T(8,128)(2,1)S(1)}, u32[]{:S(2)}, u32[]{:S(2)}) collective-permute-start(bf16[512,1152]{1,0:T(8,128)(2,1)S(1)} %add_convert_fusion.11.q_ref), channel_id=1, source_target_pairs={{0,8},{8,0},{1,9},{9,1},{2,10},{10,2},{3,11},{11,3},{4,12},{12,4},... | collective-permute-start | bytes 3538952 | tf_op jit(solution)/shard_map/ppermute | solution.py:490
  313.9 35.5 %collective-permute-start.18 = (bf16[256,1152]{1,0:T(8,128)(2,1)S(1)}, bf16[256,1152]{1,0:T(8,128)(2,1)S(1)}, u32[]{:S(2)}, u32[]{:S(2)}) collective-permute-start(bf16[256,1152]{1,0:T(8,128)(2,1)S(1)} %fusion.17), channel_id=1, source_target_pairs={{0,8},{8,0},{1,9},{9,1},{2,10},{10,2},{3,11},{11,3},{4,12},{12,4},... | collective-permute-start | bytes 1769480 | tf_op jit(solution)/shard_map/ppermute | solution.py:490
  317.8 34.1 %collective-permute-start.17 = (bf16[512,1152]{1,0:T(8,128)(2,1)S(1)}, bf16[512,1152]{1,0:T(8,128)(2,1)S(1)}, u32[]{:S(2)}, u32[]{:S(2)}) collective-permute-start(bf16[512,1152]{1,0:T(8,128)(2,1)S(1)} %get-tuple-element.142.own_ref.refs_0_), channel_id=1, source_target_pairs={{0,4},{4,0},{1,5},{5,1},{2,6},{6,2},{3,7},{7,3},{8,12},{12,8},{9,1... | collective-permute-start | bytes 3538952 | tf_op jit(solution)/shard_map/ppermute | solution.py:494
  421.1 37.7 %collective-permute-start.27 = (bf16[576,1152]{1,0:T(8,128)(2,1)}, bf16[576,1152]{1,0:T(8,128)(2,1)}, u32[]{:S(2)}, u32[]{:S(2)}) collective-permute-start(bf16[576,1152]{1,0:T(8,128)(2,1)} %get-tuple-element.168), channel_id=1, source_target_pairs={{0,16},{16,0},{1,17},{17,1},{2,18},{18,2},{3,19},{19,3},{4,20},{20... | collective-permute-start | bytes 3981320 | tf_op jit(solution)/shard_map/ppermute | solution.py:512
  458.6 30.9 %collective-permute-start.29 = (bf16[576,1152]{1,0:T(8,128)(2,1)}, bf16[576,1152]{1,0:T(8,128)(2,1)}, u32[]{:S(2)}, u32[]{:S(2)}) collective-permute-start(bf16[576,1152]{1,0:T(8,128)(2,1)} %get-tuple-element.177), channel_id=1, source_target_pairs={{0,16},{16,0},{1,17},{17,1},{2,18},{18,2},{3,19},{19,3},{4,20},{20... | collective-permute-start | bytes 3981320 | tf_op jit(solution)/shard_map/ppermute | solution.py:512
  464.7 44.9 %collective-permute-start.28 = (bf16[512,1152]{1,0:T(8,128)(2,1)}, bf16[512,1152]{1,0:T(8,128)(2,1)}, u32[]{:S(2)}, u32[]{:S(2)}) collective-permute-start(bf16[512,1152]{1,0:T(8,128)(2,1)} %add_convert_fusion.8.q_ref), channel_id=1, source_target_pairs={{0,8},{8,0},{1,9},{9,1},{2,10},{10,2},{3,11},{11,3},{4,12},{12,4},... | collective-permute-start | bytes 3538952 | tf_op jit(solution)/shard_map/ppermute | solution.py:490
  466.2 248.4 %reduce-scatter.11.cloned.1.call-start = ((), (), s32[]{:S(2)}) async-start(), calls=%async_computation.12 | async-start | bytes 1658880 | tf_op jit(solution)/shard_map/reduce_scatter | solution.py:534
  532.6 30.9 %collective-permute-start.33 = (bf16[576,1152]{1,0:T(8,128)(2,1)}, bf16[576,1152]{1,0:T(8,128)(2,1)}, u32[]{:S(2)}, u32[]{:S(2)}) collective-permute-start(bf16[576,1152]{1,0:T(8,128)(2,1)} %get-tuple-element.195), channel_id=1, source_target_pairs={{0,16},{16,0},{1,17},{17,1},{2,18},{18,2},{3,19},{19,3},{4,20},{20... | collective-permute-start | bytes 3981320 | tf_op jit(solution)/shard_map/ppermute | solution.py:512
  532.8 181.7 %reduce-scatter.15.cloned.1.call-start = ((), (), s32[]{:S(2)}) async-start(), calls=%async_computation.14 | async-start | bytes 1658880 | tf_op jit(solution)/shard_map/reduce_scatter | solution.py:534
  538.7 42.5 %collective-permute-start.32 = (bf16[512,1152]{1,0:T(8,128)(2,1)}, bf16[512,1152]{1,0:T(8,128)(2,1)}, u32[]{:S(2)}, u32[]{:S(2)}) collective-permute-start(bf16[512,1152]{1,0:T(8,128)(2,1)} %add_convert_fusion.7.q_ref), channel_id=1, source_target_pairs={{0,8},{8,0},{1,9},{9,1},{2,10},{10,2},{3,11},{11,3},{4,12},{12,4},... | collective-permute-start | bytes 3538952 | tf_op jit(solution)/shard_map/ppermute | solution.py:490
  589.5 35.4 %collective-permute-start.19 = (bf16[512,1152]{1,0:T(8,128)(2,1)}, bf16[512,1152]{1,0:T(8,128)(2,1)}, u32[]{:S(2)}, u32[]{:S(2)}) collective-permute-start(bf16[512,1152]{1,0:T(8,128)(2,1)} %get-tuple-element.145), channel_id=1, source_target_pairs={{0,4},{4,0},{1,5},{5,1},{2,6},{6,2},{3,7},{7,3},{8,12},{12,8},{9,1... | collective-permute-start | bytes 3538952 | tf_op jit(solution)/shard_map/ppermute | solution.py:494
  593.0 36.9 %collective-permute-start.36 = (bf16[576,1152]{1,0:T(8,128)(2,1)}, bf16[576,1152]{1,0:T(8,128)(2,1)}, u32[]{:S(2)}, u32[]{:S(2)}) collective-permute-start(bf16[576,1152]{1,0:T(8,128)(2,1)} %get-tuple-element.205), channel_id=1, source_target_pairs={{0,16},{16,0},{1,17},{17,1},{2,18},{18,2},{3,19},{19,3},{4,20},{20... | collective-permute-start | bytes 3981320 | tf_op jit(solution)/shard_map/ppermute | solution.py:512
  593.2 121.4 %reduce-scatter.9.cloned.1.call-start = ((), (), s32[]{:S(2)}) async-start(), calls=%async_computation.11 | async-start | bytes 1658880 | tf_op jit(solution)/shard_map/reduce_scatter | solution.py:534
  628.4 107.7 %collective-permute-start.20 = (bf16[256,1152]{1,0:T(8,128)(2,1)}, bf16[256,1152]{1,0:T(8,128)(2,1)}, u32[]{:S(2)}, u32[]{:S(2)}) collective-permute-start(bf16[256,1152]{1,0:T(8,128)(2,1)} %dynamic-slice_bitcast_fusion.5), channel_id=1, source_target_pairs={{0,8},{8,0},{1,9},{9,1},{2,10},{10,2},{3,11},{11,3},{4,12},{12,4},... | collective-permute-start | bytes 1769480 | tf_op jit(solution)/shard_map/ppermute | solution.py:490
  635.2 83.8 %reduce-scatter.7.cloned.1.call-start = ((), (), s32[]{:S(2)}) async-start(), calls=%async_computation.10 | async-start | bytes 1658880 | tf_op jit(solution)/shard_map/reduce_scatter | solution.py:534
  642.0 39.9 %collective-permute-start.37 = (bf16[256,1152]{1,0:T(8,128)(2,1)}, bf16[256,1152]{1,0:T(8,128)(2,1)S(1)}, u32[]{:S(2)}, u32[]{:S(2)}) collective-permute-start(bf16[256,1152]{1,0:T(8,128)(2,1)} %get-tuple-element.338), channel_id=1, source_target_pairs={{0,8},{8,0},{1,9},{9,1},{2,10},{10,2},{3,11},{11,3},{4,12},{12,4},... | collective-permute-start | bytes 1769480 | tf_op jit(solution)/shard_map/ppermute | solution.py:490
  682.0 146.3 %reduce-scatter.17.cloned.1.call-start = ((), (), s32[]{:S(2)}) async-start(), calls=%async_computation.15 | async-start | bytes 1658880 | tf_op jit(solution)/shard_map/reduce_scatter | solution.py:534
  690.6 35.7 %collective-permute-start.45 = (f32[24,1152]{1,0:T(8,128)S(1)}, f32[24,1152]{1,0:T(8,128)}, u32[]{:S(2)}, u32[]{:S(2)}) collective-permute-start(f32[24,1152]{1,0:T(8,128)S(1)} %concatenate.57), channel_id=1, source_target_pairs={{0,1},{1,0},{2,3},{3,2},{4,5},{5,4},{6,7},{7,6},{8,9},{9,8},{10,11... | collective-permute-start | bytes 331784 | tf_op jit(solution)/shard_map/ppermute | solution.py:512
  (174 other events, 1402.1 us)
Sparse Core Ops, SparseCore 0:
  41.9 59.0 all-gather.4
  103.6 85.9 all-gather.6
  192.3 52.7 all-gather.8
  247.1 107.1 all-gather.10
  466.3 33.5 reduce-scatter.12
  532.9 33.5 reduce-scatter.10
  593.3 33.9 reduce-scatter.14
  635.3 33.6 reduce-scatter.8
  682.1 36.8 reduce-scatter.6
  769.3 58.9 reduce-scatter.16

commit v3 on v2

--- a/solution.py
+++ b/solution.py
@@ -54,6 +54,11 @@
     return pl.BlockSpec(tuple(dims), lambda i: (0,) * len(dims))
 
 
+def columns(weight):
+    array, width, place = weight
+    return pl.BlockSpec((array.shape[0], width), lambda i: (0, place))
+
+
 def split(half, block, width):
     n = half // block
     own = pl.BlockSpec((block, width), lambda i: (jnp.minimum(i, n - 1), 0))
@@ -84,42 +89,52 @@
     return pl.pallas_call(
         project_kernel,
         grid=(2 * n,),
-        in_specs=[own_spec, rec_spec, const(weight.shape), const((1, width))],
+        in_specs=[own_spec, rec_spec, columns(weight), const((1, width))],
         out_specs=pl.BlockSpec((half // n, width), lambda i: (i, 0)),
         out_shape=shape((2 * half, width), bf16),
         compiler_params=params(24),
         cost_estimate=cost(4 * half * depth * width, 2 * depth * (2 * half + width)),
-    )(own, rec, weight, shift[None])
+    )(own, rec, weight[0], shift[None])
 
 
 def attend_kernel(heads, dim, offset, count, *refs):
     qid_ref, kid_ref, q_ref, wo_ref = refs[:4]
     kv_refs = refs[4 : 4 + count]
-    o_ref, own_ref, rec_ref = refs[4 + count :]
+    o_ref, total_ref, own_ref, rec_ref = refs[4 + count :]
     factor = dim**-0.5 * math.log2(math.e)
     width = heads * dim
     same = qid_ref[...] == kid_ref[...]
-    outs = []
-    for h in range(heads):
+
+    def scores(h):
         lo = h * dim
-        at = offset + width + lo
         q = q_ref[:, lo : lo + dim]
         k = jnp.concatenate([ref[:, offset + lo : offset + lo + dim] for ref in kv_refs])
+        return jnp.where(same, mm_last(q, k), NEGATIVE)
+
+    keys = sum(ref.shape[0] for ref in kv_refs)
+    ones = jnp.ones((keys, 8), bf16)
+    outs, totals = [], []
+    following = scores(0)
+    for h in range(heads):
+        at = offset + width + h * dim
         v = jnp.concatenate([ref[:, at : at + dim] for ref in kv_refs])
-        s = jnp.where(same, mm_last(q, k), NEGATIVE)
+        s = following
+        if h < heads - 1:
+            following = scores(h + 1)
         top = jnp.max(s, axis=1, keepdims=True)
-        p = jnp.exp2((s - top) * factor)
-        total = jnp.sum(p, axis=1, keepdims=True)
-        outs.append(mm(p.astype(bf16), v) / total)
-    o = jnp.concatenate(outs, axis=1).astype(bf16)
-    o_ref[...] = o
-    terms = mm(o, wo_ref[...])
+        p = jnp.exp2((s - top) * factor).astype(bf16)
+        o = mm(p, jnp.concatenate([v, ones], axis=1))
+        total = o[:, dim : dim + 1]
+        outs.append(o[:, :dim] * (1.0 / total))
+        totals.append(top * factor + jnp.log2(total))
+    o_ref[...] = jnp.concatenate(outs, axis=1).astype(bf16)
+    total_ref[...] = jnp.concatenate(totals + totals, axis=1)
 
     def own_work():
-        own_ref[...] = terms
+        own_ref[...] = mm(o_ref[...], wo_ref[...])
 
     def rec_work():
-        rec_ref[...] = terms.astype(bf16)
+        rec_ref[...] = mm(o_ref[...], wo_ref[...]).astype(bf16)
 
     either(own_work, rec_work)
 
@@ -139,9 +154,15 @@
             const(out_full.shape),
         ]
         + [const(kv.shape) for kv in kvs],
-        out_specs=[pl.BlockSpec((block, width), lambda i: (i, 0)), own_spec, rec_spec],
+        out_specs=[
+            pl.BlockSpec((block, width), lambda i: (i, 0)),
+            pl.BlockSpec((block, 2 * heads), lambda i: (i, 0)),
+            own_spec,
+            rec_spec,
+        ],
         out_shape=[
             shape((rows, width), bf16),
+            shape((rows, 2 * heads), f32),
             shape((rows // 2, wide), f32),
             shape((rows // 2, wide), bf16),
         ],
@@ -151,9 +172,9 @@
 
 
 def attend_back_kernel(heads, dim, offset, count, first, last, *refs):
-    qid_ref, kid_ref, q_ref, wo_ref, own_ref, rec_ref = refs[:6]
-    kv_refs = refs[6 : 6 + count]
-    rest = refs[6 + count :]
+    qid_ref, kid_ref, q_ref, o_ref, total_ref, wo_ref, own_ref, rec_ref = refs[:8]
+    kv_refs = refs[8 : 8 + count]
+    rest = refs[8 + count :]
     if not first:
         before_ref, rest = rest[0], rest[1:]
     dq_ref, dkv_ref, do_ref, acc_ref = rest
@@ -174,6 +195,7 @@
 
     either(own_work, rec_work)
     same = kid_ref[...] == qid_ref[...]
+    ones = jnp.ones((8, dim), bf16)
     dqs = []
     for h in range(heads):
         lo = h * dim
@@ -183,12 +205,12 @@
         k = jnp.concatenate([ref[:, offset + lo : offset + lo + dim] for ref in kv_refs])
         v = jnp.concatenate([ref[:, at : at + dim] for ref in kv_refs])
         s = jnp.where(same, mm_last(k, q), NEGATIVE)
-        top = jnp.max(s, axis=0, keepdims=True)
-        p = jnp.exp2((s - top) * factor)
-        p = p * (1.0 / jnp.sum(p, axis=0, keepdims=True))
+        p = jnp.exp2(s * factor - total_ref[h : h + 1, :])
         dp = mm_last(v, do)
-        delta = jnp.sum(p * dp, axis=0, keepdims=True)
-        ds = (p * (dp - delta)).astype(bf16)
+        both = do.astype(f32) * o_ref[:, lo : lo + dim].astype(f32)
+        high = both.astype(bf16)
+        delta = mm_last(ones, high) + mm_last(ones, (both - high.astype(f32)).astype(bf16))
+        ds = (p * (dp - delta[:1])).astype(bf16)
         acc_ref[heads + h] += mm(p.astype(bf16), do)
         acc_ref[h] += mm(ds, q)
         dqs.append(mm_first(ds, k) * scale)
@@ -204,7 +226,9 @@
             dkv_ref[...] = acc_ref[...]
 
 
-def attend_back(qkv, kvs, offset, query_ids, key_ids, out_full, own, rec, before, last, heads, dim):
+def attend_back(
+    qkv, kvs, offset, query_ids, key_ids, o, totals, out_full, own, rec, before, last, heads, dim
+):
     rows, width, wide = qkv.shape[0], heads * dim, out_full.shape[1]
     keys = sum(kv.shape[0] for kv in kvs)
     sums = (2 * heads, keys, dim)
@@ -219,6 +243,8 @@
             pl.BlockSpec((1, block), lambda i: (0, i)),
             const((keys, 1)),
             pl.BlockSpec((block, qkv.shape[1]), lambda i: (i, 0)),
+            pl.BlockSpec((block, width), lambda i: (i, 0)),
+            pl.BlockSpec((2 * heads, block), lambda i: (0, i)),
             const(out_full.shape),
             own_spec,
             rec_spec,
@@ -229,7 +255,7 @@
         scratch_shapes=[pltpu.VMEM((block, width), bf16), pltpu.VMEM(sums, f32)],
         compiler_params=params(52),
         cost_estimate=cost(24 * rows * keys * width, 30 * rows * width, heads * rows * keys),
-    )(query_ids[None, :], key_ids[:, None], qkv, out_full, own, rec, *kvs, *extra)
+    )(query_ids[None, :], key_ids[:, None], qkv, o, totals.T, out_full, own, rec, *kvs, *extra)
 
 
 def join_kernel(dq_ref, dkv_ref, w_ref, dqkv_ref, own_ref, rec_ref, sum_ref):
@@ -240,19 +266,19 @@
     dqkv = jnp.concatenate([dq_ref[...], dkv_ref[...]], axis=1)
     dqkv_ref[...] = dqkv
     sum_ref[...] += jnp.sum(dqkv.astype(f32), axis=0, keepdims=True)
-    terms = mm_last(dqkv, w_ref[:, : dqkv.shape[1]])
+    width = dqkv.shape[1]
 
     def own_work():
-        own_ref[...] = terms
+        own_ref[...] = mm_last(dqkv_ref[...], w_ref[:, :width])
 
     def rec_work():
-        rec_ref[...] = terms.astype(bf16)
+        rec_ref[...] = mm_last(dqkv_ref[...], w_ref[:, :width]).astype(bf16)
 
     either(own_work, rec_work)
 
 
 def join(dq, dkv, chunk, weight):
-    rows, width, wide = dq.shape[0], dq.shape[1] + dkv.shape[1], weight.shape[0]
+    rows, width, wide = dq.shape[0], dq.shape[1] + dkv.shape[1], weight[0].shape[0]
     n, own_spec, rec_spec, _ = split(rows // 2, min(rows // 2, 256), wide)
     block, at = rows // (2 * n), 2 * n * chunk
     return pl.pallas_call(
@@ -261,7 +287,7 @@
         in_specs=[
             pl.BlockSpec((block, dq.shape[1]), lambda i: (i, 0)),
             pl.BlockSpec((block, dkv.shape[1]), lambda i: (at + i, 0)),
-            const(weight.shape),
+            columns(weight),
         ],
         out_specs=[pl.BlockSpec((block, width), lambda i: (i, 0)), own_spec, rec_spec, const((1, width))],
         out_shape=[
@@ -272,7 +298,7 @@
         ],
         compiler_params=params(24),
         cost_estimate=cost(2 * rows * width * wide, 4 * wide * (rows + width)),
-    )(dq, dkv, weight)
+    )(dq, dkv, weight[0])
 
 
 def hidden_kernel(own_ref, rec_ref, up_ref, down_ref, shift_ref, slope_ref, act_ref, po_ref, pr_ref):
@@ -296,13 +322,13 @@
 
 def hidden(own, rec, up, down, shift):
     half, wide = own.shape
-    ff = up.shape[1]
+    ff = up[1]
     n, own_spec, rec_spec, _ = split(half, min(half, 256), wide)
     strip = pl.BlockSpec((half // n, ff), lambda i: (i, 0))
     return pl.pallas_call(
         hidden_kernel,
         grid=(2 * n,),
-        in_specs=[own_spec, rec_spec, const(up.shape), const(down.shape), const((1, ff))],
+        in_specs=[own_spec, rec_spec, columns(up), columns(down), const((1, ff))],
         out_specs=[strip, strip, own_spec, rec_spec],
         out_shape=[
             shape((2 * half, ff), bf16),
@@ -312,7 +338,7 @@
         ],
         compiler_params=params(30),
         cost_estimate=cost(8 * half * wide * ff, 4 * wide * ff + 20 * half * wide, 2 * half * ff),
-    )(own, rec, up, down, shift[None])
+    )(own, rec, up[0], down[0], shift[None])
 
 
 def hidden_back_kernel(own_ref, rec_ref, slope_ref, up_ref, down_ref, de_ref, sum_ref, po_ref, pr_ref):
@@ -331,13 +357,13 @@
 
 def hidden_back(own, rec, slope, up, down):
     half, wide = own.shape
-    ff = up.shape[1]
+    ff = up[1]
     n, own_spec, rec_spec, _ = split(half, min(half, 256), wide)
     strip = pl.BlockSpec((half // n, ff), lambda i: (i, 0))
     return pl.pallas_call(
         hidden_back_kernel,
         grid=(2 * n,),
-        in_specs=[own_spec, rec_spec, strip, const(up.shape), const(down.shape)],
+        in_specs=[own_spec, rec_spec, strip, columns(up), columns(down)],
         out_specs=[strip, const((1, ff)), own_spec, rec_spec],
         out_shape=[
             shape((2 * half, ff), bf16),
@@ -347,7 +373,7 @@
         ],
         compiler_params=params(30),
         cost_estimate=cost(8 * half * wide * ff, 4 * wide * ff + 16 * half * wide),
-    )(own, rec, slope, up, down)
+    )(own, rec, slope, up[0], down[0])
 
 
 def outer_kernel(lefts, rights, beside, bit_ref, *refs):
@@ -532,15 +558,6 @@
 
 def scatter_rows(terms):
     return lax.psum_scatter(terms, "seq", scatter_dimension=0, tiled=True)
-
-
-def sum_everywhere(v):
-    for axis in AXES[::-1]:
-        step = 1
-        while step < lax.axis_size(axis):
-            v = v + flip(v, axis, step)
-            step *= 2
-    return v
 
 
 def body(
@@ -619,7 +636,7 @@
     payload = jnp.concatenate([came[:, : 3 * part], out_rows(0), came[:, 3 * part :]], axis=1)
     first = gather_rows(payload)
     small_full = first[:, width:].T.reshape(layers, kinds, width).astype(f32)
-    qkv_fulls.append(first)
+    qkv_fulls.append((first, first.shape[1], 0))
     out_fulls.append(first[:, 3 * part : width].reshape(part, width))
     later = [
         ff_columns(piece) for l in range(layers) for piece in (up_weight[l], down_weight[l])
@@ -632,12 +649,11 @@
             at = 2 * layers * ff_pad + (l - 1) * 3 * part
             payload = jnp.concatenate([later[:, at : at + 3 * part], out_rows(l)], axis=1)
             full = gather_rows(payload)
-            qkv_fulls.append(full)
+            qkv_fulls.append((full, width, 0))
             out_fulls.append(full[:, 3 * part :].reshape(part, width))
-        at = 2 * l * ff_pad
-        full = gather_rows(later[:, at : at + 2 * ff_pad])
-        up_fulls.append(full[:, :ff_pad])
-        down_fulls.append(full[:, ff_pad:])
+        full = gather_rows(later[:, 2 * l * ff_pad : 2 * (l + 1) * ff_pad])
+        up_fulls.append((full, ff_pad, 0))
+        down_fulls.append((full, ff_pad, 1))
     up_shift = pick(up_bias.reshape(layers, RANKS, ff_part), rank, 1).astype(f32)
     up_shift = jnp.pad(up_shift, ((0, 0), (0, ff_pad - ff_part)))
 
@@ -683,9 +699,6 @@
 
     def last_sum(qs):
         return at_x(qs, xi), swap_x(at_x(qs, 1 - xi))
-
-    def to_rows(v):
-        return plain_order(lax.ppermute(v.astype(bf16), AXES, back))
 
     GAIN1, GAIN2, OFF1, QB, VB, OB, OFF2, DB = range(8)
     starts = chunks_of(arrived)
@@ -702,12 +715,13 @@
         qkv = [project(own, rec, qkv_fulls[l], shift) for own, rec in attn_in]
         kvs = [keys_of(v) for v in qkv]
         offset, kvs = kvs[0][1], [v[0] for v in kvs]
-        attended, after, normed = [], [], []
+        attended, totals, after, normed = [], [], [], []
         for j in range(CHUNKS):
-            o, own, other = attend(
+            o, total, own, other = attend(
                 qkv[j], kvs, offset, query_ids[j], key_ids, out_fulls[l], heads, dim
             )
             attended.append(o)
+            totals.append(total)
             q = core_sum(own, other)
             if l == layers - 1 and j == 0:
                 q, cotangent = tie((q, cotangent))
@@ -720,7 +734,7 @@
             normed.append(m)
         mlp_in = [(v, swap_c(v)) for v in normed]
         if l == layers - 1:
-            mlp_in, rounded = tie((mlp_in, chunks_of(arrived)))
+            rounded = chunks_of(arrived)
         slopes, acts, qs, following, normed = [], [], [], [], []
         for j in range(CHUNKS):
             slope, act, own, other = hidden(*mlp_in[j], up_fulls[l], down_fulls[l], up_shift[l])
@@ -734,12 +748,10 @@
                 )
                 following.append(u)
                 normed.append(m)
-        saved.append((current, attn_in, qkv, kvs, attended, after, mlp_in, slopes, acts))
+        saved.append((current, attn_in, qkv, kvs, attended, totals, after, mlp_in, slopes, acts))
         current = following
         if l == layers - 1:
-            q, come = last_sum(qs)
-            final = at_x(after, xi) + (q.astype(f32) + come.astype(f32) + small[DB])
-            output = to_rows(final)
+            output = (qs, after, small[DB])
 
     grads = [None] * layers
     vectors = [None] * layers
@@ -749,11 +761,18 @@
     tokens_grad = None
     top_bit = (lax.axis_index("hi") // (blocks // 2)).astype(jnp.int32)[None]
 
-    waiting = None
+    def home_of(pieces):
+        return exchange(jnp.concatenate(pieces, axis=1).reshape(RANKS, held, -1))
+
+
+    waiting, homes = None, [None] * layers
     for l in reversed(range(layers)):
-        (current, attn_in, qkv, kvs, attended, after, mlp_in, slopes, acts) = saved[l]
+        (current, attn_in, qkv, kvs, attended, totals, after, mlp_in, slopes, acts) = saved[l]
         small = small_full[l]
+        last_layer = waiting is None
         down_in = [(v, swap_c(v)) for v in rounded]
+        down_terms = outer([v for pair in down_in for v in pair], acts, top_bit)
+        down_in, down_terms = tie((down_in, down_terms))
         des, qs, bias = [], [], 0.0
         for j in range(CHUNKS):
             de, sums, own, other = hidden_back(*down_in[j], slopes[j], up_fulls[l], down_fulls[l])
@@ -761,16 +780,26 @@
             bias = bias + sums[0]
             qs.append(core_sum(own, other))
         biases[l] = bias
-        qs, des, down_in = tie((qs, des, down_in))
-        comes = [swap_x(q) for q in qs]
-        down_terms = outer([v for pair in down_in for v in pair], acts, top_bit)
-        up_terms = outer([v for pair in mlp_in for v in pair], des, top_bit)
-        if waiting is None:
-            comes, down_terms, up_terms = tie((comes, down_terms, up_terms))
+        if last_layer:
+            qs, des = tie((qs, des))
         else:
             waiting = halve_rows(*waiting)
-            comes, down_terms, up_terms, waiting = tie((comes, down_terms, up_terms, waiting))
-            grads[l + 1][2] = scatter_rows(waiting)
+            qs, des, waiting = tie((qs, des, waiting))
+            waiting = scatter_rows(waiting)
+        comes = [swap_x(q) for q in qs]
+        up_terms = outer([v for pair in mlp_in for v in pair], des, top_bit)
+        down_terms = halve_rows(*down_terms)
+        if last_layer:
+            comes, down_terms, up_terms, output = tie((comes, down_terms, up_terms, output))
+            q, come = last_sum(output[0])
+            output = at_x(output[1], xi) + (q.astype(f32) + come.astype(f32) + output[2])
+            output = output.astype(bf16)
+        else:
+            comes, down_terms, up_terms, grads[l + 1][2], output = tie(
+                (comes, down_terms, up_terms, waiting, output)
+            )
+            output = lax.ppermute(output, AXES, back)
+        down_owned = scatter_rows(down_terms)
         rounded, mid, sums = [], [], 0.0
         for j in range(CHUNKS):
             g, r, s = norm_back(after[j], qs[j], comes[j], grad[j], small, GAIN2)
@@ -782,8 +811,8 @@
         acc, dqs = None, []
         for j in range(CHUNKS):
             dq, acc = attend_back(
-                qkv[j], kvs, 0 if ways > 1 else part, query_ids[j], key_ids, out_fulls[l],
-                *out_in[j], acc, j == CHUNKS - 1, heads, dim,
+                qkv[j], kvs, 0 if ways > 1 else part, query_ids[j], key_ids, attended[j],
+                totals[j], out_fulls[l], *out_in[j], acc, j == CHUNKS - 1, heads, dim,
             )
             dqs.append(dq)
         if ways > 1:
@@ -795,15 +824,24 @@
                 tiled=True,
                 axis_index_groups=seq_groups,
             )
-        dqkvs, qs, columns = [], [], 0.0
+        if not last_layer:
+            dqs, acc, output = tie((dqs, acc, output))
+        dqkvs, qs, sums_qkv = [], [], 0.0
         for j in range(CHUNKS):
             dqkv, own, other, s = join(dqs[j], acc, j, qkv_fulls[l])
             dqkvs.append(dqkv)
-            columns = columns + s[0]
+            sums_qkv = sums_qkv + s[0]
             qs.append(core_sum(own, other))
-        down_terms = halve_rows(*down_terms)
-        qs, dqkvs, out_in, down_terms = tie((qs, dqkvs, out_in, down_terms))
-        down_owned = scatter_rows(down_terms)
+        up_terms = halve_rows(*up_terms)
+        if last_layer:
+            qs, dqkvs, out_in, up_terms, down_owned, output = tie(
+                (qs, dqkvs, out_in, up_terms, down_owned, output)
+            )
+        else:
+            qs, dqkvs, out_in, up_terms, down_owned = tie(
+                (qs, dqkvs, out_in, up_terms, down_owned)
+            )
+        up_owned = scatter_rows(up_terms)
         if l > 0:
             comes = [swap_x(q) for q in qs]
         else:
@@ -813,9 +851,10 @@
             [v for pair in out_in for v in pair],
         ).reshape(width, part)
         waiting = outer([v for pair in attn_in for v in pair], dqkvs, top_bit, out_terms)
-        up_terms = halve_rows(*up_terms)
-        comes, waiting, up_terms = tie((comes, waiting, up_terms))
-        up_owned = scatter_rows(up_terms)
+        if not last_layer:
+            homes[l + 1] = home_of([grads[l + 1][0], grads[l + 1][1], grads[l + 1][2][:, : 3 * part]])
+            comes, homes[l + 1] = tie((comes, homes[l + 1]))
+        comes, waiting, up_owned = tie((comes, waiting, up_owned))
         d_next = None
         if l > 0:
             grad, rounded, sums = [], [], 0.0
@@ -827,14 +866,14 @@
             d_next = sums[2]
         else:
             g, r, sums = norm_back(at_x(current, xi), q, comes, at_x(mid, xi), small, GAIN1)
-            tokens_grad = to_rows(r)
+            tokens_grad = r
         vectors[l] = jnp.stack(
             [
                 sums[0],
                 gain_two_sum,
                 sums[1],
-                placed(columns[:part]),
-                placed(columns[2 * part :]),
+                placed(sums_qkv[:part]),
+                placed(sums_qkv[2 * part :]),
                 o_sum,
                 off_two_sum,
                 d_sum,
@@ -842,31 +881,6 @@
         )
         d_sum = d_next
         grads[l] = [up_owned, down_owned, None]
-
-    waiting = halve_rows(*waiting)
-    early = [v for l in range(layers) for v in grads[l][: 2 if l == 0 else 3]]
-    early, waiting = tie((early, waiting))
-    grads[0][2] = scatter_rows(waiting)
-    for l in range(1, layers):
-        grads[l][2] = early[3 * l + 1]
-    early = [v[:, : 3 * part] if i > 2 and i % 3 == 1 else v for i, v in enumerate(early)]
-    widths = [v.shape[1] for v in early]
-    early = exchange(jnp.concatenate(early, axis=1).reshape(RANKS, held, -1))
-    homes = iter(
-        lax.slice_in_dim(early, sum(widths[:i]), sum(widths[: i + 1]), axis=2)
-        for i in range(len(widths))
-    )
-    results = [[None] * layers for _ in range(4)]
-    for l in range(layers):
-        owned = grads[l][2]
-        results[1][l] = plain_order(owned[:, 3 * part :].reshape(held, width))
-        for i in (2, 3):
-            results[i][l] = next(homes)[:, :, :ff_part].transpose(1, 0, 2).reshape(held, ff)
-        owned = owned[:, : 3 * part].reshape(RANKS, held, 3 * part)
-        qkv_grad = exchange(owned) if l == 0 else next(homes)
-        qkv_grad = qkv_grad.reshape(RANKS, held, 3, blocks, chunk).transpose(1, 2, 3, 0, 4)
-        results[0][l] = qkv_grad.reshape(held, 3 * width)
-    results = [jnp.stack(v).astype(f32) for v in results]
 
     spots = (jnp.arange(RANKS) == rank)[None, :, None]
     bias = jnp.where(spots, jnp.stack(biases)[:, None, :], 0.0).reshape(layers * RANKS, ff_pad)
@@ -877,15 +891,42 @@
             jnp.pad(bias, ((0, 0), (0, wide - ff_pad))),
         ]
     )
-    both = sum_everywhere(both)
+    tokens_grad = lax.ppermute(tokens_grad, AXES, back)
+
+    def sum_along(v, axis):
+        step = 1
+        while step < lax.axis_size(axis):
+            v = v + flip(v, axis, step)
+            step *= 2
+        return v
+
+    both = sum_along(sum_along(sum_along(both, "c"), "x"), "hi")
+    mine_last, theirs_last = waiting
+    mine_last, both, tokens_grad = tie((mine_last, both, tokens_grad))
+    last = scatter_rows(halve_rows(mine_last, theirs_last))
+    both = sum_along(both, "seq")
+    grads[0][2] = last
+    homes[0] = home_of([grads[0][0], grads[0][1], last[:, : 3 * part]])
+    results = [[None] * layers for _ in range(4)]
+    for l in range(layers):
+        owned = grads[l][2]
+        results[1][l] = plain_order(owned[:, 3 * part :].reshape(held, width))
+        for i in (2, 3):
+            home = homes[l][:, :, (i - 2) * ff_pad : (i - 2) * ff_pad + ff_part]
+            results[i][l] = home.transpose(1, 0, 2).reshape(held, ff)
+        qkv_grad = homes[l][:, :, 2 * ff_pad :]
+        qkv_grad = qkv_grad.reshape(RANKS, held, 3, blocks, chunk).transpose(1, 2, 3, 0, 4)
+        results[0][l] = qkv_grad.reshape(held, 3 * width)
+    results = [jnp.stack(v).astype(f32) for v in results]
+
     vector = both[: layers * kinds, :width].reshape(layers, kinds, blocks, seqs, RANKS, held)
     for axis, index in ((2, "hi"), (2, "seq")):
         vector = pick(vector, lax.axis_index(index), axis)
     vector = pick(vector, rank, 2).swapaxes(1, 2)
     bias = both[layers * kinds :, :ff_part].reshape(layers, ff)
     return (
-        output,
-        tokens_grad,
+        plain_order(output),
+        plain_order(tokens_grad),
         *results,
         bias,
         vector[:, :, :2],

time: 860 us -> 824 us (0.958)
  waiting for transfers between devices: 310 us -> 236 us
  local copies, waits for them, and re-layouts: 145 us -> 171 us
  starting transfers between devices: 101 us -> 115 us
  other arithmetic: 68.7 us -> 79.6 us
    ppermute x11, waiting for transfers between devices: 101 us -> 55.7 us  [flip(): return lax.ppermute(v, axis, [(i, i ^ step) for i in range(size)])]
    unnamed x290 -> x274, local copies, waits for them, and re-layouts: 65 us -> 83.6 us
    ppermute x14, starting transfers between devices: 21 us -> 31 us  [swap_x(): return lax.ppermute(v, 'x', SWAP)]
    ppermute x20, waiting for transfers between devices: 19.3 us -> 9.75 us  [swap_c(): return lax.ppermute(v, 'c', SWAP)]
    pallas_call x2, Pallas kernels: 33.9 us -> 25.1 us  [attend(): pl.pallas_call(functools.partial(attend_kernel, heads, dim, offset, len(k...]
    reduce_scatter x6, waiting for transfers between devices: 47.8 us -> 39.2 us  [scatter_rows(): return lax.psum_scatter(terms, 'seq', scatter_dimension=0, tiled=True)]
  transfers between devices with their start and end apart: 60 -> 60, of which waited for: 32 -> 24; matrix products, arithmetic and copies ran while one was open for 20% -> 19% of each run, Pallas kernels for 21% -> 20%
where the time goes in v3:
time: 824 us; the launch traced here: 816 us
  waiting for transfers between devices  236 us (29%)
  Pallas kernels  185 us (22%)
  local copies, waits for them, and re-layouts  171 us (21%)
  starting transfers between devices  115 us (14%)
  other arithmetic  79.6 us (10%)
  between operations  16.3 us (2%)
  matrix products  13.3 us (2%)
    ppermute x14, waiting for transfers between devices, swap_x(): return lax.ppermute(v, 'x', SWAP)  99.5 us
    unnamed x274, local copies, waits for them, and re-layouts  83.6 us
    ppermute x20, starting transfers between devices, swap_c(): return lax.ppermute(v, 'c', SWAP)  58.7 us
    ppermute x11, waiting for transfers between devices, flip(): return lax.ppermute(v, axis, [(i, i ^ step) for i in range(size)])  55.7 us
    pallas_call x2, Pallas kernels, attend_back(): pl.pallas_call(functools.partial(attend_back_kernel, heads, dim, offset,...  44 us
    reduce_scatter x6, waiting for transfers between devices, scatter_rows(): return lax.psum_scatter(terms, 'seq', scatter_dimension=0, tiled=True)  39.2 us
    pallas_call x6, Pallas kernels, outer(): pl.pallas_call(functools.partial(outer_kernel, len(lefts), len(rights), l...  31.4 us
    ppermute x14, starting transfers between devices, swap_x(): return lax.ppermute(v, 'x', SWAP)  31 us
  transfers between devices with their start and end apart: 60, of which 24 were waited for; matrix products, arithmetic and copies ran while one was open for 19% of the time, Pallas kernels for 20%

profile of v3, /device:TPU:1, one launch (start us, length us, event | category | flops | bytes accessed | tf_op | source)
XLA Modules:
  0.0 816.2 jit_solution(5304359935461755674)
XLA Ops:
  45.2 12.5 %collective-permute-done.9 = bf16[2,36,5472]{2,0,1:T(2,128)(2,1)S(1)} collective-permute-done((bf16[2,36,5472]{2,0,1:T(2,128)(2,1)S(1)}, bf16[2,36,5472]{2,0,1:T(2,128)(2,1)S(1)}, u32[]{:S(2)}, u32[]{:S(2)}) %collective-permute-start.9) | collective-permute-done | bytes 788000 | tf_op jit(solution)/shard_map/ppermute | solution.py:516
  64.4 7.2 collective-permute-start.10
  83.9 13.5 %collective-permute-done.4 = bf16[256,1152]{1,0:T(8,128)(2,1)S(1)} collective-permute-done((bf16[256,1152]{1,0:T(8,128)(2,1)S(1)}, bf16[256,1152]{1,0:T(8,128)(2,1)S(1)}, u32[]{:S(2)}, u32[]{:S(2)}) %collective-permute-start.4) | collective-permute-done | bytes 589856 | tf_op jit(solution)/shard_map/ppermute | solution.py:516
  98.8 10.1 %all-gather.5.cloned.1.call-done.w_ref = bf16[1152,1168]{1,0:T(8,128)(2,1)} async-done(((bf16[144,1168]{1,0:T(8,128)(2,1)}), bf16[1152,1168]{1,0:T(8,128)(2,1)}) %all-gather.5.cloned.1.call-update) | async-done | bytes 2691088 | tf_op jit(solution)/shard_map/all_gather | solution.py:542
  134.2 13.1 %shard_map.170 = (bf16[1024,288]{1,0:T(8,128)(2,1)S(1)}, f32[1024,8]{1,0:T(8,128)S(1)}, f32[512,1152]{1,0:T(8,128)S(1)}, bf16[512,1152]{1,0:T(8,128)(2,1)}) custom-call(s32[1024,1]{1,0:T(8,128)S(1)} %copy.200.refs_0_, s32[1,1024]{1,0:T(1,128)S(1)} %bitcast.190, bf16[1024,864]{1,0:T(8,128)(2,1)S(1)} %shard_map.169.refs_2_.refs_4_.refs_8_, ...), custom_call_target="tpu_custom_call" | custom-call | flops 301989888 | bytes 471859 | tf_op jit(solution)/shard_map/pallas_call | solution.py:147
  163.4 25.8 %collective-permute-done.7.come_ref = bf16[512,1152]{1,0:T(8,128)(2,1)S(1)} collective-permute-done((bf16[512,1152]{1,0:T(8,128)(2,1)S(1)}, bf16[512,1152]{1,0:T(8,128)(2,1)S(1)}, u32[]{:S(2)}, u32[]{:S(2)}) %collective-permute-start.7) | collective-permute-done | bytes 1179680 | tf_op jit(solution)/shard_map/ppermute | solution.py:516
  200.7 10.4 %shard_map.172 = (bf16[1024,1152]{1,0:T(8,128)(2,1)S(1)}, bf16[1024,1152]{1,0:T(8,128)(2,1)S(1)}, f32[512,1152]{1,0:T(8,128)S(1)}, bf16[512,1152]{1,0:T(8,128)(2,1)}) custom-call(bf16[512,1152]{1,0:T(8,128)(2,1)} %get-tuple-element.141.own_ref.refs_0_, bf16[512,1152]{1,0:T(8,128)(2,1)} %collective-permute-done.8.rec_ref.refs_1_, ...), custom_call_target="tpu_custom_call" | custom-call | flops 543581824 | bytes 1710489 | tf_op jit(solution)/shard_map/pallas_call | solution.py:328
  223.5 26.0 %collective-permute-done.12.come_ref = bf16[512,1152]{1,0:T(8,128)(2,1)S(1)} collective-permute-done((bf16[512,1152]{1,0:T(8,128)(2,1)S(1)}, bf16[512,1152]{1,0:T(8,128)(2,1)S(1)}, u32[]{:S(2)}, u32[]{:S(2)}) %collective-permute-start.12) | collective-permute-done | bytes 1179680 | tf_op jit(solution)/shard_map/ppermute | solution.py:516
  267.5 12.0 %shard_map.175 = (bf16[1024,288]{1,0:T(8,128)(2,1)S(1)}, f32[1024,8]{1,0:T(8,128)S(1)}, f32[512,1152]{1,0:T(8,128)S(1)}, bf16[512,1152]{1,0:T(8,128)(2,1)S(1)}) custom-call(s32[1024,1]{1,0:T(8,128)S(1)} %copy.200.refs_0_, s32[1,1024]{1,0:T(1,128)S(1)} %bitcast.191, bf16[1024,864]{1,0:T(8,128)(2,1)S(1)} %shard_map.174.refs_2_.refs_4_.refs_8_, ...), custom_call_target="tpu_custom_call" | custom-call | flops 301989888 | bytes 471859 | tf_op jit(solution)/shard_map/pallas_call | solution.py:147
  287.9 18.4 %collective-permute-done.16 = bf16[256,1152]{1,0:T(8,128)(2,1)S(1)} collective-permute-done((bf16[256,1152]{1,0:T(8,128)(2,1)S(1)}, bf16[256,1152]{1,0:T(8,128)(2,1)S(1)}, u32[]{:S(2)}, u32[]{:S(2)}) %collective-permute-start.16) | collective-permute-done | bytes 589856 | tf_op jit(solution)/shard_map/ppermute | solution.py:728
  306.3 10.8 %collective-permute-done.15.come_ref = bf16[512,1152]{1,0:T(8,128)(2,1)S(1)} collective-permute-done((bf16[512,1152]{1,0:T(8,128)(2,1)S(1)}, bf16[512,1152]{1,0:T(8,128)(2,1)S(1)}, u32[]{:S(2)}, u32[]{:S(2)}) %collective-permute-start.15) | collective-permute-done | bytes 1179680 | tf_op jit(solution)/shard_map/ppermute | solution.py:516
  324.2 31.6 %collective-permute-start.19 = (bf16[512,1152]{1,0:T(8,128)(2,1)}, bf16[512,1152]{1,0:T(8,128)(2,1)}, u32[]{:S(2)}, u32[]{:S(2)}) collective-permute-start(bf16[512,1152]{1,0:T(8,128)(2,1)} %get-tuple-element.156.own_ref.refs_0_), channel_id=1, source_target_pairs={{0,4},{4,0},{1,5},{5,1},{2,6},{6,2},{3,7},{7,3},{8,12},{12,8},{9,1... | collective-permute-start | bytes 3538952 | tf_op jit(solution)/shard_map/ppermute | solution.py:520
  365.1 9.7 %shard_map.177 = (bf16[1024,1152]{1,0:T(8,128)(2,1)S(1)}, bf16[1024,1152]{1,0:T(8,128)(2,1)S(1)}, f32[512,1152]{1,0:T(8,128)S(1)}, bf16[512,1152]{1,0:T(8,128)(2,1)S(1)}) custom-call(bf16[512,1152]{1,0:T(8,128)(2,1)} %get-tuple-element.156.own_ref.refs_0_, bf16[512,1152]{1,0:T(8,128)(2,1)} %collective-permute-done.19.rec_ref.refs_1_, ...), custom_call_target="tpu_custom_call" | custom-call | flops 543581824 | bytes 1710489 | tf_op jit(solution)/shard_map/pallas_call | solution.py:328
  380.3 9.0 %shard_map.179 = (bf16[1024,1152]{1,0:T(8,128)(2,1)S(1)}, f32[1,1152]{1,0:T(1,128)S(1)}, f32[512,1152]{1,0:T(8,128)S(1)}, bf16[512,1152]{1,0:T(8,128)(2,1)S(1)}) custom-call(bf16[512,1152]{1,0:T(8,128)(2,1)} %get-tuple-element.160.refs_0_.own_ref, bf16[512,1152]{1,0:T(8,128)(2,1)} %collective-permute-done.18.refs_1_.rec_ref, ...), custom_call_target="tpu_custom_call" | custom-call | flops 543581824 | bytes 1474560 | tf_op jit(solution)/shard_map/pallas_call | solution.py:363
  403.9 16.8 %collective-permute-done.22 = bf16[576,1152]{1,0:T(8,128)(2,1)S(1)} collective-permute-done((bf16[576,1152]{1,0:T(8,128)(2,1)S(1)}, bf16[576,1152]{1,0:T(8,128)(2,1)S(1)}, u32[]{:S(2)}, u32[]{:S(2)}) %collective-permute-start.22) | collective-permute-done | bytes 1327136 | tf_op jit(solution)/shard_map/ppermute | solution.py:538
  440.1 21.8 %shard_map.182 = (bf16[1024,288]{1,0:T(8,128)(2,1)S(1)}, bf16[1024,576]{1,0:T(8,128)(2,1)}) custom-call(s32[1,1024]{1,0:T(1,128)S(1)} %bitcast.188, s32[1024,1]{1,0:T(8,128)S(1)} %copy.212.refs_1_, bf16[1024,864]{1,0:T(8,128)(2,1)} %copy-done.5, bf16[1024,288]{1,0:T(8,128)(2,1)} %copy-done.30, f32[8,1024]{1,0:T(8,128)S(1)} %bitcast.186, ...), custom_call_target="tpu_custom_call" | custom-call | flops 724775744 | bytes 884736 | tf_op jit(solution)/shard_map/pallas_call | solution.py:239
  489.5 5.6 shard_map.185
  496.1 10.9 %collective-permute-done.28.come_ref = bf16[512,1152]{1,0:T(8,128)(2,1)} collective-permute-done((bf16[512,1152]{1,0:T(8,128)(2,1)}, bf16[512,1152]{1,0:T(8,128)(2,1)}, u32[]{:S(2)}, u32[]{:S(2)}) %collective-permute-start.28) | collective-permute-done | bytes 1179680 | tf_op jit(solution)/shard_map/ppermute | solution.py:516
  542.3 10.1 %shard_map.188 = (bf16[1024,1152]{1,0:T(8,128)(2,1)S(1)}, f32[1,1152]{1,0:T(1,128)S(1)}, f32[512,1152]{1,0:T(8,128)S(1)}, bf16[512,1152]{1,0:T(8,128)(2,1)}) custom-call(bf16[512,1152]{1,0:T(8,128)(2,1)} %get-tuple-element.200.refs_0_.own_ref, bf16[512,1152]{1,0:T(8,128)(2,1)} %collective-permute-done.29.refs_1_.rec_ref, bf16[1024,1152]{1,0:T(8,128)(2,1)S(1)} %copy-done.48, ...), custom_call_target="tpu_custom_call" | custom-call | flops 543581824 | bytes 1474560 | tf_op jit(solution)/shard_map/pallas_call | solution.py:363
  582.7 14.6 %collective-permute-done.33 = bf16[576,1152]{1,0:T(8,128)(2,1)} collective-permute-done((bf16[576,1152]{1,0:T(8,128)(2,1)}, bf16[576,1152]{1,0:T(8,128)(2,1)}, u32[]{:S(2)}, u32[]{:S(2)}) %collective-permute-start.33) | collective-permute-done | bytes 1327136 | tf_op jit(solution)/shard_map/ppermute | solution.py:538
  622.0 22.2 %shard_map.191 = (bf16[1024,288]{1,0:T(8,128)(2,1)S(1)}, bf16[1024,576]{1,0:T(8,128)(2,1)}) custom-call(s32[1,1024]{1,0:T(1,128)S(1)} %bitcast.189, s32[1024,1]{1,0:T(8,128)S(1)} %copy.212.refs_1_, bf16[1024,864]{1,0:T(8,128)(2,1)} %copy-done.4, bf16[1024,288]{1,0:T(8,128)(2,1)} %copy-done.28, f32[8,1024]{1,0:T(8,128)S(1)} %bitcast.185, ...), custom_call_target="tpu_custom_call" | custom-call | flops 724775744 | bytes 884736 | tf_op jit(solution)/shard_map/pallas_call | solution.py:239
  665.5 10.9 %collective-permute-start.38 = (bf16[256,1152]{1,0:T(8,128)(2,1)}, bf16[256,1152]{1,0:T(8,128)(2,1)S(1)}, u32[]{:S(2)}, u32[]{:S(2)}) collective-permute-start(bf16[256,1152]{1,0:T(8,128)(2,1)} %get-tuple-element.349), channel_id=1, source_target_pairs={{0,8},{8,0},{1,9},{9,1},{2,10},{10,2},{3,11},{11,3},{4,12},{12,4},... | collective-permute-start | bytes 1769480 | tf_op jit(solution)/shard_map/ppermute | solution.py:516
  717.3 14.6 %collective-permute-done.43 = f32[24,1152]{1,0:T(8,128)S(1)} collective-permute-done((f32[24,1152]{1,0:T(8,128)S(1)}, f32[24,1152]{1,0:T(8,128)S(1)}, u32[]{:S(2)}, u32[]{:S(2)}) %collective-permute-start.43) | collective-permute-done | bytes 110624 | tf_op jit(solution)/shard_map/ppermute | solution.py:538
  740.6 30.9 %reduce-scatter.17.cloned.1.call-done = bf16[144,1152]{1,0:T(8,128)(2,1)} async-done(((bf16[576,1152]{1,0:T(8,128)(2,1)}), bf16[144,1152]{1,0:T(8,128)(2,1)}) %reduce-scatter.17.cloned.1.call-update) | async-done | bytes 331792 | tf_op jit(solution)/shard_map/reduce_scatter | solution.py:560
  (616 shorter events, 431.3 us)
Async XLA Ops:
  7.2 101.7 %all-gather.5.cloned.1.call-start = ((), (), s32[]{:S(2)}) async-start(), calls=%async_computation.6 | async-start | bytes 3317760 | tf_op jit(solution)/shard_map/all_gather | solution.py:542
  45.2 152.4 %all-gather.7.cloned.1.call-start = ((), (), s32[]{:S(2)}) async-start(), calls=%async_computation.7 | async-start | bytes 5971968 | tf_op jit(solution)/shard_map/all_gather | solution.py:542
  79.8 174.7 %all-gather.9.cloned.1.call-start = ((), (), s32[]{:S(2)}) async-start(), calls=%async_computation.8 | async-start | bytes 2985984 | tf_op jit(solution)/shard_map/all_gather | solution.py:542
  156.5 206.1 %all-gather.11.cloned.1.call-start = ((), (), s32[]{:S(2)}) async-start(), calls=%async_computation.9 | async-start | bytes 5971968 | tf_op jit(solution)/shard_map/all_gather | solution.py:542
  217.0 262.1 %reduce-scatter.7.cloned.1.call-start = ((), (), s32[]{:S(2)}) async-start(), calls=%async_computation.10 | async-start | bytes 1658880 | tf_op jit(solution)/shard_map/reduce_scatter | solution.py:560
  282.8 34.3 %collective-permute-start.15 = (bf16[512,1152]{1,0:T(8,128)(2,1)S(1)}, bf16[512,1152]{1,0:T(8,128)(2,1)S(1)}, u32[]{:S(2)}, u32[]{:S(2)}) collective-permute-start(bf16[512,1152]{1,0:T(8,128)(2,1)S(1)} %add_convert_fusion.11.q_ref), channel_id=1, source_target_pairs={{0,8},{8,0},{1,9},{9,1},{2,10},{10,2},{3,11},{11,3},{4,12},{12,4},... | collective-permute-start | bytes 3538952 | tf_op jit(solution)/shard_map/ppermute | solution.py:516
  318.4 37.4 %collective-permute-start.17 = (bf16[256,1152]{1,0:T(8,128)(2,1)S(1)}, bf16[256,1152]{1,0:T(8,128)(2,1)S(1)}, u32[]{:S(2)}, u32[]{:S(2)}) collective-permute-start(bf16[256,1152]{1,0:T(8,128)(2,1)S(1)} %fusion.17), channel_id=1, source_target_pairs={{0,8},{8,0},{1,9},{9,1},{2,10},{10,2},{3,11},{11,3},{4,12},{12,4},... | collective-permute-start | bytes 1769480 | tf_op jit(solution)/shard_map/ppermute | solution.py:516
  324.2 38.4 %collective-permute-start.19 = (bf16[512,1152]{1,0:T(8,128)(2,1)}, bf16[512,1152]{1,0:T(8,128)(2,1)}, u32[]{:S(2)}, u32[]{:S(2)}) collective-permute-start(bf16[512,1152]{1,0:T(8,128)(2,1)} %get-tuple-element.156.own_ref.refs_0_), channel_id=1, source_target_pairs={{0,4},{4,0},{1,5},{5,1},{2,6},{6,2},{3,7},{7,3},{8,12},{12,8},{9,1... | collective-permute-start | bytes 3538952 | tf_op jit(solution)/shard_map/ppermute | solution.py:520
  389.9 30.8 %collective-permute-start.22 = (bf16[576,1152]{1,0:T(8,128)(2,1)S(1)}, bf16[576,1152]{1,0:T(8,128)(2,1)S(1)}, u32[]{:S(2)}, u32[]{:S(2)}) collective-permute-start(bf16[576,1152]{1,0:T(8,128)(2,1)S(1)} %get-tuple-element.168), channel_id=1, source_target_pairs={{0,16},{16,0},{1,17},{17,1},{2,18},{18,2},{3,19},{19,3},{4,20},{20... | collective-permute-start | bytes 3981320 | tf_op jit(solution)/shard_map/ppermute | solution.py:538
  431.8 80.6 %reduce-scatter.9.cloned.1.call-start = ((), (), s32[]{:S(2)}) async-start(), calls=%async_computation.11 | async-start | bytes 1658880 | tf_op jit(solution)/shard_map/reduce_scatter | solution.py:560
  432.2 40.9 %collective-permute-start.26 = (bf16[576,1152]{1,0:T(8,128)(2,1)}, bf16[576,1152]{1,0:T(8,128)(2,1)}, u32[]{:S(2)}, u32[]{:S(2)}) collective-permute-start(bf16[576,1152]{1,0:T(8,128)(2,1)} %copy-done.84), channel_id=1, source_target_pairs={{0,16},{16,0},{1,17},{17,1},{2,18},{18,2},{3,19},{19,3},{4,20},{20... | collective-permute-start | bytes 3981320 | tf_op jit(solution)/shard_map/ppermute | solution.py:538
  434.5 36.0 %collective-permute-start.27 = (bf16[256,1152]{1,0:T(8,128)(2,1)}, bf16[256,1152]{1,0:T(8,128)(2,1)}, u32[]{:S(2)}, u32[]{:S(2)}) collective-permute-start(bf16[256,1152]{1,0:T(8,128)(2,1)} %dynamic-slice_bitcast_fusion.5), channel_id=1, source_target_pairs={{0,8},{8,0},{1,9},{9,1},{2,10},{10,2},{3,11},{11,3},{4,12},{12,4},... | collective-permute-start | bytes 1769480 | tf_op jit(solution)/shard_map/ppermute | solution.py:516
  479.1 121.0 %reduce-scatter.11.cloned.1.call-start = ((), (), s32[]{:S(2)}) async-start(), calls=%async_computation.12 | async-start | bytes 1658880 | tf_op jit(solution)/shard_map/reduce_scatter | solution.py:560
  523.8 33.0 %collective-permute-start.31 = (bf16[576,1152]{1,0:T(8,128)(2,1)}, bf16[576,1152]{1,0:T(8,128)(2,1)}, u32[]{:S(2)}, u32[]{:S(2)}) collective-permute-start(bf16[576,1152]{1,0:T(8,128)(2,1)} %get-tuple-element.207), channel_id=1, source_target_pairs={{0,16},{16,0},{1,17},{17,1},{2,18},{18,2},{3,19},{19,3},{4,20},{20... | collective-permute-start | bytes 3981320 | tf_op jit(solution)/shard_map/ppermute | solution.py:538
  562.7 97.2 %reduce-scatter.13.cloned.1.call-start = ((), (), s32[]{:S(2)}) async-start(), calls=%async_computation.13 | async-start | bytes 1658880 | tf_op jit(solution)/shard_map/reduce_scatter | solution.py:560
  566.5 30.9 %collective-permute-start.33 = (bf16[576,1152]{1,0:T(8,128)(2,1)}, bf16[576,1152]{1,0:T(8,128)(2,1)}, u32[]{:S(2)}, u32[]{:S(2)}) collective-permute-start(bf16[576,1152]{1,0:T(8,128)(2,1)} %copy-done.83), channel_id=1, source_target_pairs={{0,16},{16,0},{1,17},{17,1},{2,18},{18,2},{3,19},{19,3},{4,20},{20... | collective-permute-start | bytes 3981320 | tf_op jit(solution)/shard_map/ppermute | solution.py:538
  568.1 31.9 %collective-permute-start.32 = (bf16[512,1152]{1,0:T(8,128)(2,1)}, bf16[512,1152]{1,0:T(8,128)(2,1)}, u32[]{:S(2)}, u32[]{:S(2)}) collective-permute-start(bf16[512,1152]{1,0:T(8,128)(2,1)} %add_convert_fusion.7.q_ref), channel_id=1, source_target_pairs={{0,8},{8,0},{1,9},{9,1},{2,10},{10,2},{3,11},{11,3},{4,12},{12,4},... | collective-permute-start | bytes 3538952 | tf_op jit(solution)/shard_map/ppermute | solution.py:516
  600.1 99.3 %reduce-scatter.15.cloned.1.call-start = ((), (), s32[]{:S(2)}) async-start(), calls=%async_computation.14 | async-start | bytes 1658880 | tf_op jit(solution)/shard_map/reduce_scatter | solution.py:560
  619.2 35.2 %collective-permute-start.39 = (bf16[2,36,3168]{2,0,1:T(2,128)(2,1)S(1)}, bf16[2,36,3168]{2,0,1:T(2,128)(2,1)S(1)}, u32[]{:S(2)}, u32[]{:S(2)}) collective-permute-start(bf16[2,36,3168]{2,0,1:T(2,128)(2,1)S(1)} %bitcast.206), channel_id=1, source_target_pairs={{0,8},{8,0},{1,9},{9,1},{2,10},{10,2},{3,11},{11,3},{4,12},{12,4},... | collective-permute-start | bytes 1368584 | tf_op jit(solution)/shard_map/ppermute | solution.py:516
  621.1 34.2 %collective-permute-start.37 = (bf16[576,1152]{1,0:T(8,128)(2,1)S(1)}, bf16[576,1152]{1,0:T(8,128)(2,1)S(1)}, u32[]{:S(2)}, u32[]{:S(2)}) collective-permute-start(bf16[576,1152]{1,0:T(8,128)(2,1)S(1)} %copy-done.82), channel_id=1, source_target_pairs={{0,16},{16,0},{1,17},{17,1},{2,18},{18,2},{3,19},{19,3},{4,20},{20... | collective-permute-start | bytes 3981320 | tf_op jit(solution)/shard_map/ppermute | solution.py:538
  659.9 111.6 %reduce-scatter.17.cloned.1.call-start = ((), (), s32[]{:S(2)}) async-start(), calls=%async_computation.15 | async-start | bytes 1658880 | tf_op jit(solution)/shard_map/reduce_scatter | solution.py:560
  665.5 30.2 %collective-permute-start.38 = (bf16[256,1152]{1,0:T(8,128)(2,1)}, bf16[256,1152]{1,0:T(8,128)(2,1)S(1)}, u32[]{:S(2)}, u32[]{:S(2)}) collective-permute-start(bf16[256,1152]{1,0:T(8,128)(2,1)} %get-tuple-element.349), channel_id=1, source_target_pairs={{0,8},{8,0},{1,9},{9,1},{2,10},{10,2},{3,11},{11,3},{4,12},{12,4},... | collective-permute-start | bytes 1769480 | tf_op jit(solution)/shard_map/ppermute | solution.py:516
  699.4 33.2 %collective-permute-start.45 = (bf16[576,1152]{1,0:T(8,128)(2,1)}, bf16[576,1152]{1,0:T(8,128)(2,1)}, u32[]{:S(2)}, u32[]{:S(2)}) collective-permute-start(bf16[576,1152]{1,0:T(8,128)(2,1)} %copy-done.80), channel_id=1, source_target_pairs={{0,16},{16,0},{1,17},{17,1},{2,18},{18,2},{3,19},{19,3},{4,20},{20... | collective-permute-start | bytes 3981320 | tf_op jit(solution)/shard_map/ppermute | solution.py:538
  740.6 36.4 %collective-permute-start.48 = (f32[24,1152]{1,0:T(8,128)}, f32[24,1152]{1,0:T(8,128)}, u32[]{:S(2)}, u32[]{:S(2)}) collective-permute-start(f32[24,1152]{1,0:T(8,128)} %add.455), channel_id=1, source_target_pairs={{0,1},{1,0},{2,3},{3,2},{4,5},{5,4},{6,7},{7,6},{8,9},{9,8},{10,11... | collective-permute-start | bytes 331784 | tf_op jit(solution)/shard_map/ppermute | solution.py:538
  (169 other events, 1213.5 us)
Sparse Core Ops, SparseCore 0:
  45.3 63.5 all-gather.4
  111.6 85.9 all-gather.6
  200.2 52.7 all-gather.8
  255.0 103.6 all-gather.10
  431.9 32.6 reduce-scatter.6
  479.2 33.0 reduce-scatter.8
  562.8 28.9 reduce-scatter.10
  600.2 36.5 reduce-scatter.12
  660.0 39.3 reduce-scatter.14
  736.1 35.4 reduce-scatter.16

commit v4 on v3

--- a/solution.py
+++ b/solution.py
@@ -172,9 +172,9 @@
 
 
 def attend_back_kernel(heads, dim, offset, count, first, last, *refs):
-    qid_ref, kid_ref, q_ref, o_ref, total_ref, wo_ref, own_ref, rec_ref = refs[:8]
-    kv_refs = refs[8 : 8 + count]
-    rest = refs[8 + count :]
+    qid_ref, kid_ref, q_ref, total_ref, wo_ref, own_ref, rec_ref = refs[:7]
+    kv_refs = refs[7 : 7 + count]
+    rest = refs[7 + count :]
     if not first:
         before_ref, rest = rest[0], rest[1:]
     dq_ref, dkv_ref, do_ref, acc_ref = rest
@@ -195,7 +195,6 @@
 
     either(own_work, rec_work)
     same = kid_ref[...] == qid_ref[...]
-    ones = jnp.ones((8, dim), bf16)
     dqs = []
     for h in range(heads):
         lo = h * dim
@@ -207,10 +206,8 @@
         s = jnp.where(same, mm_last(k, q), NEGATIVE)
         p = jnp.exp2(s * factor - total_ref[h : h + 1, :])
         dp = mm_last(v, do)
-        both = do.astype(f32) * o_ref[:, lo : lo + dim].astype(f32)
-        high = both.astype(bf16)
-        delta = mm_last(ones, high) + mm_last(ones, (both - high.astype(f32)).astype(bf16))
-        ds = (p * (dp - delta[:1])).astype(bf16)
+        delta = jnp.sum(p * dp, axis=0, keepdims=True)
+        ds = (p * (dp - delta)).astype(bf16)
         acc_ref[heads + h] += mm(p.astype(bf16), do)
         acc_ref[h] += mm(ds, q)
         dqs.append(mm_first(ds, k) * scale)
@@ -227,7 +224,7 @@
 
 
 def attend_back(
-    qkv, kvs, offset, query_ids, key_ids, o, totals, out_full, own, rec, before, last, heads, dim
+    qkv, kvs, offset, query_ids, key_ids, totals, out_full, own, rec, before, last, heads, dim
 ):
     rows, width, wide = qkv.shape[0], heads * dim, out_full.shape[1]
     keys = sum(kv.shape[0] for kv in kvs)
@@ -243,7 +240,6 @@
             pl.BlockSpec((1, block), lambda i: (0, i)),
             const((keys, 1)),
             pl.BlockSpec((block, qkv.shape[1]), lambda i: (i, 0)),
-            pl.BlockSpec((block, width), lambda i: (i, 0)),
             pl.BlockSpec((2 * heads, block), lambda i: (0, i)),
             const(out_full.shape),
             own_spec,
@@ -255,7 +251,7 @@
         scratch_shapes=[pltpu.VMEM((block, width), bf16), pltpu.VMEM(sums, f32)],
         compiler_params=params(52),
         cost_estimate=cost(24 * rows * keys * width, 30 * rows * width, heads * rows * keys),
-    )(query_ids[None, :], key_ids[:, None], qkv, o, totals.T, out_full, own, rec, *kvs, *extra)
+    )(query_ids[None, :], key_ids[:, None], qkv, totals.T, out_full, own, rec, *kvs, *extra)
 
 
 def join_kernel(dq_ref, dkv_ref, w_ref, dqkv_ref, own_ref, rec_ref, sum_ref):
@@ -606,11 +602,11 @@
         spots = (jnp.arange(RANKS) == rank)[None, None, :, None]
         return jnp.where(spots, v, 0.0).reshape(width)
 
-    there = []
+    there, spots = [], (0, 3, 1, 2)
     for b in range(blocks):
         for r in range(RANKS):
             for s in range(seqs):
-                target = (b * RANKS + s % RANKS) * seqs + r * ways + s // RANKS
+                target = (b * RANKS + s % RANKS) * seqs + spots[r] * ways + s // RANKS
                 there.append(((b * RANKS + r) * seqs + s, target))
     back = [(target, source) for source, target in there]
 
@@ -635,23 +631,32 @@
     came = came.reshape(RANKS * held, -1)
     payload = jnp.concatenate([came[:, : 3 * part], out_rows(0), came[:, 3 * part :]], axis=1)
     first = gather_rows(payload)
-    small_full = first[:, width:].T.reshape(layers, kinds, width).astype(f32)
-    qkv_fulls.append((first, first.shape[1], 0))
-    out_fulls.append(first[:, 3 * part : width].reshape(part, width))
     later = [
         ff_columns(piece) for l in range(layers) for piece in (up_weight[l], down_weight[l])
     ] + [rank_columns(qkv_weight[l]) for l in range(1, layers)]
     arrived = lax.ppermute(tokens, AXES, there)
     later, arrived, _ = tie((jnp.concatenate(later, axis=2), arrived, payload))
+    own = mixed_order(arrived)
     later = exchange(later).reshape(RANKS * held, -1)
+    payloads = []
     for l in range(layers):
         if l > 0:
             at = 2 * layers * ff_pad + (l - 1) * 3 * part
-            payload = jnp.concatenate([later[:, at : at + 3 * part], out_rows(l)], axis=1)
-            full = gather_rows(payload)
+            piece = jnp.concatenate([later[:, at : at + 3 * part], out_rows(l)], axis=1)
+            payloads.append(piece)
+        payloads.append(later[:, 2 * l * ff_pad : 2 * (l + 1) * ff_pad])
+    payloads, first, starts = tie((payloads, first, in_order("x", own, swap_x(own))))
+    gathered = iter([gather_rows(v) for v in payloads])
+    unit = jnp.eye(layers * kinds, dtype=bf16)
+    small_full = mm_last(unit, first[:, width:]).reshape(layers, kinds, width)
+    qkv_fulls.append((first, first.shape[1], 0))
+    out_fulls.append(first[:, 3 * part : width].reshape(part, width))
+    for l in range(layers):
+        if l > 0:
+            full = next(gathered)
             qkv_fulls.append((full, width, 0))
             out_fulls.append(full[:, 3 * part :].reshape(part, width))
-        full = gather_rows(later[:, 2 * l * ff_pad : 2 * (l + 1) * ff_pad])
+        full = next(gathered)
         up_fulls.append((full, ff_pad, 0))
         down_fulls.append((full, ff_pad, 1))
     up_shift = pick(up_bias.reshape(layers, RANKS, ff_part), rank, 1).astype(f32)
@@ -701,7 +706,7 @@
         return at_x(qs, xi), swap_x(at_x(qs, 1 - xi))
 
     GAIN1, GAIN2, OFF1, QB, VB, OB, OFF2, DB = range(8)
-    starts = chunks_of(arrived)
+    starts = list(starts) if CHUNKS == 2 else [jnp.concatenate(starts)]
     current = [v.astype(f32) for v in starts]
     normed = [
         (spread(v)[0] * small_full[0, GAIN1] + small_full[0, OFF1]).astype(bf16) for v in current
@@ -765,7 +770,7 @@
         return exchange(jnp.concatenate(pieces, axis=1).reshape(RANKS, held, -1))
 
 
-    waiting, homes = None, [None] * layers
+    waiting, homes = None, {}
     for l in reversed(range(layers)):
         (current, attn_in, qkv, kvs, attended, totals, after, mlp_in, slopes, acts) = saved[l]
         small = small_full[l]
@@ -799,7 +804,8 @@
                 (comes, down_terms, up_terms, waiting, output)
             )
             output = lax.ppermute(output, AXES, back)
-        down_owned = scatter_rows(down_terms)
+        if l > 0:
+            down_owned = scatter_rows(down_terms)
         rounded, mid, sums = [], [], 0.0
         for j in range(CHUNKS):
             g, r, s = norm_back(after[j], qs[j], comes[j], grad[j], small, GAIN2)
@@ -811,8 +817,8 @@
         acc, dqs = None, []
         for j in range(CHUNKS):
             dq, acc = attend_back(
-                qkv[j], kvs, 0 if ways > 1 else part, query_ids[j], key_ids, attended[j],
-                totals[j], out_fulls[l], *out_in[j], acc, j == CHUNKS - 1, heads, dim,
+                qkv[j], kvs, 0 if ways > 1 else part, query_ids[j], key_ids, totals[j],
+                out_fulls[l], *out_in[j], acc, j == CHUNKS - 1, heads, dim,
             )
             dqs.append(dq)
         if ways > 1:
@@ -825,7 +831,7 @@
                 axis_index_groups=seq_groups,
             )
         if not last_layer:
-            dqs, acc, output = tie((dqs, acc, output))
+            dqs, acc, output, down_terms = tie((dqs, acc, output, down_terms))
         dqkvs, qs, sums_qkv = [], [], 0.0
         for j in range(CHUNKS):
             dqkv, own, other, s = join(dqs[j], acc, j, qkv_fulls[l])
@@ -838,9 +844,8 @@
                 (qs, dqkvs, out_in, up_terms, down_owned, output)
             )
         else:
-            qs, dqkvs, out_in, up_terms, down_owned = tie(
-                (qs, dqkvs, out_in, up_terms, down_owned)
-            )
+            down_owned = scatter_rows(down_terms)
+            qs, dqkvs, out_in, up_terms = tie((qs, dqkvs, out_in, up_terms))
         up_owned = scatter_rows(up_terms)
         if l > 0:
             comes = [swap_x(q) for q in qs]
@@ -852,9 +857,12 @@
         ).reshape(width, part)
         waiting = outer([v for pair in attn_in for v in pair], dqkvs, top_bit, out_terms)
         if not last_layer:
+            grads[l + 1], waiting = tie((grads[l + 1], waiting))
             homes[l + 1] = home_of([grads[l + 1][0], grads[l + 1][1], grads[l + 1][2][:, : 3 * part]])
-            comes, homes[l + 1] = tie((comes, homes[l + 1]))
-        comes, waiting, up_owned = tie((comes, waiting, up_owned))
+        if l > 0:
+            comes, waiting, up_owned = tie((comes, waiting, up_owned))
+        else:
+            comes, waiting, down_owned = tie((comes, waiting, down_owned))
         d_next = None
         if l > 0:
             grad, rounded, sums = [], [], 0.0
@@ -900,9 +908,11 @@
             step *= 2
         return v
 
-    both = sum_along(sum_along(sum_along(both, "c"), "x"), "hi")
+    both = sum_along(sum_along(both, "c"), "x")
+    both, grads[0][0] = tie((both, grads[0][0]))
+    both = sum_along(both, "hi")
     mine_last, theirs_last = waiting
-    mine_last, both, tokens_grad = tie((mine_last, both, tokens_grad))
+    mine_last, both, tokens_grad, homes = tie((mine_last, both, tokens_grad, homes))
     last = scatter_rows(halve_rows(mine_last, theirs_last))
     both = sum_along(both, "seq")
     grads[0][2] = last

time: 824 us -> 793 us (0.962)
  waiting for transfers between devices: 236 us -> 278 us
  starting transfers between devices: 115 us -> 80.2 us
  local copies, waits for them, and re-layouts: 171 us -> 144 us
    ppermute x20, starting transfers between devices: 58.7 us -> 21.5 us  [swap_c(): return lax.ppermute(v, 'c', SWAP)]
    all_gather x4, waiting for transfers between devices: 11.3 us -> 37.8 us  [gather_rows(): return lax.all_gather(payload, ('hi', 'seq'), axis=0, tiled=True)]
    unnamed x274 -> x265, local copies, waits for them, and re-layouts: 83.6 us -> 65.4 us
    ppermute x14, waiting for transfers between devices: 99.5 us -> 115 us  [swap_x(): return lax.ppermute(v, 'x', SWAP)]
  transfers between devices with their start and end apart: 60 -> 60, of which waited for: 24 -> 30; matrix products, arithmetic and copies ran while one was open for 19% -> 19% of each run, Pallas kernels for 20% -> 19%
where the time goes in v4:
time: 793 us; the launch traced here: 787 us
  waiting for transfers between devices  278 us (35%)
  Pallas kernels  178 us (22%)
  local copies, waits for them, and re-layouts  144 us (18%)
  starting transfers between devices  80.2 us (10%)
  other arithmetic  75.6 us (10%)
  between operations  16.4 us (2%)
  matrix products  15 us (2%)
    ppermute x14, waiting for transfers between devices, swap_x(): return lax.ppermute(v, 'x', SWAP)  115 us
    unnamed x265, local copies, waits for them, and re-layouts  65.4 us
    ppermute x11, waiting for transfers between devices, flip(): return lax.ppermute(v, axis, [(i, i ^ step) for i in range(size)])  55.7 us
    pallas_call x2, Pallas kernels, attend_back(): pl.pallas_call(functools.partial(attend_back_kernel, heads, dim, offset,...  41.4 us
    all_gather x4, waiting for transfers between devices, gather_rows(): return lax.all_gather(payload, ('hi', 'seq'), axis=0, tiled=True)  37.8 us
    reduce_scatter x6, waiting for transfers between devices, scatter_rows(): return lax.psum_scatter(terms, 'seq', scatter_dimension=0, tiled=True)  32.3 us
    pallas_call x6, Pallas kernels, outer(): pl.pallas_call(functools.partial(outer_kernel, len(lefts), len(rights), l...  30.6 us
    pallas_call x2, Pallas kernels, attend(): pl.pallas_call(functools.partial(attend_kernel, heads, dim, offset, len(k...  25.1 us
  transfers between devices with their start and end apart: 60, of which 30 were waited for; matrix products, arithmetic and copies ran while one was open for 19% of the time, Pallas kernels for 19%

profile of v4, /device:TPU:1, one launch (start us, length us, event | category | flops | bytes accessed | tf_op | source)
XLA Modules:
  0.0 786.9 jit_solution(5033163737273065888)
XLA Ops:
  49.3 14.8 %collective-permute-done.4 = bf16[2,36,5472]{2,0,1:T(2,128)(2,1)S(1)} collective-permute-done((bf16[2,36,5472]{2,0,1:T(2,128)(2,1)S(1)}, bf16[2,36,5472]{2,0,1:T(2,128)(2,1)S(1)}, u32[]{:S(2)}, u32[]{:S(2)}) %collective-permute-start.4) | collective-permute-done | bytes 788000 | tf_op jit(solution)/shard_map/ppermute | solution.py:512
  90.3 12.4 %all-gather.5.cloned.1.call-done.w_ref = bf16[1152,1168]{1,0:T(8,128)(2,1)} async-done(((bf16[144,1168]{1,0:T(8,128)(2,1)}), bf16[1152,1168]{1,0:T(8,128)(2,1)}) %all-gather.5.cloned.1.call-update) | async-done | bytes 2691088 | tf_op jit(solution)/shard_map/all_gather | solution.py:538
  124.6 13.1 %shard_map.170 = (bf16[1024,288]{1,0:T(8,128)(2,1)S(1)}, f32[1024,8]{1,0:T(8,128)S(1)}, f32[512,1152]{1,0:T(8,128)S(1)}, bf16[512,1152]{1,0:T(8,128)(2,1)}) custom-call(s32[1024,1]{1,0:T(8,128)S(1)} %copy-done.33, s32[1,1024]{1,0:T(1,128)S(1)} %bitcast.186, bf16[1024,864]{1,0:T(8,128)(2,1)S(1)} %shard_map.169.refs_2_.refs_4_.refs_7_, ...), custom_call_target="tpu_custom_call" | custom-call | flops 301989888 | bytes 471859 | tf_op jit(solution)/shard_map/pallas_call | solution.py:147
  148.3 26.1 %collective-permute-done.9.come_ref = bf16[512,1152]{1,0:T(8,128)(2,1)S(1)} collective-permute-done((bf16[512,1152]{1,0:T(8,128)(2,1)S(1)}, bf16[512,1152]{1,0:T(8,128)(2,1)S(1)}, u32[]{:S(2)}, u32[]{:S(2)}) %collective-permute-start.9) | collective-permute-done | bytes 1179680 | tf_op jit(solution)/shard_map/ppermute | solution.py:512
  179.8 11.6 %all-gather.7.cloned.1.call-done.up_ref.down_ref = bf16[1152,2304]{1,0:T(8,128)(2,1)} async-done(((bf16[144,2304]{1,0:T(8,128)(2,1)}), bf16[1152,2304]{1,0:T(8,128)(2,1)}) %all-gather.7.cloned.1.call-update) | async-done | bytes 5308432 | tf_op jit(solution)/shard_map/all_gather | solution.py:538
  193.9 10.4 %shard_map.172 = (bf16[1024,1152]{1,0:T(8,128)(2,1)S(1)}, bf16[1024,1152]{1,0:T(8,128)(2,1)S(1)}, f32[512,1152]{1,0:T(8,128)S(1)}, bf16[512,1152]{1,0:T(8,128)(2,1)}) custom-call(bf16[512,1152]{1,0:T(8,128)(2,1)} %get-tuple-element.156.own_ref.refs_0_, bf16[512,1152]{1,0:T(8,128)(2,1)} %collective-permute-done.10.rec_ref.refs_1_, ...), custom_call_target="tpu_custom_call" | custom-call | flops 543581824 | bytes 1710489 | tf_op jit(solution)/shard_map/pallas_call | solution.py:324
  216.3 26.1 %collective-permute-done.12.come_ref = bf16[512,1152]{1,0:T(8,128)(2,1)S(1)} collective-permute-done((bf16[512,1152]{1,0:T(8,128)(2,1)S(1)}, bf16[512,1152]{1,0:T(8,128)(2,1)S(1)}, u32[]{:S(2)}, u32[]{:S(2)}) %collective-permute-start.12) | collective-permute-done | bytes 1179680 | tf_op jit(solution)/shard_map/ppermute | solution.py:512
  257.6 12.0 %shard_map.175 = (bf16[1024,288]{1,0:T(8,128)(2,1)S(1)}, f32[1024,8]{1,0:T(8,128)S(1)}, f32[512,1152]{1,0:T(8,128)S(1)}, bf16[512,1152]{1,0:T(8,128)(2,1)S(1)}) custom-call(s32[1024,1]{1,0:T(8,128)S(1)} %copy-done.34, s32[1,1024]{1,0:T(1,128)S(1)} %bitcast.187, bf16[1024,864]{1,0:T(8,128)(2,1)S(1)} %shard_map.174.refs_2_.refs_4_.refs_7_, ...), custom_call_target="tpu_custom_call" | custom-call | flops 301989888 | bytes 471859 | tf_op jit(solution)/shard_map/pallas_call | solution.py:147
  279.8 20.8 %collective-permute-done.16 = bf16[256,1152]{1,0:T(8,128)(2,1)S(1)} collective-permute-done((bf16[256,1152]{1,0:T(8,128)(2,1)S(1)}, bf16[256,1152]{1,0:T(8,128)(2,1)S(1)}, u32[]{:S(2)}, u32[]{:S(2)}) %collective-permute-start.16) | collective-permute-done | bytes 589856 | tf_op jit(solution)/shard_map/ppermute | solution.py:733
  300.6 12.6 %collective-permute-done.15.come_ref = bf16[512,1152]{1,0:T(8,128)(2,1)S(1)} collective-permute-done((bf16[512,1152]{1,0:T(8,128)(2,1)S(1)}, bf16[512,1152]{1,0:T(8,128)(2,1)S(1)}, u32[]{:S(2)}, u32[]{:S(2)}) %collective-permute-start.15) | collective-permute-done | bytes 1179680 | tf_op jit(solution)/shard_map/ppermute | solution.py:512
  321.6 7.9 %collective-permute-done.17 = bf16[256,1152]{1,0:T(8,128)(2,1)S(1)} collective-permute-done((bf16[256,1152]{1,0:T(8,128)(2,1)S(1)}, bf16[256,1152]{1,0:T(8,128)(2,1)S(1)}, u32[]{:S(2)}, u32[]{:S(2)}) %collective-permute-start.17) | collective-permute-done | bytes 589856 | tf_op jit(solution)/shard_map/ppermute | solution.py:512
  333.4 13.8 %all-gather.11.cloned.1.call-done.up_ref.down_ref = bf16[1152,2304]{1,0:T(8,128)(2,1)} async-done(((bf16[144,2304]{1,0:T(8,128)(2,1)}), bf16[1152,2304]{1,0:T(8,128)(2,1)}) %all-gather.11.cloned.1.call-update) | async-done | bytes 5308432 | tf_op jit(solution)/shard_map/all_gather | solution.py:538
  349.7 9.7 %shard_map.177 = (bf16[1024,1152]{1,0:T(8,128)(2,1)S(1)}, bf16[1024,1152]{1,0:T(8,128)(2,1)S(1)}, f32[512,1152]{1,0:T(8,128)S(1)}, bf16[512,1152]{1,0:T(8,128)(2,1)S(1)}) custom-call(bf16[512,1152]{1,0:T(8,128)(2,1)} %get-tuple-element.171.own_ref.refs_0_, bf16[512,1152]{1,0:T(8,128)(2,1)} %collective-permute-done.19.rec_ref.refs_1_, ...), custom_call_target="tpu_custom_call" | custom-call | flops 543581824 | bytes 1710489 | tf_op jit(solution)/shard_map/pallas_call | solution.py:324
  364.8 9.0 %shard_map.179 = (bf16[1024,1152]{1,0:T(8,128)(2,1)S(1)}, f32[1,1152]{1,0:T(1,128)S(1)}, f32[512,1152]{1,0:T(8,128)S(1)}, bf16[512,1152]{1,0:T(8,128)(2,1)S(1)}) custom-call(bf16[512,1152]{1,0:T(8,128)(2,1)} %get-tuple-element.176.refs_0_.own_ref, bf16[512,1152]{1,0:T(8,128)(2,1)} %collective-permute-done.18.refs_1_.rec_ref, ...), custom_call_target="tpu_custom_call" | custom-call | flops 543581824 | bytes 1474560 | tf_op jit(solution)/shard_map/pallas_call | solution.py:359
  388.9 17.0 %collective-permute-done.22 = bf16[576,1152]{1,0:T(8,128)(2,1)S(1)} collective-permute-done((bf16[576,1152]{1,0:T(8,128)(2,1)S(1)}, bf16[576,1152]{1,0:T(8,128)(2,1)S(1)}, u32[]{:S(2)}, u32[]{:S(2)}) %collective-permute-start.22) | collective-permute-done | bytes 1327136 | tf_op jit(solution)/shard_map/ppermute | solution.py:534
  425.3 20.9 %shard_map.182 = (bf16[1024,288]{1,0:T(8,128)(2,1)S(1)}, bf16[1024,576]{1,0:T(8,128)(2,1)}) custom-call(s32[1,1024]{1,0:T(1,128)S(1)} %bitcast.184, s32[1024,1]{1,0:T(8,128)S(1)} %copy-done.31, bf16[1024,864]{1,0:T(8,128)(2,1)} %copy-done.5, f32[8,1024]{1,0:T(8,128)S(1)} %bitcast.182, bf16[288,1152]{1,0:T(8,128)(2,1)S(1)} %copy-done.20, ...), custom_call_target="tpu_custom_call" | custom-call | flops 724775744 | bytes 884736 | tf_op jit(solution)/shard_map/pallas_call | solution.py:236
  477.7 13.2 %collective-permute-done.28.come_ref = bf16[512,1152]{1,0:T(8,128)(2,1)} collective-permute-done((bf16[512,1152]{1,0:T(8,128)(2,1)}, bf16[512,1152]{1,0:T(8,128)(2,1)}, u32[]{:S(2)}, u32[]{:S(2)}) %collective-permute-start.28) | collective-permute-done | bytes 1179680 | tf_op jit(solution)/shard_map/ppermute | solution.py:512
  514.4 9.7 %shard_map.188 = (bf16[1024,1152]{1,0:T(8,128)(2,1)S(1)}, f32[1,1152]{1,0:T(1,128)S(1)}, f32[512,1152]{1,0:T(8,128)S(1)}, bf16[512,1152]{1,0:T(8,128)(2,1)}) custom-call(bf16[512,1152]{1,0:T(8,128)(2,1)} %get-tuple-element.217.refs_0_.own_ref, bf16[512,1152]{1,0:T(8,128)(2,1)S(1)} %collective-permute-done.29.refs_1_.rec_ref, ...), custom_call_target="tpu_custom_call" | custom-call | flops 543581824 | bytes 1474560 | tf_op jit(solution)/shard_map/pallas_call | solution.py:359
  542.6 6.4 shard_map.189
  550.1 17.6 %collective-permute-done.33 = bf16[576,1152]{1,0:T(8,128)(2,1)} collective-permute-done((bf16[576,1152]{1,0:T(8,128)(2,1)}, bf16[576,1152]{1,0:T(8,128)(2,1)}, u32[]{:S(2)}, u32[]{:S(2)}) %collective-permute-start.33) | collective-permute-done | bytes 1327136 | tf_op jit(solution)/shard_map/ppermute | solution.py:534
  582.8 20.5 %shard_map.191 = (bf16[1024,288]{1,0:T(8,128)(2,1)S(1)}, bf16[1024,576]{1,0:T(8,128)(2,1)}) custom-call(s32[1,1024]{1,0:T(1,128)S(1)} %bitcast.185, s32[1024,1]{1,0:T(8,128)S(1)} %copy-done.32, bf16[1024,864]{1,0:T(8,128)(2,1)} %copy-done.4, f32[8,1024]{1,0:T(8,128)S(1)} %bitcast.181, bf16[288,1152]{1,0:T(8,128)(2,1)S(1)} %reshape.390.refs_3_.refs_4_, ...), custom_call_target="tpu_custom_call" | custom-call | flops 724775744 | bytes 884736 | tf_op jit(solution)/shard_map/pallas_call | solution.py:236
  645.2 6.9 collective-permute-done.43
  686.3 16.6 %collective-permute-done.41 = f32[24,1152]{1,0:T(8,128)S(1)} collective-permute-done((f32[24,1152]{1,0:T(8,128)S(1)}, f32[24,1152]{1,0:T(8,128)S(1)}, u32[]{:S(2)}, u32[]{:S(2)}) %collective-permute-start.41) | collective-permute-done | bytes 110624 | tf_op jit(solution)/shard_map/ppermute | solution.py:534
  713.2 29.1 %reduce-scatter.17.cloned.1.call-done = bf16[144,1152]{1,0:T(8,128)(2,1)} async-done(((bf16[576,1152]{1,0:T(8,128)(2,1)}), bf16[144,1152]{1,0:T(8,128)(2,1)}) %reduce-scatter.17.cloned.1.call-update) | async-done | bytes 331792 | tf_op jit(solution)/shard_map/reduce_scatter | solution.py:556
  (606 shorter events, 412.4 us)
Async XLA Ops:
  7.2 95.5 %all-gather.5.cloned.1.call-start = ((), (), s32[]{:S(2)}) async-start(), calls=%async_computation.6 | async-start | bytes 3317760 | tf_op jit(solution)/shard_map/all_gather | solution.py:538
  44.7 146.6 %all-gather.7.cloned.1.call-start = ((), (), s32[]{:S(2)}) async-start(), calls=%async_computation.7 | async-start | bytes 5971968 | tf_op jit(solution)/shard_map/all_gather | solution.py:538
  47.9 28.9 %collective-permute-start.6 = (bf16[256,1152]{1,0:T(8,128)(2,1)}, bf16[256,1152]{1,0:T(8,128)(2,1)}, u32[]{:S(2)}, u32[]{:S(2)}) collective-permute-start(bf16[256,1152]{1,0:T(8,128)(2,1)} %fusion.16), channel_id=1, source_target_pairs={{0,8},{8,0},{1,9},{9,1},{2,10},{10,2},{3,11},{11,3},{4,12},{12,4},... | collective-permute-start | bytes 1769480 | tf_op jit(solution)/shard_map/ppermute | solution.py:512
  102.8 144.1 %all-gather.9.cloned.1.call-start = ((), (), s32[]{:S(2)}) async-start(), calls=%async_computation.8 | async-start | bytes 2985984 | tf_op jit(solution)/shard_map/all_gather | solution.py:538
  139.5 207.7 %all-gather.11.cloned.1.call-start = ((), (), s32[]{:S(2)}) async-start(), calls=%async_computation.9 | async-start | bytes 5971968 | tf_op jit(solution)/shard_map/all_gather | solution.py:538
  144.2 30.2 %collective-permute-start.9 = (bf16[512,1152]{1,0:T(8,128)(2,1)S(1)}, bf16[512,1152]{1,0:T(8,128)(2,1)S(1)}, u32[]{:S(2)}, u32[]{:S(2)}) collective-permute-start(bf16[512,1152]{1,0:T(8,128)(2,1)S(1)} %add_convert_fusion.13.q_ref), channel_id=1, source_target_pairs={{0,8},{8,0},{1,9},{9,1},{2,10},{10,2},{3,11},{11,3},{4,12},{12,4},... | collective-permute-start | bytes 3538952 | tf_op jit(solution)/shard_map/ppermute | solution.py:512
  210.1 252.5 %reduce-scatter.7.cloned.1.call-start = ((), (), s32[]{:S(2)}) async-start(), calls=%async_computation.10 | async-start | bytes 1658880 | tf_op jit(solution)/shard_map/reduce_scatter | solution.py:556
  274.3 38.9 %collective-permute-start.15 = (bf16[512,1152]{1,0:T(8,128)(2,1)S(1)}, bf16[512,1152]{1,0:T(8,128)(2,1)S(1)}, u32[]{:S(2)}, u32[]{:S(2)}) collective-permute-start(bf16[512,1152]{1,0:T(8,128)(2,1)S(1)} %add_convert_fusion.11.q_ref), channel_id=1, source_target_pairs={{0,8},{8,0},{1,9},{9,1},{2,10},{10,2},{3,11},{11,3},{4,12},{12,4},... | collective-permute-start | bytes 3538952 | tf_op jit(solution)/shard_map/ppermute | solution.py:512
  375.5 30.4 %collective-permute-start.22 = (bf16[576,1152]{1,0:T(8,128)(2,1)S(1)}, bf16[576,1152]{1,0:T(8,128)(2,1)S(1)}, u32[]{:S(2)}, u32[]{:S(2)}) collective-permute-start(bf16[576,1152]{1,0:T(8,128)(2,1)S(1)} %get-tuple-element.184), channel_id=1, source_target_pairs={{0,16},{16,0},{1,17},{17,1},{2,18},{18,2},{3,19},{19,3},{4,20},{20... | collective-permute-start | bytes 3981320 | tf_op jit(solution)/shard_map/ppermute | solution.py:534
  379.1 28.2 %collective-permute-start.21 = (bf16[512,1152]{1,0:T(8,128)(2,1)}, bf16[512,1152]{1,0:T(8,128)(2,1)}, u32[]{:S(2)}, u32[]{:S(2)}) collective-permute-start(bf16[512,1152]{1,0:T(8,128)(2,1)} %add_convert_fusion.10.q_ref), channel_id=1, source_target_pairs={{0,8},{8,0},{1,9},{9,1},{2,10},{10,2},{3,11},{11,3},{4,12},{12,4},... | collective-permute-start | bytes 3538952 | tf_op jit(solution)/shard_map/ppermute | solution.py:512
  417.4 74.7 %reduce-scatter.9.cloned.1.call-start = ((), (), s32[]{:S(2)}) async-start(), calls=%async_computation.11 | async-start | bytes 1658880 | tf_op jit(solution)/shard_map/reduce_scatter | solution.py:556
  417.4 39.8 %collective-permute-start.26 = (bf16[576,1152]{1,0:T(8,128)(2,1)}, bf16[576,1152]{1,0:T(8,128)(2,1)}, u32[]{:S(2)}, u32[]{:S(2)}) collective-permute-start(bf16[576,1152]{1,0:T(8,128)(2,1)} %copy-done.79), channel_id=1, source_target_pairs={{0,16},{16,0},{1,17},{17,1},{2,18},{18,2},{3,19},{19,3},{4,20},{20... | collective-permute-start | bytes 3981320 | tf_op jit(solution)/shard_map/ppermute | solution.py:534
  419.7 34.7 %collective-permute-start.27 = (bf16[256,1152]{1,0:T(8,128)(2,1)}, bf16[256,1152]{1,0:T(8,128)(2,1)}, u32[]{:S(2)}, u32[]{:S(2)}) collective-permute-start(bf16[256,1152]{1,0:T(8,128)(2,1)} %dynamic-slice_bitcast_fusion.5), channel_id=1, source_target_pairs={{0,8},{8,0},{1,9},{9,1},{2,10},{10,2},{3,11},{11,3},{4,12},{12,4},... | collective-permute-start | bytes 1769480 | tf_op jit(solution)/shard_map/ppermute | solution.py:512
  462.7 107.7 %reduce-scatter.11.cloned.1.call-start = ((), (), s32[]{:S(2)}) async-start(), calls=%async_computation.12 | async-start | bytes 1658880 | tf_op jit(solution)/shard_map/reduce_scatter | solution.py:556
  500.2 31.1 %collective-permute-start.31 = (bf16[576,1152]{1,0:T(8,128)(2,1)}, bf16[576,1152]{1,0:T(8,128)(2,1)}, u32[]{:S(2)}, u32[]{:S(2)}) collective-permute-start(bf16[576,1152]{1,0:T(8,128)(2,1)} %get-tuple-element.224), channel_id=1, source_target_pairs={{0,16},{16,0},{1,17},{17,1},{2,18},{18,2},{3,19},{19,3},{4,20},{20... | collective-permute-start | bytes 3981320 | tf_op jit(solution)/shard_map/ppermute | solution.py:534
  537.4 127.3 %reduce-scatter.13.cloned.1.call-start = ((), (), s32[]{:S(2)}) async-start(), calls=%async_computation.13 | async-start | bytes 1658880 | tf_op jit(solution)/shard_map/reduce_scatter | solution.py:556
  537.4 30.3 %collective-permute-start.33 = (bf16[576,1152]{1,0:T(8,128)(2,1)}, bf16[576,1152]{1,0:T(8,128)(2,1)}, u32[]{:S(2)}, u32[]{:S(2)}) collective-permute-start(bf16[576,1152]{1,0:T(8,128)(2,1)} %copy-done.78), channel_id=1, source_target_pairs={{0,16},{16,0},{1,17},{17,1},{2,18},{18,2},{3,19},{19,3},{4,20},{20... | collective-permute-start | bytes 3981320 | tf_op jit(solution)/shard_map/ppermute | solution.py:534
  540.7 29.7 %collective-permute-start.32 = (bf16[512,1152]{1,0:T(8,128)(2,1)}, bf16[512,1152]{1,0:T(8,128)(2,1)}, u32[]{:S(2)}, u32[]{:S(2)}) collective-permute-start(bf16[512,1152]{1,0:T(8,128)(2,1)} %add_convert_fusion.7.q_ref), channel_id=1, source_target_pairs={{0,8},{8,0},{1,9},{9,1},{2,10},{10,2},{3,11},{11,3},{4,12},{12,4},... | collective-permute-start | bytes 3538952 | tf_op jit(solution)/shard_map/ppermute | solution.py:512
  580.4 33.8 %collective-permute-start.37 = (bf16[576,1152]{1,0:T(8,128)(2,1)}, bf16[576,1152]{1,0:T(8,128)(2,1)}, u32[]{:S(2)}, u32[]{:S(2)}) collective-permute-start(bf16[576,1152]{1,0:T(8,128)(2,1)} %get-tuple-element.247), channel_id=1, source_target_pairs={{0,16},{16,0},{1,17},{17,1},{2,18},{18,2},{3,19},{19,3},{4,20},{20... | collective-permute-start | bytes 3981320 | tf_op jit(solution)/shard_map/ppermute | solution.py:534
  612.5 69.9 %reduce-scatter.15.cloned.1.call-start = ((), (), s32[]{:S(2)}) async-start(), calls=%async_computation.14 | async-start | bytes 1658880 | tf_op jit(solution)/shard_map/reduce_scatter | solution.py:556
  645.1 97.1 %reduce-scatter.17.cloned.1.call-start = ((), (), s32[]{:S(2)}) async-start(), calls=%async_computation.15 | async-start | bytes 1658880 | tf_op jit(solution)/shard_map/reduce_scatter | solution.py:556
  671.5 31.5 %collective-permute-start.42 = (bf16[256,1152]{1,0:T(8,128)(2,1)}, bf16[256,1152]{1,0:T(8,128)(2,1)}, u32[]{:S(2)}, u32[]{:S(2)}) collective-permute-start(bf16[256,1152]{1,0:T(8,128)(2,1)} %copy-done.80), channel_id=1, source_target_pairs={{0,0},{4,1},{8,2},{12,3},{3,4},{7,5},{11,6},{15,7},{1,8},{5,9},{9,... | collective-permute-start | bytes 1769480 | tf_op jit(solution)/shard_map/ppermute | solution.py:902
  673.6 29.4 %collective-permute-start.45 = (bf16[576,1152]{1,0:T(8,128)(2,1)}, bf16[576,1152]{1,0:T(8,128)(2,1)}, u32[]{:S(2)}, u32[]{:S(2)}) collective-permute-start(bf16[576,1152]{1,0:T(8,128)(2,1)} %copy-done.77), channel_id=1, source_target_pairs={{0,16},{16,0},{1,17},{17,1},{2,18},{18,2},{3,19},{19,3},{4,20},{20... | collective-permute-start | bytes 3981320 | tf_op jit(solution)/shard_map/ppermute | solution.py:534
  709.4 36.7 %collective-permute-start.48 = (f32[24,1152]{1,0:T(8,128)S(1)}, f32[24,1152]{1,0:T(8,128)}, u32[]{:S(2)}, u32[]{:S(2)}) collective-permute-start(f32[24,1152]{1,0:T(8,128)S(1)} %add.455), channel_id=1, source_target_pairs={{0,1},{1,0},{2,3},{3,2},{4,5},{5,4},{6,7},{7,6},{8,9},{9,8},{10,11... | collective-permute-start | bytes 331784 | tf_op jit(solution)/shard_map/ppermute | solution.py:534
  (164 other events, 1978.1 us)
Sparse Core Ops, SparseCore 0:
  44.9 57.8 all-gather.4
  105.4 85.9 all-gather.6
  194.1 52.7 all-gather.8
  248.8 98.3 all-gather.10
  417.5 29.1 reduce-scatter.6
  462.8 29.2 reduce-scatter.8
  537.5 30.3 reduce-scatter.10
  612.6 35.0 reduce-scatter.12
  650.0 32.3 reduce-scatter.14
  705.9 36.2 reduce-scatter.16

commit v5 on v4

--- a/solution.py
+++ b/solution.py
@@ -631,34 +631,41 @@
     came = came.reshape(RANKS * held, -1)
     payload = jnp.concatenate([came[:, : 3 * part], out_rows(0), came[:, 3 * part :]], axis=1)
     first = gather_rows(payload)
-    later = [
-        ff_columns(piece) for l in range(layers) for piece in (up_weight[l], down_weight[l])
-    ] + [rank_columns(qkv_weight[l]) for l in range(1, layers)]
+    def ff_pieces(weights):
+        return [ff_columns(piece) for piece in weights]
+
+    def pieces_of(weights):
+        return [v for i, w in enumerate(weights) for v in (map(ff_columns, w) if i % 2 == 0 else [rank_columns(w)])]
+
+    def payloads_of(weights, l):
+        sent = exchange(jnp.concatenate(pieces_of(weights), axis=2)).reshape(RANKS * held, -1)
+        payloads, at = [], 0
+        for i in range(len(weights)):
+            if i % 2 == 0:
+                payloads.append(sent[:, at : at + 2 * ff_pad])
+                at += 2 * ff_pad
+            else:
+                l += 1
+                columns = sent[:, at : at + 3 * part]
+                payloads.append(jnp.concatenate([columns, out_rows(l)], axis=1))
+                at += 3 * part
+        return payloads
+
+    order = []
+    for l in range(layers):
+        order += [(up_weight[l], down_weight[l])] + [qkv_weight[i] for i in range(l + 1, min(l + 2, layers))]
     arrived = lax.ppermute(tokens, AXES, there)
-    later, arrived, _ = tie((jnp.concatenate(later, axis=2), arrived, payload))
+    soon, _ = tie((order[:2], payload))
+    soon, arrived = tie((soon, arrived))
+    soon = payloads_of(soon, 0)
     own = mixed_order(arrived)
-    later = exchange(later).reshape(RANKS * held, -1)
-    payloads = []
-    for l in range(layers):
-        if l > 0:
-            at = 2 * layers * ff_pad + (l - 1) * 3 * part
-            piece = jnp.concatenate([later[:, at : at + 3 * part], out_rows(l)], axis=1)
-            payloads.append(piece)
-        payloads.append(later[:, 2 * l * ff_pad : 2 * (l + 1) * ff_pad])
-    payloads, first, starts = tie((payloads, first, in_order("x", own, swap_x(own))))
-    gathered = iter([gather_rows(v) for v in payloads])
+    soon, first, starts = tie((soon, first, in_order("x", own, swap_x(own))))
+    gathered = [gather_rows(v) for v in soon]
+
     unit = jnp.eye(layers * kinds, dtype=bf16)
     small_full = mm_last(unit, first[:, width:]).reshape(layers, kinds, width)
     qkv_fulls.append((first, first.shape[1], 0))
     out_fulls.append(first[:, 3 * part : width].reshape(part, width))
-    for l in range(layers):
-        if l > 0:
-            full = next(gathered)
-            qkv_fulls.append((full, width, 0))
-            out_fulls.append(full[:, 3 * part :].reshape(part, width))
-        full = next(gathered)
-        up_fulls.append((full, ff_pad, 0))
-        down_fulls.append((full, ff_pad, 1))
     up_shift = pick(up_bias.reshape(layers, RANKS, ff_part), rank, 1).astype(f32)
     up_shift = jnp.pad(up_shift, ((0, 0), (0, ff_pad - ff_part)))
 
@@ -714,6 +721,12 @@
     saved = []
     output = None
     for l in range(layers):
+        if l > 0:
+            full = gathered[2 * l - 1]
+            qkv_fulls.append((full, width, 0))
+            out_fulls.append(full[:, 3 * part :].reshape(part, width))
+        up_fulls.append((gathered[2 * l], ff_pad, 0))
+        down_fulls.append((gathered[2 * l], ff_pad, 1))
         small = small_full[l]
         attn_in = [(v, swap_c(v)) for v in normed]
         shift = jnp.concatenate([mine(small[QB]), jnp.zeros((part,), f32), mine(small[VB])])
@@ -731,7 +744,12 @@
             if l == layers - 1 and j == 0:
                 q, cotangent = tie((q, cotangent))
                 arrived = lax.ppermute(cotangent, AXES, there)
+            if l == 0 and j == 0:
+                q, rest = tie((q, order[2:]))
             come = swap_x(q)
+            if l == 0 and j == 0:
+                come, rest = tie((come, payloads_of(rest, 1)))
+                gathered += [gather_rows(v) for v in rest]
             if l == layers - 1 and j == 0:
                 come, arrived = tie((come, arrived))
             u, m = add_norm(current[j], q, come, small, small, (OB, GAIN2, OFF2))

time: 793 us -> 785 us (0.990)
  other arithmetic: 75.6 us -> 55 us
  waiting for transfers between devices: 278 us -> 293 us
    ppermute x14 -> x15, waiting for transfers between devices: 115 us -> 137 us  [swap_x(): return lax.ppermute(v, 'x', SWAP)]
    another operation x9 -> x10, other arithmetic: 18.8 us -> 4.16 us  [exchange(): jnp.stack(in_order('x', pick(blocks, xi), swap_x(pick(blocks, 1 - xi))))]
    unnamed x265 -> x254, local copies, waits for them, and re-layouts: 65.4 us -> 69.3 us
    ppermute x14 -> x15, starting transfers between devices: 23.2 us -> 25.1 us  [swap_x(): return lax.ppermute(v, 'x', SWAP)]
    ppermute x20 -> x21, starting transfers between devices: 21.5 us -> 20.5 us  [swap_c(): return lax.ppermute(v, 'c', SWAP)]
  transfers between devices with their start and end apart: 60 -> 62, of which waited for: 30 -> 31; matrix products, arithmetic and copies ran while one was open for 19% -> 16% of each run, Pallas kernels for 19% -> 19%
where the time goes in v5:
time: 785 us; the launch traced here: 775 us
  waiting for transfers between devices  293 us (37%)
  Pallas kernels  177 us (23%)
  local copies, waits for them, and re-layouts  138 us (18%)
  starting transfers between devices  80.9 us (10%)
  other arithmetic  55 us (7%)
  between operations  16.2 us (2%)
  matrix products  14 us (2%)
    ppermute x15, waiting for transfers between devices, swap_x(): return lax.ppermute(v, 'x', SWAP)  137 us
    unnamed x254, local copies, waits for them, and re-layouts  69.3 us
    ppermute x11, waiting for transfers between devices, flip(): return lax.ppermute(v, axis, [(i, i ^ step) for i in range(size)])  56.1 us
    pallas_call x2, Pallas kernels, attend_back(): pl.pallas_call(functools.partial(attend_back_kernel, heads, dim, offset,...  41.3 us
    all_gather x4, waiting for transfers between devices, gather_rows(): return lax.all_gather(payload, ('hi', 'seq'), axis=0, tiled=True)  34.5 us
    pallas_call x6, Pallas kernels, outer(): pl.pallas_call(functools.partial(outer_kernel, len(lefts), len(rights), l...  30.3 us
    reduce_scatter x6, waiting for transfers between devices, scatter_rows(): return lax.psum_scatter(terms, 'seq', scatter_dimension=0, tiled=True)  29.8 us
    ppermute x15, starting transfers between devices, swap_x(): return lax.ppermute(v, 'x', SWAP)  25.1 us
  transfers between devices with their start and end apart: 62, of which 31 were waited for; matrix products, arithmetic and copies ran while one was open for 16% of the time, Pallas kernels for 19%

profile of v5, /device:TPU:1, one launch (start us, length us, event | category | flops | bytes accessed | tf_op | source)
XLA Modules:
  0.0 774.9 jit_solution(11608704948106289077)
XLA Ops:
  44.2 9.6 %collective-permute-done.4 = bf16[2,36,3168]{2,1,0:T(8,128)(2,1)S(1)} collective-permute-done((bf16[2,36,3168]{2,1,0:T(8,128)(2,1)S(1)}, bf16[2,36,3168]{2,1,0:T(8,128)(2,1)S(1)}, u32[]{:S(2)}, u32[]{:S(2)}) %collective-permute-start.4) | collective-permute-done | bytes 456224 | tf_op jit(solution)/shard_map/ppermute | solution.py:512
  55.4 11.0 %collective-permute-done.6 = bf16[256,1152]{1,0:T(8,128)(2,1)S(1)} collective-permute-done((bf16[256,1152]{1,0:T(8,128)(2,1)S(1)}, bf16[256,1152]{1,0:T(8,128)(2,1)S(1)}, u32[]{:S(2)}, u32[]{:S(2)}) %collective-permute-start.6) | collective-permute-done | bytes 589856 | tf_op jit(solution)/shard_map/ppermute | solution.py:512
  71.0 19.9 %all-gather.5.cloned.1.call-done.w_ref = bf16[1152,1168]{1,0:T(8,128)(2,1)} async-done(((bf16[144,1168]{1,0:T(8,128)(2,1)}), bf16[1152,1168]{1,0:T(8,128)(2,1)}) %all-gather.5.cloned.1.call-update) | async-done | bytes 2691088 | tf_op jit(solution)/shard_map/all_gather | solution.py:538
  113.1 12.0 %shard_map.170 = (bf16[1024,288]{1,0:T(8,128)(2,1)S(1)}, f32[1024,8]{1,0:T(8,128)S(1)}, f32[512,1152]{1,0:T(8,128)S(1)}, bf16[512,1152]{1,0:T(8,128)(2,1)S(1)}) custom-call(s32[1024,1]{1,0:T(8,128)S(1)} %copy-done.36, s32[1,1024]{1,0:T(1,128)S(1)} %bitcast.240, bf16[1024,864]{1,0:T(8,128)(2,1)S(1)} %shard_map.169.refs_2_.refs_4_.refs_7_, ...), custom_call_target="tpu_custom_call" | custom-call | flops 301989888 | bytes 471859 | tf_op jit(solution)/shard_map/pallas_call | solution.py:147
  135.1 8.9 %collective-permute-done.10 = bf16[2,36,2304]{2,1,0:T(8,128)(2,1)S(1)} collective-permute-done((bf16[2,36,2304]{2,1,0:T(8,128)(2,1)S(1)}, bf16[2,36,2304]{2,1,0:T(8,128)(2,1)S(1)}, u32[]{:S(2)}, u32[]{:S(2)}) %collective-permute-start.10) | collective-permute-done | bytes 331808 | tf_op jit(solution)/shard_map/ppermute | solution.py:512
  149.8 23.0 %collective-permute-done.9.come_ref = bf16[512,1152]{1,0:T(8,128)(2,1)} collective-permute-done((bf16[512,1152]{1,0:T(8,128)(2,1)}, bf16[512,1152]{1,0:T(8,128)(2,1)}, u32[]{:S(2)}, u32[]{:S(2)}) %collective-permute-start.9) | collective-permute-done | bytes 1179680 | tf_op jit(solution)/shard_map/ppermute | solution.py:512
  184.0 9.3 %shard_map.172 = (bf16[1024,1152]{1,0:T(8,128)(2,1)S(1)}, bf16[1024,1152]{1,0:T(8,128)(2,1)S(1)}, f32[512,1152]{1,0:T(8,128)S(1)}, bf16[512,1152]{1,0:T(8,128)(2,1)S(1)}) custom-call(bf16[512,1152]{1,0:T(8,128)(2,1)} %get-tuple-element.174.own_ref.refs_0_, bf16[512,1152]{1,0:T(8,128)(2,1)S(1)} %collective-permute-done.12.rec_ref.refs_1_, ...), custom_call_target="tpu_custom_call" | custom-call | flops 543581824 | bytes 1710489 | tf_op jit(solution)/shard_map/pallas_call | solution.py:324
  204.0 25.8 %collective-permute-done.14.come_ref = bf16[512,1152]{1,0:T(8,128)(2,1)S(1)} collective-permute-done((bf16[512,1152]{1,0:T(8,128)(2,1)S(1)}, bf16[512,1152]{1,0:T(8,128)(2,1)S(1)}, u32[]{:S(2)}, u32[]{:S(2)}) %collective-permute-start.14) | collective-permute-done | bytes 1179680 | tf_op jit(solution)/shard_map/ppermute | solution.py:512
  245.7 12.0 %shard_map.175 = (bf16[1024,288]{1,0:T(8,128)(2,1)S(1)}, f32[1024,8]{1,0:T(8,128)S(1)}, f32[512,1152]{1,0:T(8,128)S(1)}, bf16[512,1152]{1,0:T(8,128)(2,1)S(1)}) custom-call(s32[1024,1]{1,0:T(8,128)S(1)} %copy-done.37, s32[1,1024]{1,0:T(1,128)S(1)} %bitcast.241, bf16[1024,864]{1,0:T(8,128)(2,1)S(1)} %shard_map.174.refs_2_.refs_4_.refs_7_, ...), custom_call_target="tpu_custom_call" | custom-call | flops 301989888 | bytes 471859 | tf_op jit(solution)/shard_map/pallas_call | solution.py:147
  267.8 21.0 %collective-permute-done.18 = bf16[256,1152]{1,0:T(8,128)(2,1)S(1)} collective-permute-done((bf16[256,1152]{1,0:T(8,128)(2,1)S(1)}, bf16[256,1152]{1,0:T(8,128)(2,1)S(1)}, u32[]{:S(2)}, u32[]{:S(2)}) %collective-permute-start.18) | collective-permute-done | bytes 589856 | tf_op jit(solution)/shard_map/ppermute | solution.py:746
  288.8 12.6 %collective-permute-done.17.come_ref = bf16[512,1152]{1,0:T(8,128)(2,1)S(1)} collective-permute-done((bf16[512,1152]{1,0:T(8,128)(2,1)S(1)}, bf16[512,1152]{1,0:T(8,128)(2,1)S(1)}, u32[]{:S(2)}, u32[]{:S(2)}) %collective-permute-start.17) | collective-permute-done | bytes 1179680 | tf_op jit(solution)/shard_map/ppermute | solution.py:512
  321.6 13.8 %all-gather.11.cloned.1.call-done.up_ref.down_ref = bf16[1152,2304]{1,0:T(8,128)(2,1)} async-done(((bf16[144,2304]{1,0:T(8,128)(2,1)}), bf16[1152,2304]{1,0:T(8,128)(2,1)}) %all-gather.11.cloned.1.call-update) | async-done | bytes 5308432 | tf_op jit(solution)/shard_map/all_gather | solution.py:538
  337.9 9.7 %shard_map.177 = (bf16[1024,1152]{1,0:T(8,128)(2,1)S(1)}, bf16[1024,1152]{1,0:T(8,128)(2,1)S(1)}, f32[512,1152]{1,0:T(8,128)S(1)}, bf16[512,1152]{1,0:T(8,128)(2,1)S(1)}) custom-call(bf16[512,1152]{1,0:T(8,128)(2,1)} %get-tuple-element.189.own_ref.refs_0_, bf16[512,1152]{1,0:T(8,128)(2,1)} %collective-permute-done.21.rec_ref.refs_1_, ...), custom_call_target="tpu_custom_call" | custom-call | flops 543581824 | bytes 1710489 | tf_op jit(solution)/shard_map/pallas_call | solution.py:324
  352.8 9.4 %shard_map.179 = (bf16[1024,1152]{1,0:T(8,128)(2,1)S(1)}, f32[1,1152]{1,0:T(1,128)S(1)}, f32[512,1152]{1,0:T(8,128)S(1)}, bf16[512,1152]{1,0:T(8,128)(2,1)S(1)}) custom-call(bf16[512,1152]{1,0:T(8,128)(2,1)} %get-tuple-element.194.refs_0_.own_ref, bf16[512,1152]{1,0:T(8,128)(2,1)} %collective-permute-done.20.refs_1_.rec_ref, ...), custom_call_target="tpu_custom_call" | custom-call | flops 543581824 | bytes 1474560 | tf_op jit(solution)/shard_map/pallas_call | solution.py:359
  377.3 17.0 %collective-permute-done.24 = bf16[576,1152]{1,0:T(8,128)(2,1)S(1)} collective-permute-done((bf16[576,1152]{1,0:T(8,128)(2,1)S(1)}, bf16[576,1152]{1,0:T(8,128)(2,1)S(1)}, u32[]{:S(2)}, u32[]{:S(2)}) %collective-permute-start.24) | collective-permute-done | bytes 1327136 | tf_op jit(solution)/shard_map/ppermute | solution.py:534
  413.7 20.7 %shard_map.182 = (bf16[1024,288]{1,0:T(8,128)(2,1)S(1)}, bf16[1024,576]{1,0:T(8,128)(2,1)}) custom-call(s32[1,1024]{1,0:T(1,128)S(1)} %bitcast.238, s32[1024,1]{1,0:T(8,128)S(1)} %copy-done.34, bf16[1024,864]{1,0:T(8,128)(2,1)} %copy-done.5, f32[8,1024]{1,0:T(8,128)S(1)} %bitcast.236, bf16[288,1152]{1,0:T(8,128)(2,1)S(1)} %copy-done.21, ...), custom_call_target="tpu_custom_call" | custom-call | flops 724775744 | bytes 884736 | tf_op jit(solution)/shard_map/pallas_call | solution.py:236
  465.6 12.8 %collective-permute-done.30.come_ref = bf16[512,1152]{1,0:T(8,128)(2,1)} collective-permute-done((bf16[512,1152]{1,0:T(8,128)(2,1)}, bf16[512,1152]{1,0:T(8,128)(2,1)}, u32[]{:S(2)}, u32[]{:S(2)}) %collective-permute-start.30) | collective-permute-done | bytes 1179680 | tf_op jit(solution)/shard_map/ppermute | solution.py:512
  502.5 9.7 %shard_map.188 = (bf16[1024,1152]{1,0:T(8,128)(2,1)S(1)}, f32[1,1152]{1,0:T(1,128)S(1)}, f32[512,1152]{1,0:T(8,128)S(1)}, bf16[512,1152]{1,0:T(8,128)(2,1)}) custom-call(bf16[512,1152]{1,0:T(8,128)(2,1)} %get-tuple-element.235.refs_0_.own_ref, bf16[512,1152]{1,0:T(8,128)(2,1)S(1)} %collective-permute-done.31.refs_1_.rec_ref, ...), custom_call_target="tpu_custom_call" | custom-call | flops 543581824 | bytes 1474560 | tf_op jit(solution)/shard_map/pallas_call | solution.py:359
  538.9 16.3 %collective-permute-done.35 = bf16[576,1152]{1,0:T(8,128)(2,1)} collective-permute-done((bf16[576,1152]{1,0:T(8,128)(2,1)}, bf16[576,1152]{1,0:T(8,128)(2,1)}, u32[]{:S(2)}, u32[]{:S(2)}) %collective-permute-start.35) | collective-permute-done | bytes 1327136 | tf_op jit(solution)/shard_map/ppermute | solution.py:534
  570.1 20.6 %shard_map.191 = (bf16[1024,288]{1,0:T(8,128)(2,1)S(1)}, bf16[1024,576]{1,0:T(8,128)(2,1)}) custom-call(s32[1,1024]{1,0:T(1,128)S(1)} %bitcast.239, s32[1024,1]{1,0:T(8,128)S(1)} %copy-done.35, bf16[1024,864]{1,0:T(8,128)(2,1)} %copy-done.4, f32[8,1024]{1,0:T(8,128)S(1)} %bitcast.235, bf16[288,1152]{1,0:T(8,128)(2,1)S(1)} %reshape.409.refs_3_.refs_4_, ...), custom_call_target="tpu_custom_call" | custom-call | flops 724775744 | bytes 884736 | tf_op jit(solution)/shard_map/pallas_call | solution.py:236
  633.9 7.9 %collective-permute-done.45 = bf16[2,36,3168]{2,1,0:T(8,128)(2,1)} collective-permute-done((bf16[2,36,3168]{2,1,0:T(8,128)(2,1)}, bf16[2,36,3168]{2,1,0:T(8,128)(2,1)}, u32[]{:S(2)}, u32[]{:S(2)}) %collective-permute-start.45) | collective-permute-done | bytes 456224 | tf_op jit(solution)/shard_map/ppermute | solution.py:512
  646.0 8.5 %collective-permute-done.40.come_ref = bf16[256,1152]{1,0:T(8,128)(2,1)} collective-permute-done((bf16[256,1152]{1,0:T(8,128)(2,1)}, bf16[256,1152]{1,0:T(8,128)(2,1)}, u32[]{:S(2)}, u32[]{:S(2)}) %collective-permute-start.40) | collective-permute-done | bytes 589856 | tf_op jit(solution)/shard_map/ppermute | solution.py:512
  674.6 18.3 %collective-permute-done.43 = f32[24,1152]{1,0:T(8,128)S(1)} collective-permute-done((f32[24,1152]{1,0:T(8,128)S(1)}, f32[24,1152]{1,0:T(8,128)S(1)}, u32[]{:S(2)}, u32[]{:S(2)}) %collective-permute-start.43) | collective-permute-done | bytes 110624 | tf_op jit(solution)/shard_map/ppermute | solution.py:534
  704.7 28.1 %reduce-scatter.17.cloned.1.call-done = bf16[144,1152]{1,0:T(8,128)(2,1)} async-done(((bf16[576,1152]{1,0:T(8,128)(2,1)}), bf16[144,1152]{1,0:T(8,128)(2,1)}) %reduce-scatter.17.cloned.1.call-update) | async-done | bytes 331792 | tf_op jit(solution)/shard_map/reduce_scatter | solution.py:556
  (614 shorter events, 400.8 us)
Async XLA Ops:
  7.2 83.7 %all-gather.5.cloned.1.call-start = ((), (), s32[]{:S(2)}) async-start(), calls=%async_computation.6 | async-start | bytes 3317760 | tf_op jit(solution)/shard_map/all_gather | solution.py:538
  7.2 28.1 %collective-permute-start.3 = (bf16[256,1152]{1,0:T(8,128)(2,1)}, bf16[256,1152]{1,0:T(8,128)(2,1)S(1)}, u32[]{:S(2)}, u32[]{:S(2)}) collective-permute-start(bf16[256,1152]{1,0:T(8,128)(2,1)} %param.10), channel_id=1, source_target_pairs={{0,0},{1,4},{2,8},{3,12},{4,3},{5,7},{6,11},{7,15},{8,1},{9,5},{10... | collective-permute-start | bytes 1769480 | tf_op jit(solution)/shard_map/ppermute | solution.py:657
  35.0 146.1 %all-gather.7.cloned.1.call-start = ((), (), s32[]{:S(2)}) async-start(), calls=%async_computation.7 | async-start | bytes 5971968 | tf_op jit(solution)/shard_map/all_gather | solution.py:538
  90.9 144.2 %all-gather.9.cloned.1.call-start = ((), (), s32[]{:S(2)}) async-start(), calls=%async_computation.8 | async-start | bytes 2985984 | tf_op jit(solution)/shard_map/all_gather | solution.py:538
  135.1 200.3 %all-gather.11.cloned.1.call-start = ((), (), s32[]{:S(2)}) async-start(), calls=%async_computation.9 | async-start | bytes 5971968 | tf_op jit(solution)/shard_map/all_gather | solution.py:538
  144.8 28.0 %collective-permute-start.9 = (bf16[512,1152]{1,0:T(8,128)(2,1)}, bf16[512,1152]{1,0:T(8,128)(2,1)}, u32[]{:S(2)}, u32[]{:S(2)}) collective-permute-start(bf16[512,1152]{1,0:T(8,128)(2,1)} %add_convert_fusion.13.q_ref), channel_id=1, source_target_pairs={{0,8},{8,0},{1,9},{9,1},{2,10},{10,2},{3,11},{11,3},{4,12},{12,4},... | collective-permute-start | bytes 3538952 | tf_op jit(solution)/shard_map/ppermute | solution.py:512
  198.0 252.4 %reduce-scatter.7.cloned.1.call-start = ((), (), s32[]{:S(2)}) async-start(), calls=%async_computation.10 | async-start | bytes 1658880 | tf_op jit(solution)/shard_map/reduce_scatter | solution.py:556
  262.5 38.9 %collective-permute-start.17 = (bf16[512,1152]{1,0:T(8,128)(2,1)S(1)}, bf16[512,1152]{1,0:T(8,128)(2,1)S(1)}, u32[]{:S(2)}, u32[]{:S(2)}) collective-permute-start(bf16[512,1152]{1,0:T(8,128)(2,1)S(1)} %add_convert_fusion.11.q_ref), channel_id=1, source_target_pairs={{0,8},{8,0},{1,9},{9,1},{2,10},{10,2},{3,11},{11,3},{4,12},{12,4},... | collective-permute-start | bytes 3538952 | tf_op jit(solution)/shard_map/ppermute | solution.py:512
  363.9 30.4 %collective-permute-start.24 = (bf16[576,1152]{1,0:T(8,128)(2,1)S(1)}, bf16[576,1152]{1,0:T(8,128)(2,1)S(1)}, u32[]{:S(2)}, u32[]{:S(2)}) collective-permute-start(bf16[576,1152]{1,0:T(8,128)(2,1)S(1)} %get-tuple-element.202), channel_id=1, source_target_pairs={{0,16},{16,0},{1,17},{17,1},{2,18},{18,2},{3,19},{19,3},{4,20},{20... | collective-permute-start | bytes 3981320 | tf_op jit(solution)/shard_map/ppermute | solution.py:534
  367.5 28.1 %collective-permute-start.23 = (bf16[512,1152]{1,0:T(8,128)(2,1)}, bf16[512,1152]{1,0:T(8,128)(2,1)}, u32[]{:S(2)}, u32[]{:S(2)}) collective-permute-start(bf16[512,1152]{1,0:T(8,128)(2,1)} %add_convert_fusion.10.q_ref), channel_id=1, source_target_pairs={{0,8},{8,0},{1,9},{9,1},{2,10},{10,2},{3,11},{11,3},{4,12},{12,4},... | collective-permute-start | bytes 3538952 | tf_op jit(solution)/shard_map/ppermute | solution.py:512
  405.8 74.3 %reduce-scatter.9.cloned.1.call-start = ((), (), s32[]{:S(2)}) async-start(), calls=%async_computation.11 | async-start | bytes 1658880 | tf_op jit(solution)/shard_map/reduce_scatter | solution.py:556
  405.8 39.3 %collective-permute-start.28 = (bf16[576,1152]{1,0:T(8,128)(2,1)}, bf16[576,1152]{1,0:T(8,128)(2,1)}, u32[]{:S(2)}, u32[]{:S(2)}) collective-permute-start(bf16[576,1152]{1,0:T(8,128)(2,1)} %copy-done.82), channel_id=1, source_target_pairs={{0,16},{16,0},{1,17},{17,1},{2,18},{18,2},{3,19},{19,3},{4,20},{20... | collective-permute-start | bytes 3981320 | tf_op jit(solution)/shard_map/ppermute | solution.py:534
  408.1 34.5 %collective-permute-start.29 = (bf16[256,1152]{1,0:T(8,128)(2,1)}, bf16[256,1152]{1,0:T(8,128)(2,1)}, u32[]{:S(2)}, u32[]{:S(2)}) collective-permute-start(bf16[256,1152]{1,0:T(8,128)(2,1)} %dynamic-slice_bitcast_fusion.4), channel_id=1, source_target_pairs={{0,8},{8,0},{1,9},{9,1},{2,10},{10,2},{3,11},{11,3},{4,12},{12,4},... | collective-permute-start | bytes 1769480 | tf_op jit(solution)/shard_map/ppermute | solution.py:512
  450.5 107.5 %reduce-scatter.11.cloned.1.call-start = ((), (), s32[]{:S(2)}) async-start(), calls=%async_computation.12 | async-start | bytes 1658880 | tf_op jit(solution)/shard_map/reduce_scatter | solution.py:556
  488.1 31.1 %collective-permute-start.33 = (bf16[576,1152]{1,0:T(8,128)(2,1)}, bf16[576,1152]{1,0:T(8,128)(2,1)}, u32[]{:S(2)}, u32[]{:S(2)}) collective-permute-start(bf16[576,1152]{1,0:T(8,128)(2,1)} %get-tuple-element.242), channel_id=1, source_target_pairs={{0,16},{16,0},{1,17},{17,1},{2,18},{18,2},{3,19},{19,3},{4,20},{20... | collective-permute-start | bytes 3981320 | tf_op jit(solution)/shard_map/ppermute | solution.py:534
  524.8 129.6 %reduce-scatter.13.cloned.1.call-start = ((), (), s32[]{:S(2)}) async-start(), calls=%async_computation.13 | async-start | bytes 1658880 | tf_op jit(solution)/shard_map/reduce_scatter | solution.py:556
  524.9 30.3 %collective-permute-start.35 = (bf16[576,1152]{1,0:T(8,128)(2,1)}, bf16[576,1152]{1,0:T(8,128)(2,1)}, u32[]{:S(2)}, u32[]{:S(2)}) collective-permute-start(bf16[576,1152]{1,0:T(8,128)(2,1)} %copy-done.81), channel_id=1, source_target_pairs={{0,16},{16,0},{1,17},{17,1},{2,18},{18,2},{3,19},{19,3},{4,20},{20... | collective-permute-start | bytes 3981320 | tf_op jit(solution)/shard_map/ppermute | solution.py:534
  528.2 29.7 %collective-permute-start.34 = (bf16[512,1152]{1,0:T(8,128)(2,1)}, bf16[512,1152]{1,0:T(8,128)(2,1)}, u32[]{:S(2)}, u32[]{:S(2)}) collective-permute-start(bf16[512,1152]{1,0:T(8,128)(2,1)} %add_convert_fusion.7.q_ref), channel_id=1, source_target_pairs={{0,8},{8,0},{1,9},{9,1},{2,10},{10,2},{3,11},{11,3},{4,12},{12,4},... | collective-permute-start | bytes 3538952 | tf_op jit(solution)/shard_map/ppermute | solution.py:512
  567.7 33.8 %collective-permute-start.39 = (bf16[576,1152]{1,0:T(8,128)(2,1)}, bf16[576,1152]{1,0:T(8,128)(2,1)}, u32[]{:S(2)}, u32[]{:S(2)}) collective-permute-start(bf16[576,1152]{1,0:T(8,128)(2,1)} %get-tuple-element.265), channel_id=1, source_target_pairs={{0,16},{16,0},{1,17},{17,1},{2,18},{18,2},{3,19},{19,3},{4,20},{20... | collective-permute-start | bytes 3981320 | tf_op jit(solution)/shard_map/ppermute | solution.py:534
  599.9 70.6 %reduce-scatter.15.cloned.1.call-start = ((), (), s32[]{:S(2)}) async-start(), calls=%async_computation.14 | async-start | bytes 1658880 | tf_op jit(solution)/shard_map/reduce_scatter | solution.py:556
  633.9 98.9 %reduce-scatter.17.cloned.1.call-start = ((), (), s32[]{:S(2)}) async-start(), calls=%async_computation.15 | async-start | bytes 1658880 | tf_op jit(solution)/shard_map/reduce_scatter | solution.py:556
  661.3 31.7 %collective-permute-start.44 = (bf16[256,1152]{1,0:T(8,128)(2,1)}, bf16[256,1152]{1,0:T(8,128)(2,1)}, u32[]{:S(2)}, u32[]{:S(2)}) collective-permute-start(bf16[256,1152]{1,0:T(8,128)(2,1)} %copy-done.83), channel_id=1, source_target_pairs={{0,0},{4,1},{8,2},{12,3},{3,4},{7,5},{11,6},{15,7},{1,8},{5,9},{9,... | collective-permute-start | bytes 1769480 | tf_op jit(solution)/shard_map/ppermute | solution.py:920
  663.6 29.3 %collective-permute-start.47 = (bf16[576,1152]{1,0:T(8,128)(2,1)}, bf16[576,1152]{1,0:T(8,128)(2,1)}, u32[]{:S(2)}, u32[]{:S(2)}) collective-permute-start(bf16[576,1152]{1,0:T(8,128)(2,1)} %copy-done.80), channel_id=1, source_target_pairs={{0,16},{16,0},{1,17},{17,1},{2,18},{18,2},{3,19},{19,3},{4,20},{20... | collective-permute-start | bytes 3981320 | tf_op jit(solution)/shard_map/ppermute | solution.py:534
  701.0 36.1 %collective-permute-start.50 = (f32[24,1152]{1,0:T(8,128)S(1)}, f32[24,1152]{1,0:T(8,128)S(1)}, u32[]{:S(2)}, u32[]{:S(2)}) collective-permute-start(f32[24,1152]{1,0:T(8,128)S(1)} %add.459), channel_id=1, source_target_pairs={{0,1},{1,0},{2,3},{3,2},{4,5},{5,4},{6,7},{7,6},{8,9},{9,8},{10,11... | collective-permute-start | bytes 331784 | tf_op jit(solution)/shard_map/ppermute | solution.py:534
  (161 other events, 1918.6 us)
Sparse Core Ops, SparseCore 0:
  35.1 55.7 all-gather.4
  93.6 85.9 all-gather.6
  182.2 52.7 all-gather.8
  237.0 98.3 all-gather.10
  405.9 29.1 reduce-scatter.6
  450.6 29.3 reduce-scatter.8
  525.0 30.3 reduce-scatter.10
  600.0 35.1 reduce-scatter.12
  637.5 30.5 reduce-scatter.14
  695.8 36.9 reduce-scatter.16

commit v6 on v5

--- a/solution.py
+++ b/solution.py
@@ -729,6 +729,9 @@
         down_fulls.append((gathered[2 * l], ff_pad, 1))
         small = small_full[l]
         attn_in = [(v, swap_c(v)) for v in normed]
+        if l == layers - 1:
+            attn_in, cotangent = tie((attn_in, cotangent))
+            arrived = lax.ppermute(cotangent, AXES, there)
         shift = jnp.concatenate([mine(small[QB]), jnp.zeros((part,), f32), mine(small[VB])])
         qkv = [project(own, rec, qkv_fulls[l], shift) for own, rec in attn_in]
         kvs = [keys_of(v) for v in qkv]
@@ -738,12 +741,11 @@
             o, total, own, other = attend(
                 qkv[j], kvs, offset, query_ids[j], key_ids, out_fulls[l], heads, dim
             )
+            if l == layers - 1 and j == 0:
+                o, total, own, other, arrived = tie((o, total, own, other, arrived))
             attended.append(o)
             totals.append(total)
             q = core_sum(own, other)
-            if l == layers - 1 and j == 0:
-                q, cotangent = tie((q, cotangent))
-                arrived = lax.ppermute(cotangent, AXES, there)
             if l == 0 and j == 0:
                 q, rest = tie((q, order[2:]))
             come = swap_x(q)

time: 785 us -> 784 us (level)
    ppermute x15, waiting for transfers between devices: 137 us -> 153 us  [swap_x(): return lax.ppermute(v, 'x', SWAP)]
    all_gather x4, waiting for transfers between devices: 34.5 us -> 23.2 us  [gather_rows(): return lax.all_gather(payload, ('hi', 'seq'), axis=0, tiled=True)]
    unnamed x254 -> x264, local copies, waits for them, and re-layouts: 69.3 us -> 76.6 us
  transfers between devices with their start and end apart: 62 -> 62, of which waited for: 31 -> 31; matrix products, arithmetic and copies ran while one was open for 16% -> 17% of each run, Pallas kernels for 19% -> 19%
where the time goes in v6:
time: 784 us; the launch traced here: 774 us
  waiting for transfers between devices  295 us (38%)
  Pallas kernels  173 us (22%)
  local copies, waits for them, and re-layouts  145 us (18%)
  starting transfers between devices  73.8 us (9%)
  other arithmetic  55.1 us (7%)
  between operations  16.3 us (2%)
  matrix products  15 us (2%)
    ppermute x15, waiting for transfers between devices, swap_x(): return lax.ppermute(v, 'x', SWAP)  153 us
    unnamed x264, local copies, waits for them, and re-layouts  76.6 us
    ppermute x11, waiting for transfers between devices, flip(): return lax.ppermute(v, axis, [(i, i ^ step) for i in range(size)])  56.2 us
    pallas_call x2, Pallas kernels, attend_back(): pl.pallas_call(functools.partial(attend_back_kernel, heads, dim, offset,...  41.4 us
    reduce_scatter x6, waiting for transfers between devices, scatter_rows(): return lax.psum_scatter(terms, 'seq', scatter_dimension=0, tiled=True)  29.7 us
    pallas_call x6, Pallas kernels, outer(): pl.pallas_call(functools.partial(outer_kernel, len(lefts), len(rights), l...  28.5 us
    pallas_call x2, Pallas kernels, attend(): pl.pallas_call(functools.partial(attend_kernel, heads, dim, offset, len(k...  24.1 us
    all_gather x4, waiting for transfers between devices, gather_rows(): return lax.all_gather(payload, ('hi', 'seq'), axis=0, tiled=True)  23.2 us
  transfers between devices with their start and end apart: 62, of which 31 were waited for; matrix products, arithmetic and copies ran while one was open for 17% of the time, Pallas kernels for 19%

profile of v6, /device:TPU:1, one launch (start us, length us, event | category | flops | bytes accessed | tf_op | source)
XLA Modules:
  0.0 773.8 jit_solution(6588390278059063873)
XLA Ops:
  44.2 9.6 %collective-permute-done.4 = bf16[2,36,3168]{2,1,0:T(8,128)(2,1)S(1)} collective-permute-done((bf16[2,36,3168]{2,1,0:T(8,128)(2,1)S(1)}, bf16[2,36,3168]{2,1,0:T(8,128)(2,1)S(1)}, u32[]{:S(2)}, u32[]{:S(2)}) %collective-permute-start.4) | collective-permute-done | bytes 456224 | tf_op jit(solution)/shard_map/ppermute | solution.py:512
  55.4 11.0 %collective-permute-done.6 = bf16[256,1152]{1,0:T(8,128)(2,1)S(1)} collective-permute-done((bf16[256,1152]{1,0:T(8,128)(2,1)S(1)}, bf16[256,1152]{1,0:T(8,128)(2,1)S(1)}, u32[]{:S(2)}, u32[]{:S(2)}) %collective-permute-start.6) | collective-permute-done | bytes 589856 | tf_op jit(solution)/shard_map/ppermute | solution.py:512
  71.0 19.9 %all-gather.5.cloned.1.call-done.w_ref = bf16[1152,1168]{1,0:T(8,128)(2,1)} async-done(((bf16[144,1168]{1,0:T(8,128)(2,1)}), bf16[1152,1168]{1,0:T(8,128)(2,1)}) %all-gather.5.cloned.1.call-update) | async-done | bytes 2691088 | tf_op jit(solution)/shard_map/all_gather | solution.py:538
  113.1 12.0 %shard_map.170 = (bf16[1024,288]{1,0:T(8,128)(2,1)S(1)}, f32[1024,8]{1,0:T(8,128)S(1)}, f32[512,1152]{1,0:T(8,128)S(1)}, bf16[512,1152]{1,0:T(8,128)(2,1)S(1)}) custom-call(s32[1024,1]{1,0:T(8,128)S(1)} %copy-done.42, s32[1,1024]{1,0:T(1,128)S(1)} %bitcast.240, bf16[1024,864]{1,0:T(8,128)(2,1)S(1)} %shard_map.169.refs_2_.refs_4_.refs_7_, ...), custom_call_target="tpu_custom_call" | custom-call | flops 301989888 | bytes 471859 | tf_op jit(solution)/shard_map/pallas_call | solution.py:147
  135.1 8.9 %collective-permute-done.10 = bf16[2,36,2304]{2,1,0:T(8,128)(2,1)S(1)} collective-permute-done((bf16[2,36,2304]{2,1,0:T(8,128)(2,1)S(1)}, bf16[2,36,2304]{2,1,0:T(8,128)(2,1)S(1)}, u32[]{:S(2)}, u32[]{:S(2)}) %collective-permute-start.10) | collective-permute-done | bytes 331808 | tf_op jit(solution)/shard_map/ppermute | solution.py:512
  149.8 23.0 %collective-permute-done.9.come_ref = bf16[512,1152]{1,0:T(8,128)(2,1)} collective-permute-done((bf16[512,1152]{1,0:T(8,128)(2,1)}, bf16[512,1152]{1,0:T(8,128)(2,1)}, u32[]{:S(2)}, u32[]{:S(2)}) %collective-permute-start.9) | collective-permute-done | bytes 1179680 | tf_op jit(solution)/shard_map/ppermute | solution.py:512
  184.0 9.3 %shard_map.172 = (bf16[1024,1152]{1,0:T(8,128)(2,1)S(1)}, bf16[1024,1152]{1,0:T(8,128)(2,1)S(1)}, f32[512,1152]{1,0:T(8,128)S(1)}, bf16[512,1152]{1,0:T(8,128)(2,1)S(1)}) custom-call(bf16[512,1152]{1,0:T(8,128)(2,1)} %get-tuple-element.180.own_ref.refs_0_, bf16[512,1152]{1,0:T(8,128)(2,1)S(1)} %collective-permute-done.12.rec_ref.refs_1_, ...), custom_call_target="tpu_custom_call" | custom-call | flops 543581824 | bytes 1710489 | tf_op jit(solution)/shard_map/pallas_call | solution.py:324
  204.1 25.8 %collective-permute-done.14.come_ref = bf16[512,1152]{1,0:T(8,128)(2,1)S(1)} collective-permute-done((bf16[512,1152]{1,0:T(8,128)(2,1)S(1)}, bf16[512,1152]{1,0:T(8,128)(2,1)S(1)}, u32[]{:S(2)}, u32[]{:S(2)}) %collective-permute-start.14) | collective-permute-done | bytes 1179680 | tf_op jit(solution)/shard_map/ppermute | solution.py:512
  251.6 12.0 %shard_map.175 = (bf16[1024,288]{1,0:T(8,128)(2,1)S(1)}, f32[1024,8]{1,0:T(8,128)S(1)}, f32[512,1152]{1,0:T(8,128)S(1)}, bf16[512,1152]{1,0:T(8,128)(2,1)S(1)}) custom-call(s32[1024,1]{1,0:T(8,128)S(1)} %copy-done.43, s32[1,1024]{1,0:T(1,128)S(1)} %bitcast.241, bf16[1024,864]{1,0:T(8,128)(2,1)S(1)} %shard_map.174.refs_2_.refs_4_.refs_7_, ...), custom_call_target="tpu_custom_call" | custom-call | flops 301989888 | bytes 471859 | tf_op jit(solution)/shard_map/pallas_call | solution.py:147
  263.7 16.1 %collective-permute-done.16 = bf16[256,1152]{1,0:T(8,128)(2,1)} collective-permute-done((bf16[256,1152]{1,0:T(8,128)(2,1)}, bf16[256,1152]{1,0:T(8,128)(2,1)}, u32[]{:S(2)}, u32[]{:S(2)}) %collective-permute-start.16) | collective-permute-done | bytes 589856 | tf_op jit(solution)/shard_map/ppermute | solution.py:734
  282.9 27.5 %collective-permute-done.18.come_ref = bf16[512,1152]{1,0:T(8,128)(2,1)S(1)} collective-permute-done((bf16[512,1152]{1,0:T(8,128)(2,1)S(1)}, bf16[512,1152]{1,0:T(8,128)(2,1)S(1)}, u32[]{:S(2)}, u32[]{:S(2)}) %collective-permute-start.18) | collective-permute-done | bytes 1179680 | tf_op jit(solution)/shard_map/ppermute | solution.py:512
  317.2 9.7 %collective-permute-done.19 = bf16[256,1152]{1,0:T(8,128)(2,1)S(1)} collective-permute-done((bf16[256,1152]{1,0:T(8,128)(2,1)S(1)}, bf16[256,1152]{1,0:T(8,128)(2,1)S(1)}, u32[]{:S(2)}, u32[]{:S(2)}) %collective-permute-start.19) | collective-permute-done | bytes 589856 | tf_op jit(solution)/shard_map/ppermute | solution.py:512
  336.6 9.9 %shard_map.177 = (bf16[1024,1152]{1,0:T(8,128)(2,1)S(1)}, bf16[1024,1152]{1,0:T(8,128)(2,1)S(1)}, f32[512,1152]{1,0:T(8,128)S(1)}, bf16[512,1152]{1,0:T(8,128)(2,1)S(1)}) custom-call(bf16[512,1152]{1,0:T(8,128)(2,1)} %get-tuple-element.201.own_ref.refs_0_, bf16[512,1152]{1,0:T(8,128)(2,1)} %collective-permute-done.21.rec_ref.refs_1_, ...), custom_call_target="tpu_custom_call" | custom-call | flops 543581824 | bytes 1710489 | tf_op jit(solution)/shard_map/pallas_call | solution.py:324
  351.7 9.4 %shard_map.179 = (bf16[1024,1152]{1,0:T(8,128)(2,1)S(1)}, f32[1,1152]{1,0:T(1,128)S(1)}, f32[512,1152]{1,0:T(8,128)S(1)}, bf16[512,1152]{1,0:T(8,128)(2,1)S(1)}) custom-call(bf16[512,1152]{1,0:T(8,128)(2,1)} %get-tuple-element.206.refs_0_.own_ref, bf16[512,1152]{1,0:T(8,128)(2,1)} %collective-permute-done.20.refs_1_.rec_ref, ...), custom_call_target="tpu_custom_call" | custom-call | flops 543581824 | bytes 1474560 | tf_op jit(solution)/shard_map/pallas_call | solution.py:359
  376.2 16.9 %collective-permute-done.24 = bf16[576,1152]{1,0:T(8,128)(2,1)S(1)} collective-permute-done((bf16[576,1152]{1,0:T(8,128)(2,1)S(1)}, bf16[576,1152]{1,0:T(8,128)(2,1)S(1)}, u32[]{:S(2)}, u32[]{:S(2)}) %collective-permute-start.24) | collective-permute-done | bytes 1327136 | tf_op jit(solution)/shard_map/ppermute | solution.py:534
  412.6 20.7 %shard_map.182 = (bf16[1024,288]{1,0:T(8,128)(2,1)S(1)}, bf16[1024,576]{1,0:T(8,128)(2,1)}) custom-call(s32[1,1024]{1,0:T(1,128)S(1)} %bitcast.238, s32[1024,1]{1,0:T(8,128)S(1)} %copy-done.40, bf16[1024,864]{1,0:T(8,128)(2,1)} %copy-done.5, f32[8,1024]{1,0:T(8,128)S(1)} %bitcast.236, bf16[288,1152]{1,0:T(8,128)(2,1)S(1)} %copy-done.21, ...), custom_call_target="tpu_custom_call" | custom-call | flops 724775744 | bytes 884736 | tf_op jit(solution)/shard_map/pallas_call | solution.py:236
  465.2 12.1 %collective-permute-done.30.come_ref = bf16[512,1152]{1,0:T(8,128)(2,1)} collective-permute-done((bf16[512,1152]{1,0:T(8,128)(2,1)}, bf16[512,1152]{1,0:T(8,128)(2,1)}, u32[]{:S(2)}, u32[]{:S(2)}) %collective-permute-start.30) | collective-permute-done | bytes 1179680 | tf_op jit(solution)/shard_map/ppermute | solution.py:512
  501.4 9.7 %shard_map.188 = (bf16[1024,1152]{1,0:T(8,128)(2,1)S(1)}, f32[1,1152]{1,0:T(1,128)S(1)}, f32[512,1152]{1,0:T(8,128)S(1)}, bf16[512,1152]{1,0:T(8,128)(2,1)}) custom-call(bf16[512,1152]{1,0:T(8,128)(2,1)} %get-tuple-element.247.refs_0_.own_ref, bf16[512,1152]{1,0:T(8,128)(2,1)S(1)} %collective-permute-done.31.refs_1_.rec_ref, ...), custom_call_target="tpu_custom_call" | custom-call | flops 543581824 | bytes 1474560 | tf_op jit(solution)/shard_map/pallas_call | solution.py:359
  537.8 16.2 %collective-permute-done.35 = bf16[576,1152]{1,0:T(8,128)(2,1)} collective-permute-done((bf16[576,1152]{1,0:T(8,128)(2,1)}, bf16[576,1152]{1,0:T(8,128)(2,1)}, u32[]{:S(2)}, u32[]{:S(2)}) %collective-permute-start.35) | collective-permute-done | bytes 1327136 | tf_op jit(solution)/shard_map/ppermute | solution.py:534
  569.0 20.7 %shard_map.191 = (bf16[1024,288]{1,0:T(8,128)(2,1)S(1)}, bf16[1024,576]{1,0:T(8,128)(2,1)}) custom-call(s32[1,1024]{1,0:T(1,128)S(1)} %bitcast.239, s32[1024,1]{1,0:T(8,128)S(1)} %copy-done.41, bf16[1024,864]{1,0:T(8,128)(2,1)} %copy-done.4, f32[8,1024]{1,0:T(8,128)S(1)} %bitcast.235, bf16[288,1152]{1,0:T(8,128)(2,1)S(1)} %reshape.409.refs_3_.refs_4_, ...), custom_call_target="tpu_custom_call" | custom-call | flops 724775744 | bytes 884736 | tf_op jit(solution)/shard_map/pallas_call | solution.py:236
  632.8 8.0 %collective-permute-done.45 = bf16[2,36,3168]{2,1,0:T(8,128)(2,1)} collective-permute-done((bf16[2,36,3168]{2,1,0:T(8,128)(2,1)}, bf16[2,36,3168]{2,1,0:T(8,128)(2,1)}, u32[]{:S(2)}, u32[]{:S(2)}) %collective-permute-start.45) | collective-permute-done | bytes 456224 | tf_op jit(solution)/shard_map/ppermute | solution.py:512
  644.9 8.5 %collective-permute-done.40.come_ref = bf16[256,1152]{1,0:T(8,128)(2,1)} collective-permute-done((bf16[256,1152]{1,0:T(8,128)(2,1)}, bf16[256,1152]{1,0:T(8,128)(2,1)}, u32[]{:S(2)}, u32[]{:S(2)}) %collective-permute-start.40) | collective-permute-done | bytes 589856 | tf_op jit(solution)/shard_map/ppermute | solution.py:512
  673.5 18.4 %collective-permute-done.43 = f32[24,1152]{1,0:T(8,128)S(1)} collective-permute-done((f32[24,1152]{1,0:T(8,128)S(1)}, f32[24,1152]{1,0:T(8,128)S(1)}, u32[]{:S(2)}, u32[]{:S(2)}) %collective-permute-start.43) | collective-permute-done | bytes 110624 | tf_op jit(solution)/shard_map/ppermute | solution.py:534
  703.6 28.1 %reduce-scatter.17.cloned.1.call-done = bf16[144,1152]{1,0:T(8,128)(2,1)} async-done(((bf16[576,1152]{1,0:T(8,128)(2,1)}), bf16[144,1152]{1,0:T(8,128)(2,1)}) %reduce-scatter.17.cloned.1.call-update) | async-done | bytes 331792 | tf_op jit(solution)/shard_map/reduce_scatter | solution.py:556
  (624 shorter events, 394.1 us)
Async XLA Ops:
  7.2 83.7 %all-gather.5.cloned.1.call-start = ((), (), s32[]{:S(2)}) async-start(), calls=%async_computation.6 | async-start | bytes 3317760 | tf_op jit(solution)/shard_map/all_gather | solution.py:538
  7.2 28.1 %collective-permute-start.3 = (bf16[256,1152]{1,0:T(8,128)(2,1)}, bf16[256,1152]{1,0:T(8,128)(2,1)S(1)}, u32[]{:S(2)}, u32[]{:S(2)}) collective-permute-start(bf16[256,1152]{1,0:T(8,128)(2,1)} %param.10), channel_id=1, source_target_pairs={{0,0},{1,4},{2,8},{3,12},{4,3},{5,7},{6,11},{7,15},{8,1},{9,5},{10... | collective-permute-start | bytes 1769480 | tf_op jit(solution)/shard_map/ppermute | solution.py:657
  35.0 146.1 %all-gather.7.cloned.1.call-start = ((), (), s32[]{:S(2)}) async-start(), calls=%async_computation.7 | async-start | bytes 5971968 | tf_op jit(solution)/shard_map/all_gather | solution.py:538
  90.9 149.1 %all-gather.9.cloned.1.call-start = ((), (), s32[]{:S(2)}) async-start(), calls=%async_computation.8 | async-start | bytes 2985984 | tf_op jit(solution)/shard_map/all_gather | solution.py:538
  135.1 199.0 %all-gather.11.cloned.1.call-start = ((), (), s32[]{:S(2)}) async-start(), calls=%async_computation.9 | async-start | bytes 5971968 | tf_op jit(solution)/shard_map/all_gather | solution.py:538
  144.8 28.0 %collective-permute-start.9 = (bf16[512,1152]{1,0:T(8,128)(2,1)}, bf16[512,1152]{1,0:T(8,128)(2,1)}, u32[]{:S(2)}, u32[]{:S(2)}) collective-permute-start(bf16[512,1152]{1,0:T(8,128)(2,1)} %add_convert_fusion.13.q_ref), channel_id=1, source_target_pairs={{0,8},{8,0},{1,9},{9,1},{2,10},{10,2},{3,11},{11,3},{4,12},{12,4},... | collective-permute-start | bytes 3538952 | tf_op jit(solution)/shard_map/ppermute | solution.py:512
  198.1 251.3 %reduce-scatter.7.cloned.1.call-start = ((), (), s32[]{:S(2)}) async-start(), calls=%async_computation.10 | async-start | bytes 1658880 | tf_op jit(solution)/shard_map/reduce_scatter | solution.py:556
  237.0 42.8 %collective-permute-start.16 = (bf16[256,1152]{1,0:T(8,128)(2,1)}, bf16[256,1152]{1,0:T(8,128)(2,1)}, u32[]{:S(2)}, u32[]{:S(2)}) collective-permute-start(bf16[256,1152]{1,0:T(8,128)(2,1)} %param.11), channel_id=1, source_target_pairs={{0,0},{1,4},{2,8},{3,12},{4,3},{5,7},{6,11},{7,15},{8,1},{9,5},{10... | collective-permute-start | bytes 1769480 | tf_op jit(solution)/shard_map/ppermute | solution.py:734
  362.8 30.4 %collective-permute-start.24 = (bf16[576,1152]{1,0:T(8,128)(2,1)S(1)}, bf16[576,1152]{1,0:T(8,128)(2,1)S(1)}, u32[]{:S(2)}, u32[]{:S(2)}) collective-permute-start(bf16[576,1152]{1,0:T(8,128)(2,1)S(1)} %get-tuple-element.214), channel_id=1, source_target_pairs={{0,16},{16,0},{1,17},{17,1},{2,18},{18,2},{3,19},{19,3},{4,20},{20... | collective-permute-start | bytes 3981320 | tf_op jit(solution)/shard_map/ppermute | solution.py:534
  366.4 28.2 %collective-permute-start.23 = (bf16[512,1152]{1,0:T(8,128)(2,1)}, bf16[512,1152]{1,0:T(8,128)(2,1)}, u32[]{:S(2)}, u32[]{:S(2)}) collective-permute-start(bf16[512,1152]{1,0:T(8,128)(2,1)} %add_convert_fusion.10.q_ref), channel_id=1, source_target_pairs={{0,8},{8,0},{1,9},{9,1},{2,10},{10,2},{3,11},{11,3},{4,12},{12,4},... | collective-permute-start | bytes 3538952 | tf_op jit(solution)/shard_map/ppermute | solution.py:512
  404.7 74.2 %reduce-scatter.9.cloned.1.call-start = ((), (), s32[]{:S(2)}) async-start(), calls=%async_computation.11 | async-start | bytes 1658880 | tf_op jit(solution)/shard_map/reduce_scatter | solution.py:556
  404.8 39.2 %collective-permute-start.28 = (bf16[576,1152]{1,0:T(8,128)(2,1)}, bf16[576,1152]{1,0:T(8,128)(2,1)}, u32[]{:S(2)}, u32[]{:S(2)}) collective-permute-start(bf16[576,1152]{1,0:T(8,128)(2,1)} %copy-done.88), channel_id=1, source_target_pairs={{0,16},{16,0},{1,17},{17,1},{2,18},{18,2},{3,19},{19,3},{4,20},{20... | collective-permute-start | bytes 3981320 | tf_op jit(solution)/shard_map/ppermute | solution.py:534
  407.0 34.5 %collective-permute-start.29 = (bf16[256,1152]{1,0:T(8,128)(2,1)}, bf16[256,1152]{1,0:T(8,128)(2,1)}, u32[]{:S(2)}, u32[]{:S(2)}) collective-permute-start(bf16[256,1152]{1,0:T(8,128)(2,1)} %dynamic-slice_bitcast_fusion.4), channel_id=1, source_target_pairs={{0,8},{8,0},{1,9},{9,1},{2,10},{10,2},{3,11},{11,3},{4,12},{12,4},... | collective-permute-start | bytes 1769480 | tf_op jit(solution)/shard_map/ppermute | solution.py:512
  449.4 107.4 %reduce-scatter.11.cloned.1.call-start = ((), (), s32[]{:S(2)}) async-start(), calls=%async_computation.12 | async-start | bytes 1658880 | tf_op jit(solution)/shard_map/reduce_scatter | solution.py:556
  487.0 31.1 %collective-permute-start.33 = (bf16[576,1152]{1,0:T(8,128)(2,1)}, bf16[576,1152]{1,0:T(8,128)(2,1)}, u32[]{:S(2)}, u32[]{:S(2)}) collective-permute-start(bf16[576,1152]{1,0:T(8,128)(2,1)} %get-tuple-element.254), channel_id=1, source_target_pairs={{0,16},{16,0},{1,17},{17,1},{2,18},{18,2},{3,19},{19,3},{4,20},{20... | collective-permute-start | bytes 3981320 | tf_op jit(solution)/shard_map/ppermute | solution.py:534
  523.7 129.8 %reduce-scatter.13.cloned.1.call-start = ((), (), s32[]{:S(2)}) async-start(), calls=%async_computation.13 | async-start | bytes 1658880 | tf_op jit(solution)/shard_map/reduce_scatter | solution.py:556
  523.7 30.3 %collective-permute-start.35 = (bf16[576,1152]{1,0:T(8,128)(2,1)}, bf16[576,1152]{1,0:T(8,128)(2,1)}, u32[]{:S(2)}, u32[]{:S(2)}) collective-permute-start(bf16[576,1152]{1,0:T(8,128)(2,1)} %copy-done.87), channel_id=1, source_target_pairs={{0,16},{16,0},{1,17},{17,1},{2,18},{18,2},{3,19},{19,3},{4,20},{20... | collective-permute-start | bytes 3981320 | tf_op jit(solution)/shard_map/ppermute | solution.py:534
  527.1 29.7 %collective-permute-start.34 = (bf16[512,1152]{1,0:T(8,128)(2,1)}, bf16[512,1152]{1,0:T(8,128)(2,1)}, u32[]{:S(2)}, u32[]{:S(2)}) collective-permute-start(bf16[512,1152]{1,0:T(8,128)(2,1)} %add_convert_fusion.7.q_ref), channel_id=1, source_target_pairs={{0,8},{8,0},{1,9},{9,1},{2,10},{10,2},{3,11},{11,3},{4,12},{12,4},... | collective-permute-start | bytes 3538952 | tf_op jit(solution)/shard_map/ppermute | solution.py:512
  566.6 34.0 %collective-permute-start.39 = (bf16[576,1152]{1,0:T(8,128)(2,1)}, bf16[576,1152]{1,0:T(8,128)(2,1)}, u32[]{:S(2)}, u32[]{:S(2)}) collective-permute-start(bf16[576,1152]{1,0:T(8,128)(2,1)} %get-tuple-element.277), channel_id=1, source_target_pairs={{0,16},{16,0},{1,17},{17,1},{2,18},{18,2},{3,19},{19,3},{4,20},{20... | collective-permute-start | bytes 3981320 | tf_op jit(solution)/shard_map/ppermute | solution.py:534
  598.8 70.6 %reduce-scatter.15.cloned.1.call-start = ((), (), s32[]{:S(2)}) async-start(), calls=%async_computation.14 | async-start | bytes 1658880 | tf_op jit(solution)/shard_map/reduce_scatter | solution.py:556
  632.8 98.9 %reduce-scatter.17.cloned.1.call-start = ((), (), s32[]{:S(2)}) async-start(), calls=%async_computation.15 | async-start | bytes 1658880 | tf_op jit(solution)/shard_map/reduce_scatter | solution.py:556
  660.2 31.7 %collective-permute-start.44 = (bf16[256,1152]{1,0:T(8,128)(2,1)}, bf16[256,1152]{1,0:T(8,128)(2,1)}, u32[]{:S(2)}, u32[]{:S(2)}) collective-permute-start(bf16[256,1152]{1,0:T(8,128)(2,1)} %copy-done.89), channel_id=1, source_target_pairs={{0,0},{4,1},{8,2},{12,3},{3,4},{7,5},{11,6},{15,7},{1,8},{5,9},{9,... | collective-permute-start | bytes 1769480 | tf_op jit(solution)/shard_map/ppermute | solution.py:922
  662.5 29.3 %collective-permute-start.47 = (bf16[576,1152]{1,0:T(8,128)(2,1)}, bf16[576,1152]{1,0:T(8,128)(2,1)}, u32[]{:S(2)}, u32[]{:S(2)}) collective-permute-start(bf16[576,1152]{1,0:T(8,128)(2,1)} %copy-done.86), channel_id=1, source_target_pairs={{0,16},{16,0},{1,17},{17,1},{2,18},{18,2},{3,19},{19,3},{4,20},{20... | collective-permute-start | bytes 3981320 | tf_op jit(solution)/shard_map/ppermute | solution.py:534
  699.9 36.1 %collective-permute-start.50 = (f32[24,1152]{1,0:T(8,128)S(1)}, f32[24,1152]{1,0:T(8,128)S(1)}, u32[]{:S(2)}, u32[]{:S(2)}) collective-permute-start(f32[24,1152]{1,0:T(8,128)S(1)} %add.459), channel_id=1, source_target_pairs={{0,1},{1,0},{2,3},{3,2},{4,5},{5,4},{6,7},{7,6},{8,9},{9,8},{10,11... | collective-permute-start | bytes 331784 | tf_op jit(solution)/shard_map/ppermute | solution.py:534
  (166 other events, 1919.5 us)
Sparse Core Ops, SparseCore 0:
  35.1 55.7 all-gather.4
  93.6 85.9 all-gather.6
  182.2 52.7 all-gather.8
  237.0 97.0 all-gather.10
  404.8 29.1 reduce-scatter.6
  449.5 29.3 reduce-scatter.8
  523.8 30.3 reduce-scatter.10
  598.9 35.1 reduce-scatter.12
  636.4 30.5 reduce-scatter.14
  694.7 36.9 reduce-scatter.16

commit v7 on v6

--- a/solution.py
+++ b/solution.py
@@ -44,7 +44,7 @@
 
 
 def cost(flops, moved, exps=0):
-    share = 0.1
+    share = 0.14
     return pl.CostEstimate(
         flops=int(share * flops), bytes_accessed=int(share * moved), transcendentals=int(share * exps)
     )

time: 784 us -> 784 us (level)
  no operation moved by 1% of the time
where the time goes in v7:
time: 784 us; the launch traced here: 774 us
  waiting for transfers between devices  295 us (38%)
  Pallas kernels  173 us (22%)
  local copies, waits for them, and re-layouts  145 us (18%)
  starting transfers between devices  73.8 us (9%)
  other arithmetic  55.1 us (7%)
  between operations  16.3 us (2%)
  matrix products  15 us (2%)
    ppermute x15, waiting for transfers between devices, swap_x(): return lax.ppermute(v, 'x', SWAP)  153 us
    unnamed x264, local copies, waits for them, and re-layouts  76.6 us
    ppermute x11, waiting for transfers between devices, flip(): return lax.ppermute(v, axis, [(i, i ^ step) for i in range(size)])  56.2 us
    pallas_call x2, Pallas kernels, attend_back(): pl.pallas_call(functools.partial(attend_back_kernel, heads, dim, offset,...  41.4 us
    reduce_scatter x6, waiting for transfers between devices, scatter_rows(): return lax.psum_scatter(terms, 'seq', scatter_dimension=0, tiled=True)  29.7 us
    pallas_call x6, Pallas kernels, outer(): pl.pallas_call(functools.partial(outer_kernel, len(lefts), len(rights), l...  28.5 us
    pallas_call x2, Pallas kernels, attend(): pl.pallas_call(functools.partial(attend_kernel, heads, dim, offset, len(k...  24.1 us
    all_gather x4, waiting for transfers between devices, gather_rows(): return lax.all_gather(payload, ('hi', 'seq'), axis=0, tiled=True)  23.2 us
  transfers between devices with their start and end apart: 62, of which 31 were waited for; matrix products, arithmetic and copies ran while one was open for 17% of the time, Pallas kernels for 19%

profile of v7, /device:TPU:1, one launch (start us, length us, event | category | flops | bytes accessed | tf_op | source)
XLA Modules:
  0.0 773.8 jit_solution(6588390278059063873)
XLA Ops:
  44.2 9.6 %collective-permute-done.4 = bf16[2,36,3168]{2,1,0:T(8,128)(2,1)S(1)} collective-permute-done((bf16[2,36,3168]{2,1,0:T(8,128)(2,1)S(1)}, bf16[2,36,3168]{2,1,0:T(8,128)(2,1)S(1)}, u32[]{:S(2)}, u32[]{:S(2)}) %collective-permute-start.4) | collective-permute-done | bytes 456224 | tf_op jit(solution)/shard_map/ppermute | solution.py:512
  55.4 11.0 %collective-permute-done.6 = bf16[256,1152]{1,0:T(8,128)(2,1)S(1)} collective-permute-done((bf16[256,1152]{1,0:T(8,128)(2,1)S(1)}, bf16[256,1152]{1,0:T(8,128)(2,1)S(1)}, u32[]{:S(2)}, u32[]{:S(2)}) %collective-permute-start.6) | collective-permute-done | bytes 589856 | tf_op jit(solution)/shard_map/ppermute | solution.py:512
  71.0 19.9 %all-gather.5.cloned.1.call-done.w_ref = bf16[1152,1168]{1,0:T(8,128)(2,1)} async-done(((bf16[144,1168]{1,0:T(8,128)(2,1)}), bf16[1152,1168]{1,0:T(8,128)(2,1)}) %all-gather.5.cloned.1.call-update) | async-done | bytes 2691088 | tf_op jit(solution)/shard_map/all_gather | solution.py:538
  113.1 12.0 %shard_map.170 = (bf16[1024,288]{1,0:T(8,128)(2,1)S(1)}, f32[1024,8]{1,0:T(8,128)S(1)}, f32[512,1152]{1,0:T(8,128)S(1)}, bf16[512,1152]{1,0:T(8,128)(2,1)S(1)}) custom-call(s32[1024,1]{1,0:T(8,128)S(1)} %copy-done.42, s32[1,1024]{1,0:T(1,128)S(1)} %bitcast.240, bf16[1024,864]{1,0:T(8,128)(2,1)S(1)} %shard_map.169.refs_2_.refs_4_.refs_7_, ...), custom_call_target="tpu_custom_call" | custom-call | flops 422785856 | bytes 660602 | tf_op jit(solution)/shard_map/pallas_call | solution.py:147
  135.1 8.9 %collective-permute-done.10 = bf16[2,36,2304]{2,1,0:T(8,128)(2,1)S(1)} collective-permute-done((bf16[2,36,2304]{2,1,0:T(8,128)(2,1)S(1)}, bf16[2,36,2304]{2,1,0:T(8,128)(2,1)S(1)}, u32[]{:S(2)}, u32[]{:S(2)}) %collective-permute-start.10) | collective-permute-done | bytes 331808 | tf_op jit(solution)/shard_map/ppermute | solution.py:512
  149.8 23.0 %collective-permute-done.9.come_ref = bf16[512,1152]{1,0:T(8,128)(2,1)} collective-permute-done((bf16[512,1152]{1,0:T(8,128)(2,1)}, bf16[512,1152]{1,0:T(8,128)(2,1)}, u32[]{:S(2)}, u32[]{:S(2)}) %collective-permute-start.9) | collective-permute-done | bytes 1179680 | tf_op jit(solution)/shard_map/ppermute | solution.py:512
  184.0 9.3 %shard_map.172 = (bf16[1024,1152]{1,0:T(8,128)(2,1)S(1)}, bf16[1024,1152]{1,0:T(8,128)(2,1)S(1)}, f32[512,1152]{1,0:T(8,128)S(1)}, bf16[512,1152]{1,0:T(8,128)(2,1)S(1)}) custom-call(bf16[512,1152]{1,0:T(8,128)(2,1)} %get-tuple-element.180.own_ref.refs_0_, bf16[512,1152]{1,0:T(8,128)(2,1)S(1)} %collective-permute-done.12.rec_ref.refs_1_, ...), custom_call_target="tpu_custom_call" | custom-call | flops 761014528 | bytes 2394685 | tf_op jit(solution)/shard_map/pallas_call | solution.py:324
  204.1 25.8 %collective-permute-done.14.come_ref = bf16[512,1152]{1,0:T(8,128)(2,1)S(1)} collective-permute-done((bf16[512,1152]{1,0:T(8,128)(2,1)S(1)}, bf16[512,1152]{1,0:T(8,128)(2,1)S(1)}, u32[]{:S(2)}, u32[]{:S(2)}) %collective-permute-start.14) | collective-permute-done | bytes 1179680 | tf_op jit(solution)/shard_map/ppermute | solution.py:512
  251.6 12.0 %shard_map.175 = (bf16[1024,288]{1,0:T(8,128)(2,1)S(1)}, f32[1024,8]{1,0:T(8,128)S(1)}, f32[512,1152]{1,0:T(8,128)S(1)}, bf16[512,1152]{1,0:T(8,128)(2,1)S(1)}) custom-call(s32[1024,1]{1,0:T(8,128)S(1)} %copy-done.43, s32[1,1024]{1,0:T(1,128)S(1)} %bitcast.241, bf16[1024,864]{1,0:T(8,128)(2,1)S(1)} %shard_map.174.refs_2_.refs_4_.refs_7_, ...), custom_call_target="tpu_custom_call" | custom-call | flops 422785856 | bytes 660602 | tf_op jit(solution)/shard_map/pallas_call | solution.py:147
  263.7 16.1 %collective-permute-done.16 = bf16[256,1152]{1,0:T(8,128)(2,1)} collective-permute-done((bf16[256,1152]{1,0:T(8,128)(2,1)}, bf16[256,1152]{1,0:T(8,128)(2,1)}, u32[]{:S(2)}, u32[]{:S(2)}) %collective-permute-start.16) | collective-permute-done | bytes 589856 | tf_op jit(solution)/shard_map/ppermute | solution.py:734
  282.9 27.5 %collective-permute-done.18.come_ref = bf16[512,1152]{1,0:T(8,128)(2,1)S(1)} collective-permute-done((bf16[512,1152]{1,0:T(8,128)(2,1)S(1)}, bf16[512,1152]{1,0:T(8,128)(2,1)S(1)}, u32[]{:S(2)}, u32[]{:S(2)}) %collective-permute-start.18) | collective-permute-done | bytes 1179680 | tf_op jit(solution)/shard_map/ppermute | solution.py:512
  317.2 9.7 %collective-permute-done.19 = bf16[256,1152]{1,0:T(8,128)(2,1)S(1)} collective-permute-done((bf16[256,1152]{1,0:T(8,128)(2,1)S(1)}, bf16[256,1152]{1,0:T(8,128)(2,1)S(1)}, u32[]{:S(2)}, u32[]{:S(2)}) %collective-permute-start.19) | collective-permute-done | bytes 589856 | tf_op jit(solution)/shard_map/ppermute | solution.py:512
  336.6 9.9 %shard_map.177 = (bf16[1024,1152]{1,0:T(8,128)(2,1)S(1)}, bf16[1024,1152]{1,0:T(8,128)(2,1)S(1)}, f32[512,1152]{1,0:T(8,128)S(1)}, bf16[512,1152]{1,0:T(8,128)(2,1)S(1)}) custom-call(bf16[512,1152]{1,0:T(8,128)(2,1)} %get-tuple-element.201.own_ref.refs_0_, bf16[512,1152]{1,0:T(8,128)(2,1)} %collective-permute-done.21.rec_ref.refs_1_, ...), custom_call_target="tpu_custom_call" | custom-call | flops 761014528 | bytes 2394685 | tf_op jit(solution)/shard_map/pallas_call | solution.py:324
  351.7 9.4 %shard_map.179 = (bf16[1024,1152]{1,0:T(8,128)(2,1)S(1)}, f32[1,1152]{1,0:T(1,128)S(1)}, f32[512,1152]{1,0:T(8,128)S(1)}, bf16[512,1152]{1,0:T(8,128)(2,1)S(1)}) custom-call(bf16[512,1152]{1,0:T(8,128)(2,1)} %get-tuple-element.206.refs_0_.own_ref, bf16[512,1152]{1,0:T(8,128)(2,1)} %collective-permute-done.20.refs_1_.rec_ref, ...), custom_call_target="tpu_custom_call" | custom-call | flops 761014528 | bytes 2064384 | tf_op jit(solution)/shard_map/pallas_call | solution.py:359
  376.2 16.9 %collective-permute-done.24 = bf16[576,1152]{1,0:T(8,128)(2,1)S(1)} collective-permute-done((bf16[576,1152]{1,0:T(8,128)(2,1)S(1)}, bf16[576,1152]{1,0:T(8,128)(2,1)S(1)}, u32[]{:S(2)}, u32[]{:S(2)}) %collective-permute-start.24) | collective-permute-done | bytes 1327136 | tf_op jit(solution)/shard_map/ppermute | solution.py:534
  412.6 20.7 %shard_map.182 = (bf16[1024,288]{1,0:T(8,128)(2,1)S(1)}, bf16[1024,576]{1,0:T(8,128)(2,1)}) custom-call(s32[1,1024]{1,0:T(1,128)S(1)} %bitcast.238, s32[1024,1]{1,0:T(8,128)S(1)} %copy-done.40, bf16[1024,864]{1,0:T(8,128)(2,1)} %copy-done.5, f32[8,1024]{1,0:T(8,128)S(1)} %bitcast.236, bf16[288,1152]{1,0:T(8,128)(2,1)S(1)} %copy-done.21, ...), custom_call_target="tpu_custom_call" | custom-call | flops 1014686016 | bytes 1238630 | tf_op jit(solution)/shard_map/pallas_call | solution.py:236
  465.2 12.1 %collective-permute-done.30.come_ref = bf16[512,1152]{1,0:T(8,128)(2,1)} collective-permute-done((bf16[512,1152]{1,0:T(8,128)(2,1)}, bf16[512,1152]{1,0:T(8,128)(2,1)}, u32[]{:S(2)}, u32[]{:S(2)}) %collective-permute-start.30) | collective-permute-done | bytes 1179680 | tf_op jit(solution)/shard_map/ppermute | solution.py:512
  501.4 9.7 %shard_map.188 = (bf16[1024,1152]{1,0:T(8,128)(2,1)S(1)}, f32[1,1152]{1,0:T(1,128)S(1)}, f32[512,1152]{1,0:T(8,128)S(1)}, bf16[512,1152]{1,0:T(8,128)(2,1)}) custom-call(bf16[512,1152]{1,0:T(8,128)(2,1)} %get-tuple-element.247.refs_0_.own_ref, bf16[512,1152]{1,0:T(8,128)(2,1)S(1)} %collective-permute-done.31.refs_1_.rec_ref, ...), custom_call_target="tpu_custom_call" | custom-call | flops 761014528 | bytes 2064384 | tf_op jit(solution)/shard_map/pallas_call | solution.py:359
  537.8 16.2 %collective-permute-done.35 = bf16[576,1152]{1,0:T(8,128)(2,1)} collective-permute-done((bf16[576,1152]{1,0:T(8,128)(2,1)}, bf16[576,1152]{1,0:T(8,128)(2,1)}, u32[]{:S(2)}, u32[]{:S(2)}) %collective-permute-start.35) | collective-permute-done | bytes 1327136 | tf_op jit(solution)/shard_map/ppermute | solution.py:534
  569.0 20.7 %shard_map.191 = (bf16[1024,288]{1,0:T(8,128)(2,1)S(1)}, bf16[1024,576]{1,0:T(8,128)(2,1)}) custom-call(s32[1,1024]{1,0:T(1,128)S(1)} %bitcast.239, s32[1024,1]{1,0:T(8,128)S(1)} %copy-done.41, bf16[1024,864]{1,0:T(8,128)(2,1)} %copy-done.4, f32[8,1024]{1,0:T(8,128)S(1)} %bitcast.235, bf16[288,1152]{1,0:T(8,128)(2,1)S(1)} %reshape.409.refs_3_.refs_4_, ...), custom_call_target="tpu_custom_call" | custom-call | flops 1014686016 | bytes 1238630 | tf_op jit(solution)/shard_map/pallas_call | solution.py:236
  632.8 8.0 %collective-permute-done.45 = bf16[2,36,3168]{2,1,0:T(8,128)(2,1)} collective-permute-done((bf16[2,36,3168]{2,1,0:T(8,128)(2,1)}, bf16[2,36,3168]{2,1,0:T(8,128)(2,1)}, u32[]{:S(2)}, u32[]{:S(2)}) %collective-permute-start.45) | collective-permute-done | bytes 456224 | tf_op jit(solution)/shard_map/ppermute | solution.py:512
  644.9 8.5 %collective-permute-done.40.come_ref = bf16[256,1152]{1,0:T(8,128)(2,1)} collective-permute-done((bf16[256,1152]{1,0:T(8,128)(2,1)}, bf16[256,1152]{1,0:T(8,128)(2,1)}, u32[]{:S(2)}, u32[]{:S(2)}) %collective-permute-start.40) | collective-permute-done | bytes 589856 | tf_op jit(solution)/shard_map/ppermute | solution.py:512
  673.5 18.4 %collective-permute-done.43 = f32[24,1152]{1,0:T(8,128)S(1)} collective-permute-done((f32[24,1152]{1,0:T(8,128)S(1)}, f32[24,1152]{1,0:T(8,128)S(1)}, u32[]{:S(2)}, u32[]{:S(2)}) %collective-permute-start.43) | collective-permute-done | bytes 110624 | tf_op jit(solution)/shard_map/ppermute | solution.py:534
  703.6 28.1 %reduce-scatter.17.cloned.1.call-done = bf16[144,1152]{1,0:T(8,128)(2,1)} async-done(((bf16[576,1152]{1,0:T(8,128)(2,1)}), bf16[144,1152]{1,0:T(8,128)(2,1)}) %reduce-scatter.17.cloned.1.call-update) | async-done | bytes 331792 | tf_op jit(solution)/shard_map/reduce_scatter | solution.py:556
  (624 shorter events, 394.1 us)
Async XLA Ops:
  7.2 83.7 %all-gather.5.cloned.1.call-start = ((), (), s32[]{:S(2)}) async-start(), calls=%async_computation.6 | async-start | bytes 3317760 | tf_op jit(solution)/shard_map/all_gather | solution.py:538
  7.2 28.1 %collective-permute-start.3 = (bf16[256,1152]{1,0:T(8,128)(2,1)}, bf16[256,1152]{1,0:T(8,128)(2,1)S(1)}, u32[]{:S(2)}, u32[]{:S(2)}) collective-permute-start(bf16[256,1152]{1,0:T(8,128)(2,1)} %param.10), channel_id=1, source_target_pairs={{0,0},{1,4},{2,8},{3,12},{4,3},{5,7},{6,11},{7,15},{8,1},{9,5},{10... | collective-permute-start | bytes 1769480 | tf_op jit(solution)/shard_map/ppermute | solution.py:657
  35.0 146.1 %all-gather.7.cloned.1.call-start = ((), (), s32[]{:S(2)}) async-start(), calls=%async_computation.7 | async-start | bytes 5971968 | tf_op jit(solution)/shard_map/all_gather | solution.py:538
  90.9 149.1 %all-gather.9.cloned.1.call-start = ((), (), s32[]{:S(2)}) async-start(), calls=%async_computation.8 | async-start | bytes 2985984 | tf_op jit(solution)/shard_map/all_gather | solution.py:538
  135.1 199.0 %all-gather.11.cloned.1.call-start = ((), (), s32[]{:S(2)}) async-start(), calls=%async_computation.9 | async-start | bytes 5971968 | tf_op jit(solution)/shard_map/all_gather | solution.py:538
  144.8 28.0 %collective-permute-start.9 = (bf16[512,1152]{1,0:T(8,128)(2,1)}, bf16[512,1152]{1,0:T(8,128)(2,1)}, u32[]{:S(2)}, u32[]{:S(2)}) collective-permute-start(bf16[512,1152]{1,0:T(8,128)(2,1)} %add_convert_fusion.13.q_ref), channel_id=1, source_target_pairs={{0,8},{8,0},{1,9},{9,1},{2,10},{10,2},{3,11},{11,3},{4,12},{12,4},... | collective-permute-start | bytes 3538952 | tf_op jit(solution)/shard_map/ppermute | solution.py:512
  198.1 251.3 %reduce-scatter.7.cloned.1.call-start = ((), (), s32[]{:S(2)}) async-start(), calls=%async_computation.10 | async-start | bytes 1658880 | tf_op jit(solution)/shard_map/reduce_scatter | solution.py:556
  237.0 42.8 %collective-permute-start.16 = (bf16[256,1152]{1,0:T(8,128)(2,1)}, bf16[256,1152]{1,0:T(8,128)(2,1)}, u32[]{:S(2)}, u32[]{:S(2)}) collective-permute-start(bf16[256,1152]{1,0:T(8,128)(2,1)} %param.11), channel_id=1, source_target_pairs={{0,0},{1,4},{2,8},{3,12},{4,3},{5,7},{6,11},{7,15},{8,1},{9,5},{10... | collective-permute-start | bytes 1769480 | tf_op jit(solution)/shard_map/ppermute | solution.py:734
  362.8 30.4 %collective-permute-start.24 = (bf16[576,1152]{1,0:T(8,128)(2,1)S(1)}, bf16[576,1152]{1,0:T(8,128)(2,1)S(1)}, u32[]{:S(2)}, u32[]{:S(2)}) collective-permute-start(bf16[576,1152]{1,0:T(8,128)(2,1)S(1)} %get-tuple-element.214), channel_id=1, source_target_pairs={{0,16},{16,0},{1,17},{17,1},{2,18},{18,2},{3,19},{19,3},{4,20},{20... | collective-permute-start | bytes 3981320 | tf_op jit(solution)/shard_map/ppermute | solution.py:534
  366.4 28.2 %collective-permute-start.23 = (bf16[512,1152]{1,0:T(8,128)(2,1)}, bf16[512,1152]{1,0:T(8,128)(2,1)}, u32[]{:S(2)}, u32[]{:S(2)}) collective-permute-start(bf16[512,1152]{1,0:T(8,128)(2,1)} %add_convert_fusion.10.q_ref), channel_id=1, source_target_pairs={{0,8},{8,0},{1,9},{9,1},{2,10},{10,2},{3,11},{11,3},{4,12},{12,4},... | collective-permute-start | bytes 3538952 | tf_op jit(solution)/shard_map/ppermute | solution.py:512
  404.7 74.2 %reduce-scatter.9.cloned.1.call-start = ((), (), s32[]{:S(2)}) async-start(), calls=%async_computation.11 | async-start | bytes 1658880 | tf_op jit(solution)/shard_map/reduce_scatter | solution.py:556
  404.8 39.2 %collective-permute-start.28 = (bf16[576,1152]{1,0:T(8,128)(2,1)}, bf16[576,1152]{1,0:T(8,128)(2,1)}, u32[]{:S(2)}, u32[]{:S(2)}) collective-permute-start(bf16[576,1152]{1,0:T(8,128)(2,1)} %copy-done.88), channel_id=1, source_target_pairs={{0,16},{16,0},{1,17},{17,1},{2,18},{18,2},{3,19},{19,3},{4,20},{20... | collective-permute-start | bytes 3981320 | tf_op jit(solution)/shard_map/ppermute | solution.py:534
  407.0 34.5 %collective-permute-start.29 = (bf16[256,1152]{1,0:T(8,128)(2,1)}, bf16[256,1152]{1,0:T(8,128)(2,1)}, u32[]{:S(2)}, u32[]{:S(2)}) collective-permute-start(bf16[256,1152]{1,0:T(8,128)(2,1)} %dynamic-slice_bitcast_fusion.4), channel_id=1, source_target_pairs={{0,8},{8,0},{1,9},{9,1},{2,10},{10,2},{3,11},{11,3},{4,12},{12,4},... | collective-permute-start | bytes 1769480 | tf_op jit(solution)/shard_map/ppermute | solution.py:512
  449.4 107.4 %reduce-scatter.11.cloned.1.call-start = ((), (), s32[]{:S(2)}) async-start(), calls=%async_computation.12 | async-start | bytes 1658880 | tf_op jit(solution)/shard_map/reduce_scatter | solution.py:556
  487.0 31.1 %collective-permute-start.33 = (bf16[576,1152]{1,0:T(8,128)(2,1)}, bf16[576,1152]{1,0:T(8,128)(2,1)}, u32[]{:S(2)}, u32[]{:S(2)}) collective-permute-start(bf16[576,1152]{1,0:T(8,128)(2,1)} %get-tuple-element.254), channel_id=1, source_target_pairs={{0,16},{16,0},{1,17},{17,1},{2,18},{18,2},{3,19},{19,3},{4,20},{20... | collective-permute-start | bytes 3981320 | tf_op jit(solution)/shard_map/ppermute | solution.py:534
  523.7 129.8 %reduce-scatter.13.cloned.1.call-start = ((), (), s32[]{:S(2)}) async-start(), calls=%async_computation.13 | async-start | bytes 1658880 | tf_op jit(solution)/shard_map/reduce_scatter | solution.py:556
  523.7 30.3 %collective-permute-start.35 = (bf16[576,1152]{1,0:T(8,128)(2,1)}, bf16[576,1152]{1,0:T(8,128)(2,1)}, u32[]{:S(2)}, u32[]{:S(2)}) collective-permute-start(bf16[576,1152]{1,0:T(8,128)(2,1)} %copy-done.87), channel_id=1, source_target_pairs={{0,16},{16,0},{1,17},{17,1},{2,18},{18,2},{3,19},{19,3},{4,20},{20... | collective-permute-start | bytes 3981320 | tf_op jit(solution)/shard_map/ppermute | solution.py:534
  527.1 29.7 %collective-permute-start.34 = (bf16[512,1152]{1,0:T(8,128)(2,1)}, bf16[512,1152]{1,0:T(8,128)(2,1)}, u32[]{:S(2)}, u32[]{:S(2)}) collective-permute-start(bf16[512,1152]{1,0:T(8,128)(2,1)} %add_convert_fusion.7.q_ref), channel_id=1, source_target_pairs={{0,8},{8,0},{1,9},{9,1},{2,10},{10,2},{3,11},{11,3},{4,12},{12,4},... | collective-permute-start | bytes 3538952 | tf_op jit(solution)/shard_map/ppermute | solution.py:512
  566.6 34.0 %collective-permute-start.39 = (bf16[576,1152]{1,0:T(8,128)(2,1)}, bf16[576,1152]{1,0:T(8,128)(2,1)}, u32[]{:S(2)}, u32[]{:S(2)}) collective-permute-start(bf16[576,1152]{1,0:T(8,128)(2,1)} %get-tuple-element.277), channel_id=1, source_target_pairs={{0,16},{16,0},{1,17},{17,1},{2,18},{18,2},{3,19},{19,3},{4,20},{20... | collective-permute-start | bytes 3981320 | tf_op jit(solution)/shard_map/ppermute | solution.py:534
  598.8 70.6 %reduce-scatter.15.cloned.1.call-start = ((), (), s32[]{:S(2)}) async-start(), calls=%async_computation.14 | async-start | bytes 1658880 | tf_op jit(solution)/shard_map/reduce_scatter | solution.py:556
  632.8 98.9 %reduce-scatter.17.cloned.1.call-start = ((), (), s32[]{:S(2)}) async-start(), calls=%async_computation.15 | async-start | bytes 1658880 | tf_op jit(solution)/shard_map/reduce_scatter | solution.py:556
  660.2 31.7 %collective-permute-start.44 = (bf16[256,1152]{1,0:T(8,128)(2,1)}, bf16[256,1152]{1,0:T(8,128)(2,1)}, u32[]{:S(2)}, u32[]{:S(2)}) collective-permute-start(bf16[256,1152]{1,0:T(8,128)(2,1)} %copy-done.89), channel_id=1, source_target_pairs={{0,0},{4,1},{8,2},{12,3},{3,4},{7,5},{11,6},{15,7},{1,8},{5,9},{9,... | collective-permute-start | bytes 1769480 | tf_op jit(solution)/shard_map/ppermute | solution.py:922
  662.5 29.3 %collective-permute-start.47 = (bf16[576,1152]{1,0:T(8,128)(2,1)}, bf16[576,1152]{1,0:T(8,128)(2,1)}, u32[]{:S(2)}, u32[]{:S(2)}) collective-permute-start(bf16[576,1152]{1,0:T(8,128)(2,1)} %copy-done.86), channel_id=1, source_target_pairs={{0,16},{16,0},{1,17},{17,1},{2,18},{18,2},{3,19},{19,3},{4,20},{20... | collective-permute-start | bytes 3981320 | tf_op jit(solution)/shard_map/ppermute | solution.py:534
  699.9 36.1 %collective-permute-start.50 = (f32[24,1152]{1,0:T(8,128)S(1)}, f32[24,1152]{1,0:T(8,128)S(1)}, u32[]{:S(2)}, u32[]{:S(2)}) collective-permute-start(f32[24,1152]{1,0:T(8,128)S(1)} %add.459), channel_id=1, source_target_pairs={{0,1},{1,0},{2,3},{3,2},{4,5},{5,4},{6,7},{7,6},{8,9},{9,8},{10,11... | collective-permute-start | bytes 331784 | tf_op jit(solution)/shard_map/ppermute | solution.py:534
  (166 other events, 1919.5 us)
Sparse Core Ops, SparseCore 0:
  35.1 55.7 all-gather.4
  93.6 85.9 all-gather.6
  182.2 52.7 all-gather.8
  237.0 97.0 all-gather.10
  404.8 29.1 reduce-scatter.6
  449.5 29.3 reduce-scatter.8
  523.8 30.3 reduce-scatter.10
  598.9 35.1 reduce-scatter.12
  636.4 30.5 reduce-scatter.14
  694.7 36.9 reduce-scatter.16
